TPU v7x, 32 devices: a whole 2x2x4 slice. The times are simulated.
32 devices in a mesh: dp: 8 (over z, core), tensor: 4 (over y, x).
Axes of the slice: x: 2, y: 2, z: 4, core: 2. Of those that a mesh axis runs over, the one named last changes fastest.
Arguments:
- requests: bfloat16 [512, 8192], P('dp'), may hold values from -6 to 6
- base_gate_up_weight: bfloat16 [8192, 2, 28672], P('dp', None, 'tensor'), may hold values from -0.0625 to 0.0625
- adapter_down_weight: bfloat16 [64, 8192, 128], P('dp', 'tensor'), may hold values from -0.0625 to 0.0625
- adapter_up_weight: bfloat16 [64, 64, 2, 28672], P('dp', None, None, 'tensor'), may hold values from -0.75 to 0.75
- request_adapter: int32 [512], P('dp'), may hold values from 0 to 63, as said below
- adapter_position: int32 [64], replicated, may hold values from 0 to 63, as said below
- counts: int32 [8], replicated, may hold values from 1 to 64, 384 in all
Outputs:
- hidden: bfloat16 [512, 28672], P('dp', 'tensor')
Inputs may be any that keep to these rules, and one draw needn't show every extreme that they name: `request_adapter`: the owner of store position s is s // 8. Among the 64 rows of one group at most 8 use adapters of one owner; in every draw one owner receives exactly 8 rows from every group. `adapter_position`: each store position appears once. `counts`: rows of a group past its count are padding.
All inputs are finite; a program needn't handle non-finite values.
Results may differ from a plain program's by a relative error of at most 0.0058.
Values may be sent and summed in bfloat16 or wider, within the bound.
No kernel may reach another device: no remote copies, remote signals or barrier semaphores. Data moves between devices by JAX's collectives and lax.ppermute only.
A program may use at most 192 MiB of HBM per device.

v0:
```python
import jax
import jax.numpy as jnp
from jax import lax
from jax.sharding import PartitionSpec as P


def body(
    requests,
    base_gate_up_weight,
    adapter_down_weight,
    adapter_up_weight,
    request_adapter,
    adapter_position,
    counts,
):
    rows = requests.shape[0]
    width = requests.shape[1]
    groups = lax.axis_size("dp")
    lanes = lax.axis_size("tensor")
    holder_adapters = adapter_down_weight.shape[0]
    rank_doubled = adapter_down_weight.shape[2]
    rank_single = rank_doubled // 2
    rank_extent = adapter_up_weight.shape[3]
    capacity = rows // 8
    buffer = groups * capacity
    group = lax.axis_index("dp")
    lane = lax.axis_index("tensor")
    match = (
        request_adapter[:, None] == jnp.arange(adapter_position.shape[0], dtype=jnp.int32)[None, :]
    )
    slot = jnp.sum(jnp.where(match, adapter_position[None, :], 0), axis=1)
    owner = slot // holder_adapters
    local = slot % holder_adapters
    owner_hot = (owner[:, None] == jnp.arange(groups, dtype=jnp.int32)[None, :]).astype(jnp.int32)
    place = jnp.sum(owner_hot * (jnp.cumsum(owner_hot, axis=0) - 1), axis=1)
    target = owner * capacity + place
    select = target[None, :] == jnp.arange(buffer, dtype=jnp.int32)[:, None]
    select_bf = select.astype(jnp.bfloat16)
    width_part = width // lanes
    piece = lax.dynamic_slice_in_dim(requests, lane * width_part, width_part, 1)
    outgoing = jnp.dot(select_bf, piece, preferred_element_type=jnp.float32).astype(jnp.bfloat16)
    row_index = jnp.arange(rows, dtype=jnp.int32)
    labels = jnp.stack(
        [
            jnp.sum(jnp.where(select, local[None, :], 0), axis=1),
            jnp.sum(jnp.where(select, row_index[None, :], 0), axis=1),
        ],
        axis=1,
    ).astype(jnp.bfloat16)
    arrived, arrived_labels = (
        lax.all_to_all(outgoing, "dp", split_axis=0, concat_axis=0, tiled=True),
        lax.all_to_all(labels, "dp", split_axis=0, concat_axis=0, tiled=True),
    )
    which = arrived_labels[:, 0].astype(jnp.int32)
    partial_down = jnp.zeros((buffer, rank_doubled), jnp.float32)
    for adapter_number in range(holder_adapters):
        selected_adapter = jnp.where(
            (which == adapter_number)[:, None], arrived, jnp.zeros_like(arrived)
        )
        partial_down = partial_down + jnp.dot(
            selected_adapter,
            adapter_down_weight[adapter_number],
            preferred_element_type=jnp.float32,
        )
    down = lax.psum(partial_down, "tensor").astype(jnp.bfloat16)
    term_gate = jnp.zeros((buffer, rank_extent), jnp.float32)
    term_up = jnp.zeros((buffer, rank_extent), jnp.float32)
    for adapter_number in range(holder_adapters):
        selected_adapter = jnp.where((which == adapter_number)[:, None], down, jnp.zeros_like(down))
        term_gate = term_gate + jnp.dot(
            selected_adapter[:, :rank_single],
            adapter_up_weight[adapter_number, :, 0, :],
            preferred_element_type=jnp.float32,
        )
        term_up = term_up + jnp.dot(
            selected_adapter[:, rank_single:],
            adapter_up_weight[adapter_number, :, 1, :],
            preferred_element_type=jnp.float32,
        )
    delta = jnp.concatenate([term_gate.astype(jnp.bfloat16), term_up.astype(jnp.bfloat16)], axis=1)
    spread = lax.all_to_all(requests, "dp", split_axis=1, concat_axis=0, tiled=True)
    weight_flat = base_gate_up_weight.reshape(base_gate_up_weight.shape[0], 2 * rank_extent)
    term = jnp.dot(spread, weight_flat, preferred_element_type=jnp.float32)
    summed = lax.psum_scatter(term, "dp", scatter_dimension=0, tiled=True)
    back = lax.all_to_all(delta, "dp", split_axis=0, concat_axis=0, tiled=True)
    summed = summed + jnp.dot(select_bf.T, back, preferred_element_type=jnp.float32)
    gate = summed[:, :rank_extent]
    up = summed[:, rank_extent:]
    live = row_index < counts[group]
    hidden = jnp.where(live[:, None], jax.nn.silu(gate) * up, 0.0)
    return hidden.astype(jnp.bfloat16)


def solution(mesh):
    placed = (
        P("dp", None),
        P("dp", None, "tensor"),
        P("dp", "tensor", None),
        P("dp", None, None, "tensor"),
        P("dp"),
        P(),
        P(),
    )
    return jax.shard_map(
        body, mesh=mesh, in_specs=placed, out_specs=P("dp", "tensor"), check_vma=False
    )
```

profile of v0, /device:TPU:9, one launch (start us, length us, event | category | flops | bytes accessed | tf_op | source)
XLA Modules:
  0.0 408.6 jit_solution(599813189817675353)
XLA Ops:
  6.5 2.3 copy.130
  8.8 5.6 %all-to-all-start = ((bf16[64,8,1024]{2,0,1:T(8,128)(2,1)}), bf16[64,8,1024]{2,0,1:T(8,128)(2,1)S(1)}, u32[]{:S(2)}, u32[]{:S(2)}) async-start(bf16[64,8,1024]{2,0,1:T(8,128)(2,1)} %bitcast.132), calls=%async_computation | async-start | bytes 2097152 | tf_op jit(solution)/shard_map/all_to_all | solution.py:81
  14.5 20.4 %copy.96 = bf16[128,8,2,7168]{3,1,2,0:T(8,128)(2,1)} copy(bf16[128,8,2,7168]{3,2,1,0:T(2,128)(2,1)} %bitcast.133) | data formatting | bytes 58720256
  34.9 2.6 all-to-all-done
  37.5 27.8 %fusion.87 = f32[512,14336]{1,0:T(8,128)} fusion(bf16[512,1024]{1,0:T(8,128)(2,1)S(1)} %bitcast.136, bf16[1024,14336]{1,0:T(8,128)(2,1)} %bitcast.134), kind=kOutput, calls=%fused_computation.168 | convolution fusion | flops 15032385536 | bytes 59768832 | tf_op jit(solution)/shard_map/dot_general | solution.py:83
  65.3 0.6 copy-done.15
  66.9 0.6 copy.61
  67.5 6.7 %all-to-all-start.1 = ((bf16[8,8,2]{1,2,0:T(2,128)(2,1)}), bf16[8,8,2]{1,2,0:T(2,128)(2,1)S(1)}, u32[]{:S(2)}, u32[]{:S(2)}) async-start(bf16[8,8,2]{1,2,0:T(2,128)(2,1)} %copy.61), calls=%async_computation.2 | async-start | bytes 8192 | tf_op jit(solution)/shard_map/all_to_all | solution.py:52
  74.2 1.9 fusion.2
  76.1 1.9 all-to-all-done.1
  78.0 5.1 %all-to-all-start.2 = ((bf16[8,8,2048]{2,1,0:T(8,128)(2,1)}), bf16[8,8,2048]{2,1,0:T(8,128)(2,1)S(1)}, u32[]{:S(2)}, u32[]{:S(2)}) async-start(bf16[8,8,2048]{2,1,0:T(8,128)(2,1)} %fusion.2), calls=%async_computation.3 | async-start | bytes 524288 | tf_op jit(solution)/shard_map/all_to_all | solution.py:51
  83.1 39.6 %fusion.86 = (bf16[1,64,1,7168]{3,2,1,0:T(2,128)(2,1)S(1)}, bf16[1,64,1,7168]{3,2,1,0:T(2,128)(2,1)}, bf16[1,64,1,7168]{3,2,1,0:T(2,128)(2,1)}, bf16[1,64,1,7168...) fusion(bf16[8,64,2,7168]{3,2,1,0:T(2,128)(2,1)} %param.10), kind=kLoop, calls=%fused_computation.167 | loop fusion | bytes 29360128 | tf_op jit(solution)/shard_map/slice | solution.py:72
  123.5 1.5 fusion.15
  125.0 1.4 convolution_add_fusion.21
  126.4 1.3 convolution_add_fusion.20
  127.7 1.3 convolution_add_fusion.19
  130.2 12.6 %psum.7 = bf16[64,128]{1,0:T(8,128)(2,1)S(1)} all-reduce(f32[64,128]{1,0:T(8,128)S(1)} %convolution_add_fusion.15), channel_id=1, replica_groups=mesh['dp'=8,'tensor'=4] {'tensor'}, use_global_device_ids=true, to_apply=%region_6.7 | all-reduce | flops 8192 | bytes 49152 | tf_op jit(solution)/shard_map/psum | solution.py:65
  142.9 2.1 fusion.6
  145.5 1.1 copy-done.12
  147.1 1.0 copy-done.11
  148.6 1.0 copy-done.10
  149.6 0.5 convolution_add_fusion.5
  150.1 1.1 copy-done.9
  151.7 1.0 copy-done.8
  152.7 0.5 convolution_add_fusion.3
  153.2 1.0 copy-done.7
  154.2 0.5 convolution_add_fusion.2
  154.7 1.0 copy-done
  155.8 0.5 fusion.1
  156.3 1.0 copy-done.6
  157.8 1.0 copy-done.5
  158.8 0.5 convolution_add_fusion.13
  159.3 1.0 copy-done.4
  160.3 0.5 convolution_add_fusion.12
  160.8 1.0 copy-done.3
  161.8 0.5 convolution_add_fusion.11
  162.3 1.0 copy-done.2
  163.3 0.5 convolution_add_fusion.10
  163.8 1.0 copy-done.1
  164.8 0.5 convolution_add_fusion.9
  165.8 1.3 maximum_bitcast_fusion
  167.1 9.1 %all-to-all-start.3 = ((bf16[8,8,14336]{2,1,0:T(8,128)(2,1)}), bf16[8,8,14336]{2,1,0:T(8,128)(2,1)S(1)}, u32[]{:S(2)}, u32[]{:S(2)}) async-start(bf16[8,8,14336]{2,1,0:T(8,128)(2,1)} %maximum_bitcast_fusion), calls=%async_computation.4 | async-start | bytes 3670016 | tf_op jit(solution)/shard_map/all_to_all | solution.py:85
  176.2 0.6 dynamic_slice.6
  176.8 0.6 iota_compare_fusion.5
  177.5 67.6 %all-to-all-done.3 = bf16[8,8,14336]{2,1,0:T(8,128)(2,1)S(1)} async-done(((bf16[8,8,14336]{2,1,0:T(8,128)(2,1)}), bf16[8,8,14336]{2,1,0:T(8,128)(2,1)S(1)}, u32[]{:S(2)}, u32[]{:S(2)}) %all-to-all-start.3) | async-done | bytes 1835040 | tf_op jit(solution)/shard_map/all_to_all | solution.py:85
  245.1 152.4 %reduce-scatter.2.cloned.1.call-done = f32[64,14336]{1,0:T(8,128)} async-done(((f32[512,14336]{1,0:T(8,128)}), f32[64,14336]{1,0:T(8,128)}) %reduce-scatter.2.cloned.1.call-update) | async-done | bytes 3670032 | tf_op jit(solution)/shard_map/reduce_scatter | solution.py:84
  397.6 2.7 convolution_add_fusion
  400.3 1.5 fusion.4
  (59 shorter events, 5.9 us)
Async XLA Ops:
  8.8 28.7 %all-to-all-start = ((bf16[64,8,1024]{2,0,1:T(8,128)(2,1)}), bf16[64,8,1024]{2,0,1:T(8,128)(2,1)S(1)}, u32[]{:S(2)}, u32[]{:S(2)}) async-start(bf16[64,8,1024]{2,0,1:T(8,128)(2,1)} %bitcast.132), calls=%async_computation | async-start | bytes 2097152 | tf_op jit(solution)/shard_map/all_to_all | solution.py:81
  14.5 383.1 %reduce-scatter.2.cloned.1.call-start = ((), (), s32[]{:S(2)}) async-start(), calls=%async_computation.5 | async-start | bytes 33030144 | tf_op jit(solution)/shard_map/reduce_scatter | solution.py:84
  65.3 0.7 copy-start.15
  65.3 0.7 copy-start.16
  67.5 10.5 %all-to-all-start.1 = ((bf16[8,8,2]{1,2,0:T(2,128)(2,1)}), bf16[8,8,2]{1,2,0:T(2,128)(2,1)S(1)}, u32[]{:S(2)}, u32[]{:S(2)}) async-start(bf16[8,8,2]{1,2,0:T(2,128)(2,1)} %copy.61), calls=%async_computation.2 | async-start | bytes 8192 | tf_op jit(solution)/shard_map/all_to_all | solution.py:52
  78.0 45.5 %all-to-all-start.2 = ((bf16[8,8,2048]{2,1,0:T(8,128)(2,1)}), bf16[8,8,2048]{2,1,0:T(8,128)(2,1)S(1)}, u32[]{:S(2)}, u32[]{:S(2)}) async-start(bf16[8,8,2048]{2,1,0:T(8,128)(2,1)} %fusion.2), calls=%async_computation.3 | async-start | bytes 524288 | tf_op jit(solution)/shard_map/all_to_all | solution.py:51
  123.5 5.5 %copy-start.14 = (bf16[8,2048,128]{2,1,0:T(8,128)(2,1)S(1)}, bf16[8,2048,128]{2,1,0:T(8,128)(2,1)}, u32[]{:S(2)}) copy-start(bf16[8,2048,128]{2,1,0:T(8,128)(2,1)} %param.9) | copy-start | bytes 12582916
  142.8 2.2 copy-start.13
  145.0 1.6 copy-start.12
  146.6 1.5 copy-start.11
  148.1 1.5 copy-start.10
  149.6 1.6 copy-start.9
  151.2 1.5 copy-start.8
  152.7 1.5 copy-start.7
  154.2 1.6 copy-start
  155.8 1.5 copy-start.6
  157.3 1.5 copy-start.5
  158.8 1.5 copy-start.4
  160.3 1.5 copy-start.3
  161.8 1.5 copy-start.2
  163.3 1.5 copy-start.1
  167.1 9.1 %copy-start.17 = (s32[8]{0:T(128)S(1)}, s32[8]{0:T(128)}, u32[]{:S(2)}) copy-start(s32[8]{0:T(128)} %param.13) | copy-start | bytes 100
  167.1 78.0 %all-to-all-start.3 = ((bf16[8,8,14336]{2,1,0:T(8,128)(2,1)}), bf16[8,8,14336]{2,1,0:T(8,128)(2,1)S(1)}, u32[]{:S(2)}, u32[]{:S(2)}) async-start(bf16[8,8,14336]{2,1,0:T(8,128)(2,1)} %maximum_bitcast_fusion), calls=%async_computation.4 | async-start | bytes 3670016 | tf_op jit(solution)/shard_map/all_to_all | solution.py:85
Sparse Core Ops, SparseCore 0:
  65.5 332.0 reduce-scatter.1
where the time goes:
time: 410 us; the launch traced here: 409 us
  waiting for transfers between devices  225 us (55%)
  local copies, waits for them, and re-layouts  78.3 us (19%)
  matrix products  48.5 us (12%)
  starting transfers between devices  26.6 us (6%)
  between operations  13.7 us (3%)
  blocking collectives  12.6 us (3%)
  other arithmetic  4.29 us (1%)
    reduce_scatter x1, waiting for transfers between devices, body(): summed = lax.psum_scatter(term, 'dp', scatter_dimension=0, tiled=True)  152 us
    all_to_all x1, waiting for transfers between devices, body(): back = lax.all_to_all(delta, 'dp', split_axis=0, concat_axis=0, tiled=True)  67.6 us
    slice x1, local copies, waits for them, and re-layouts, body(): adapter_up_weight[adapter_number, :, 0, :]  39.6 us
    unnamed x37, local copies, waits for them, and re-layouts  34.2 us
    dot_general x1, matrix products, body(): term = jnp.dot(spread, weight_flat, preferred_element_type=jnp.float32)  27.8 us
    psum x1, blocking collectives, body(): down = lax.psum(partial_down, 'tensor').astype(jnp.bfloat16)  12.6 us
    all_to_all x1, starting transfers between devices, body(): back = lax.all_to_all(delta, 'dp', split_axis=0, concat_axis=0, tiled=True)  9.14 us
  transfers between devices with their start and end apart: 5, of which 4 were waited for; matrix products, arithmetic and copies ran while one was open for 20% of the time, Pallas kernels for 0%

commit v1 on v0

v1 whole, which is shorter than its diff:
```python
import functools

import jax
import jax.numpy as jnp
from jax import lax
from jax.experimental import pallas as pl
from jax.experimental.pallas import tpu as pltpu
from jax.sharding import PartitionSpec as P

CHUNKS = 7


def partial_kernel(x_ref, d_ref, w_ref, u_ref, own_ref, other_ref):
    half = own_ref.shape[1]
    for t in range(2):
        total = jnp.dot(x_ref[...], w_ref[t], preferred_element_type=jnp.float32)
        total = total + jnp.dot(d_ref[t], u_ref[t], preferred_element_type=jnp.float32)
        own_ref[t] = total[:half]
        other_ref[t] = total[half:].astype(jnp.bfloat16)


def partial_sums(x, d, w, u, chunk, width, block):
    rows, depth = x.shape
    inner = d.shape[2]
    per = width // block
    return pl.pallas_call(
        partial_kernel,
        grid=(per,),
        in_specs=[
            pl.BlockSpec((rows, depth), lambda j: (0, 0)),
            pl.BlockSpec((2, rows, inner), lambda j: (0, 0, 0)),
            pl.BlockSpec((2, depth, block), lambda j: (0, 0, chunk * per + j)),
            pl.BlockSpec((2, inner, block), lambda j: (0, 0, chunk * per + j)),
        ],
        out_specs=[
            pl.BlockSpec((2, rows // 2, block), lambda j: (0, 0, j)),
            pl.BlockSpec((2, rows // 2, block), lambda j: (0, 0, j)),
        ],
        out_shape=[
            jax.ShapeDtypeStruct((2, rows // 2, width), jnp.float32),
            jax.ShapeDtypeStruct((2, rows // 2, width), jnp.bfloat16),
        ],
        compiler_params=pltpu.CompilerParams(vmem_limit_bytes=40 * 2**20),
        cost_estimate=pl.CostEstimate(
            flops=4 * rows * (depth + inner) * width,
            bytes_accessed=4 * (depth + inner) * width + 6 * rows * width,
            transcendentals=0,
        ),
    )(x, d, w, u)


def reversed_bits(value, bits):
    out = 0
    for _ in range(bits):
        out = out * 2 + value % 2
        value //= 2
    return out


def body(
    requests,
    base_gate_up_weight,
    adapter_down_weight,
    adapter_up_weight,
    request_adapter,
    adapter_position,
    counts,
):
    rows, width = requests.shape
    groups = lax.axis_size("dp")
    lanes = lax.axis_size("tensor")
    holder_adapters, depth_part, rank_doubled = adapter_down_weight.shape
    rank = rank_doubled // 2
    extent = adapter_up_weight.shape[3]
    capacity = rows // 8
    buffer = groups * capacity
    group = lax.axis_index("dp")
    lane = lax.axis_index("tensor")
    bits = groups.bit_length() - 1
    f32, bf16, i32 = jnp.float32, jnp.bfloat16, jnp.int32

    match = request_adapter[:, None] == jnp.arange(adapter_position.shape[0], dtype=i32)[None, :]
    slot = jnp.sum(jnp.where(match, adapter_position[None, :], 0), axis=1)
    owner = slot // holder_adapters
    local = slot % holder_adapters
    owner_hot = (owner[:, None] == jnp.arange(groups, dtype=i32)[None, :]).astype(i32)
    place = jnp.sum(owner_hot * (jnp.cumsum(owner_hot, axis=0) - 1), axis=1)
    target = owner * capacity + place
    select = (target[None, :] == jnp.arange(buffer, dtype=i32)[:, None]).astype(bf16)
    row_index = jnp.arange(rows, dtype=i32)
    piece = lax.dynamic_slice_in_dim(requests, lane * depth_part, depth_part, 1)
    column = jnp.arange(128, dtype=i32)[None, :]
    labels = jnp.where(column == 0, local[:, None], jnp.where(column == 1, row_index[:, None], 0))
    outgoing = jnp.dot(
        select, jnp.concatenate([piece, labels.astype(bf16)], axis=1), preferred_element_type=f32
    ).astype(bf16)
    arrived = lax.all_to_all(outgoing, "dp", split_axis=0, concat_axis=0, tiled=True)
    spread = lax.all_to_all(requests, "dp", split_axis=1, concat_axis=0, tiled=True)

    gate_up = base_gate_up_weight.transpose(1, 0, 2)
    adapter_up = adapter_up_weight.reshape(holder_adapters * rank, 2, extent).transpose(1, 0, 2)

    which = arrived[:, depth_part].astype(i32)
    place_row = arrived[:, depth_part + 1].astype(i32)
    mine = which[:, None] == jnp.arange(holder_adapters, dtype=i32)[None, :]
    routed = arrived[:, :depth_part]
    spaced = jnp.where(mine[:, :, None], routed[:, None, :], jnp.zeros((), bf16))
    part_down = jnp.dot(
        spaced.reshape(buffer, holder_adapters * depth_part),
        adapter_down_weight.reshape(holder_adapters * depth_part, rank_doubled),
        preferred_element_type=f32,
    )
    total_down = part_down
    for step in range(1, lanes):
        total_down = total_down + lax.ppermute(
            part_down, "tensor", [(i, i ^ step) for i in range(lanes)]
        )
    down = total_down.astype(bf16)
    whole_row = (jnp.arange(buffer, dtype=i32) // capacity) * rows + place_row
    to_row = (jnp.arange(groups * rows, dtype=i32)[:, None] == whole_row[None, :]).astype(bf16)
    spaced_down = [
        jnp.where(
            mine[:, :, None], down[:, None, t * rank : (t + 1) * rank], jnp.zeros((), bf16)
        ).reshape(buffer, holder_adapters * rank)
        for t in range(2)
    ]
    terms = jnp.stack(
        [jnp.dot(to_row, s, preferred_element_type=f32).astype(bf16) for s in spaced_down]
    )

    order = [reversed_bits(i, bits) for i in range(groups)]
    spread = spread.reshape(groups, rows, -1)
    terms = terms.reshape(2, groups, rows, -1)
    x = jnp.concatenate([lax.dynamic_index_in_dim(spread, group ^ b, 0, False) for b in order], 0)
    d = jnp.concatenate([lax.dynamic_index_in_dim(terms, group ^ b, 1, False) for b in order], 1)

    live = row_index < counts[group]
    chunk_width = extent // CHUNKS
    pieces = []
    for chunk in range(CHUNKS):
        own, other = partial_sums(x, d, gate_up, adapter_up, chunk, chunk_width, chunk_width // 2 if chunk_width % 256 == 0 else chunk_width)
        received = [lax.ppermute(other, "dp", [(i, i ^ 1) for i in range(groups)])]
        extents = groups * rows // 2
        for stage in range(1, bits):
            extents //= 2
            parts = [a[:, extents : 2 * extents].astype(f32) for a in [own] + received]
            message = functools.reduce(jnp.add, parts).astype(bf16)
            received.append(
                lax.ppermute(message, "dp", [(i, i ^ (1 << stage)) for i in range(groups)])
            )
        gate, up = functools.reduce(
            jnp.add, [a[:, :rows].astype(f32) for a in [own] + received]
        )
        hidden = jnp.where(live[:, None], jax.nn.silu(gate) * up, 0.0)
        pieces.append(hidden.astype(bf16))
    return jnp.concatenate(pieces, axis=1)


def solution(mesh):
    placed = (
        P("dp", None),
        P("dp", None, "tensor"),
        P("dp", "tensor", None),
        P("dp", None, None, "tensor"),
        P("dp"),
        P(),
        P(),
    )
    return jax.shard_map(
        body, mesh=mesh, in_specs=placed, out_specs=P("dp", "tensor"), check_vma=False
    )
```

time: 410 us -> 270 us (0.66)
  the two profiles are of different devices: /device:TPU:9 before, /device:TPU:0 now
where the time goes in v1:
time: 270 us; the launch traced here: 269 us
  waiting for transfers between devices  138 us (51%)
  Pallas kernels  40.2 us (15%)
  local copies, waits for them, and re-layouts  39.6 us (15%)
  starting transfers between devices  24.5 us (9%)
  other arithmetic  21.4 us (8%)
  matrix products  4.5 us (2%)
    ppermute x14, waiting for transfers between devices, body(): lax.ppermute(message, 'dp', [(i, i ^ 1 << stage) for i in range(groups)])  120 us
    pallas_call x7, Pallas kernels, partial_sums(): pl.pallas_call(partial_kernel, grid=(per,), in_specs=[pl.BlockSpec((rows,...  40.2 us
    unnamed x15, local copies, waits for them, and re-layouts  36.5 us
    all_to_all x1, waiting for transfers between devices, body(): lax.all_to_all(requests, 'dp', split_axis=1, concat_axis=0, tiled=True)  15.1 us
    convert_element_type x14, other arithmetic, body(): message = functools.reduce(jnp.add, parts).astype(bf16)  11.8 us
    ppermute x14, starting transfers between devices, body(): lax.ppermute(message, 'dp', [(i, i ^ 1 << stage) for i in range(groups)])  7.61 us
    all_to_all x1, starting transfers between devices, body(): lax.all_to_all(outgoing, 'dp', split_axis=0, concat_axis=0, tiled=True)  6.33 us
    add x7, other arithmetic, body(): functools.reduce(jnp.add, [a[:, :rows].astype(f32) for a in [own] + recei...  5.74 us
  transfers between devices with their start and end apart: 26, of which 15 were waited for; matrix products, arithmetic and copies ran while one was open for 23% of the time, Pallas kernels for 9%

profile of v1, /device:TPU:0, one launch (start us, length us, event | category | flops | bytes accessed | tf_op | source)
XLA Modules:
  0.0 268.8 jit_solution(16862214908736497101)
XLA Ops:
  0.0 0.9 select_reduce_fusion.1
  1.3 1.0 constant_dynamic-slice_fusion
  3.3 6.3 %all-to-all-start.1 = ((bf16[8,8,2176]{2,1,0:T(8,128)(2,1)}), bf16[8,8,2176]{2,1,0:T(8,128)(2,1)S(1)}, u32[]{:S(2)}, u32[]{:S(2)}) async-start(bf16[8,8,2176]{2,1,0:T(8,128)(2,1)} %fusion), calls=%async_computation.1 | async-start | bytes 557056 | tf_op jit(solution)/shard_map/all_to_all | solution.py:97
  9.7 1.0 copy.38
  10.7 20.8 %copy.37 = bf16[1024,2,7168]{2,0,1:T(8,128)(2,1)} copy(bf16[1024,2,7168]{2,1,0:T(2,128)(2,1)} %param.8) | data formatting | bytes 58720256 | tf_op args[1]
  31.5 15.6 %copy.33 = bf16[8,64,2,7168]{3,1,0,2:T(8,128)(2,1)} copy(bf16[8,64,2,7168]{3,2,1,0:T(2,128)(2,1)} %param.10) | data formatting | bytes 29360128 | tf_op args[3]
  48.3 5.1 %all-to-all-start = ((bf16[64,8,1024]{2,0,1:T(8,128)(2,1)}), bf16[64,8,1024]{2,0,1:T(8,128)(2,1)S(1)}, u32[]{:S(2)}, u32[]{:S(2)}) async-start(bf16[64,8,1024]{2,0,1:T(8,128)(2,1)} %bitcast.168), calls=%async_computation | async-start | bytes 2097152 | tf_op jit(solution)/shard_map/all_to_all | solution.py:98
  53.7 3.0 %fusion.4 = f32[64,128]{1,0:T(8,128)S(1)} fusion(bf16[8,2048,128]{2,1,0:T(8,128)(2,1)} %param.9, pred[64,8]{0,1:T(8,128)(4,1)S(1)} %iota_compare_fusion.7, bf16[64,2048]{1,0:T(8,128)(2,1)S(1)} %slice.246), kind=kOutput, calls=%fused_computation.24 | convolution fusion | flops 269484032 | bytes 4489728 | tf_op jit(solution)/shard_map/dot_general | solution.py:108
  56.7 2.5 collective-permute-start.2
  60.3 1.2 collective-permute-done.2
  61.5 1.5 collective-permute-done.1
  64.9 15.1 %all-to-all-done = bf16[64,8,1024]{2,0,1:T(8,128)(2,1)S(1)} async-done(((bf16[64,8,1024]{2,0,1:T(8,128)(2,1)}), bf16[64,8,1024]{2,0,1:T(8,128)(2,1)S(1)}, u32[]{:S(2)}, u32[]{:S(2)}) %all-to-all-start) | async-done | bytes 1048608 | tf_op jit(solution)/shard_map/all_to_all | solution.py:98
  80.2 5.7 %shard_map.73 = (f32[2,256,1024]{2,1,0:T(8,128)S(1)}, bf16[2,256,1024]{2,1,0:T(8,128)(2,1)S(1)}) custom-call(bf16[512,1024]{1,0:T(8,128)(2,1)S(1)} %bitcast_dynamic-update-slice_fusion.8.x_ref, bf16[2,512,512]{2,1,0:T(8,128)(2,1)S(1)} %bitcast_dynamic-update-slice_fusion.d_ref, bf16[2,1024,7168]{2,1,0:T(8,128)(2,1)} %bitcast.169, bf16[2,512,7168]{2,1,0:T(8,128)(2,1)} %bitcast.176), custom_call_target="tpu_custom_call" | custom-call | flops 3221225472 | bytes 9437184 | tf_op jit(solution)/shard_map/pallas_call | solution.py:26
  85.9 5.7 %shard_map.74 = (f32[2,256,1024]{2,1,0:T(8,128)S(1)}, bf16[2,256,1024]{2,1,0:T(8,128)(2,1)S(1)}) custom-call(bf16[512,1024]{1,0:T(8,128)(2,1)S(1)} %bitcast_dynamic-update-slice_fusion.8.x_ref, bf16[2,512,512]{2,1,0:T(8,128)(2,1)S(1)} %bitcast_dynamic-update-slice_fusion.d_ref, bf16[2,1024,7168]{2,1,0:T(8,128)(2,1)} %bitcast.170, bf16[2,512,7168]{2,1,0:T(8,128)(2,1)} %bitcast.177), custom_call_target="tpu_custom_call" | custom-call | flops 3221225472 | bytes 9437184 | tf_op jit(solution)/shard_map/pallas_call | solution.py:26
  91.7 5.7 %shard_map.75 = (f32[2,256,1024]{2,1,0:T(8,128)S(1)}, bf16[2,256,1024]{2,1,0:T(8,128)(2,1)S(1)}) custom-call(bf16[512,1024]{1,0:T(8,128)(2,1)S(1)} %bitcast_dynamic-update-slice_fusion.8.x_ref, bf16[2,512,512]{2,1,0:T(8,128)(2,1)S(1)} %bitcast_dynamic-update-slice_fusion.d_ref, bf16[2,1024,7168]{2,1,0:T(8,128)(2,1)} %bitcast.171, bf16[2,512,7168]{2,1,0:T(8,128)(2,1)} %bitcast.178), custom_call_target="tpu_custom_call" | custom-call | flops 3221225472 | bytes 9437184 | tf_op jit(solution)/shard_map/pallas_call | solution.py:26
  97.5 5.7 %shard_map.76 = (f32[2,256,1024]{2,1,0:T(8,128)S(1)}, bf16[2,256,1024]{2,1,0:T(8,128)(2,1)S(1)}) custom-call(bf16[512,1024]{1,0:T(8,128)(2,1)S(1)} %bitcast_dynamic-update-slice_fusion.8.x_ref, bf16[2,512,512]{2,1,0:T(8,128)(2,1)S(1)} %bitcast_dynamic-update-slice_fusion.d_ref, bf16[2,1024,7168]{2,1,0:T(8,128)(2,1)} %bitcast.172, bf16[2,512,7168]{2,1,0:T(8,128)(2,1)} %bitcast.179), custom_call_target="tpu_custom_call" | custom-call | flops 3221225472 | bytes 9437184 | tf_op jit(solution)/shard_map/pallas_call | solution.py:26
  104.3 5.7 %shard_map.77 = (f32[2,256,1024]{2,1,0:T(8,128)S(1)}, bf16[2,256,1024]{2,1,0:T(8,128)(2,1)S(1)}) custom-call(bf16[512,1024]{1,0:T(8,128)(2,1)S(1)} %bitcast_dynamic-update-slice_fusion.8.x_ref, bf16[2,512,512]{2,1,0:T(8,128)(2,1)S(1)} %bitcast_dynamic-update-slice_fusion.d_ref, bf16[2,1024,7168]{2,1,0:T(8,128)(2,1)} %bitcast.173, bf16[2,512,7168]{2,1,0:T(8,128)(2,1)} %bitcast.180), custom_call_target="tpu_custom_call" | custom-call | flops 3221225472 | bytes 9437184 | tf_op jit(solution)/shard_map/pallas_call | solution.py:26
  110.1 5.7 %shard_map.78 = (f32[2,256,1024]{2,1,0:T(8,128)S(1)}, bf16[2,256,1024]{2,1,0:T(8,128)(2,1)S(1)}) custom-call(bf16[512,1024]{1,0:T(8,128)(2,1)S(1)} %bitcast_dynamic-update-slice_fusion.8.x_ref, bf16[2,512,512]{2,1,0:T(8,128)(2,1)S(1)} %bitcast_dynamic-update-slice_fusion.d_ref, bf16[2,1024,7168]{2,1,0:T(8,128)(2,1)} %bitcast.174, bf16[2,512,7168]{2,1,0:T(8,128)(2,1)} %bitcast.181), custom_call_target="tpu_custom_call" | custom-call | flops 3221225472 | bytes 9437184 | tf_op jit(solution)/shard_map/pallas_call | solution.py:26
  115.8 5.9 %shard_map.79 = (f32[2,256,1024]{2,1,0:T(8,128)S(1)}, bf16[2,256,1024]{2,1,0:T(8,128)(2,1)S(1)}) custom-call(bf16[512,1024]{1,0:T(8,128)(2,1)S(1)} %bitcast_dynamic-update-slice_fusion.8.x_ref, bf16[2,512,512]{2,1,0:T(8,128)(2,1)S(1)} %bitcast_dynamic-update-slice_fusion.d_ref, bf16[2,1024,7168]{2,1,0:T(8,128)(2,1)} %bitcast.175, bf16[2,512,7168]{2,1,0:T(8,128)(2,1)} %bitcast.182), custom_call_target="tpu_custom_call" | custom-call | flops 3221225472 | bytes 9437184 | tf_op jit(solution)/shard_map/pallas_call | solution.py:26
  122.3 1.2 add_convert_fusion.6
  123.7 1.2 add_convert_fusion.5
  125.0 1.2 add_convert_fusion.4
  126.2 2.1 collective-permute-start.7
  128.3 1.2 add_convert_fusion.3
  129.6 1.2 add_convert_fusion.2
  130.8 2.1 collective-permute-start.13
  133.3 6.4 %collective-permute-done.4 = bf16[2,128,1024]{2,1,0:T(8,128)(2,1)S(1)} collective-permute-done((bf16[2,128,1024]{2,1,0:T(8,128)(2,1)S(1)}, bf16[2,128,1024]{2,1,0:T(8,128)(2,1)S(1)}, u32[]{:S(2)}, u32[]{:S(2)}) %collective-permute-start.4) | collective-permute-done | bytes 524320 | tf_op jit(solution)/shard_map/ppermute | solution.py:149
  139.7 1.1 add_convert_fusion.13
  140.8 10.1 %collective-permute-done.7 = bf16[2,128,1024]{2,1,0:T(8,128)(2,1)S(1)} collective-permute-done((bf16[2,128,1024]{2,1,0:T(8,128)(2,1)S(1)}, bf16[2,128,1024]{2,1,0:T(8,128)(2,1)S(1)}, u32[]{:S(2)}, u32[]{:S(2)}) %collective-permute-start.7) | collective-permute-done | bytes 524320 | tf_op jit(solution)/shard_map/ppermute | solution.py:149
  151.0 1.1 add_convert_fusion.12
  152.0 10.1 %collective-permute-done.10 = bf16[2,128,1024]{2,1,0:T(8,128)(2,1)S(1)} collective-permute-done((bf16[2,128,1024]{2,1,0:T(8,128)(2,1)S(1)}, bf16[2,128,1024]{2,1,0:T(8,128)(2,1)S(1)}, u32[]{:S(2)}, u32[]{:S(2)}) %collective-permute-start.10) | collective-permute-done | bytes 524320 | tf_op jit(solution)/shard_map/ppermute | solution.py:149
  162.1 1.1 add_convert_fusion.11
  163.2 15.8 %collective-permute-done.13 = bf16[2,128,1024]{2,1,0:T(8,128)(2,1)S(1)} collective-permute-done((bf16[2,128,1024]{2,1,0:T(8,128)(2,1)S(1)}, bf16[2,128,1024]{2,1,0:T(8,128)(2,1)S(1)}, u32[]{:S(2)}, u32[]{:S(2)}) %collective-permute-start.13) | collective-permute-done | bytes 524320 | tf_op jit(solution)/shard_map/ppermute | solution.py:149
  179.0 1.1 add_convert_fusion.10
  180.1 15.8 %collective-permute-done.16 = bf16[2,128,1024]{2,1,0:T(8,128)(2,1)S(1)} collective-permute-done((bf16[2,128,1024]{2,1,0:T(8,128)(2,1)S(1)}, bf16[2,128,1024]{2,1,0:T(8,128)(2,1)S(1)}, u32[]{:S(2)}, u32[]{:S(2)}) %collective-permute-start.16) | collective-permute-done | bytes 524320 | tf_op jit(solution)/shard_map/ppermute | solution.py:149
  195.9 1.1 add_convert_fusion.9
  196.9 15.8 %collective-permute-done.19 = bf16[2,128,1024]{2,1,0:T(8,128)(2,1)S(1)} collective-permute-done((bf16[2,128,1024]{2,1,0:T(8,128)(2,1)S(1)}, bf16[2,128,1024]{2,1,0:T(8,128)(2,1)S(1)}, u32[]{:S(2)}, u32[]{:S(2)}) %collective-permute-start.19) | collective-permute-done | bytes 524320 | tf_op jit(solution)/shard_map/ppermute | solution.py:149
  212.8 10.8 %collective-permute-done.22 = bf16[2,128,1024]{2,1,0:T(8,128)(2,1)S(1)} collective-permute-done((bf16[2,128,1024]{2,1,0:T(8,128)(2,1)S(1)}, bf16[2,128,1024]{2,1,0:T(8,128)(2,1)S(1)}, u32[]{:S(2)}, u32[]{:S(2)}) %collective-permute-start.22) | collective-permute-done | bytes 524320 | tf_op jit(solution)/shard_map/ppermute | solution.py:149
  223.7 3.0 %collective-permute-start.20 = (bf16[2,64,1024]{2,1,0:T(8,128)(2,1)S(1)}, bf16[2,64,1024]{2,1,0:T(8,128)(2,1)S(1)}, u32[]{:S(2)}, u32[]{:S(2)}) collective-permute-start(bf16[2,64,1024]{2,1,0:T(8,128)(2,1)S(1)} %add_convert_fusion.8), channel_id=1, source_target_pairs={{0,16},{4,20},{8,24},{12,28},{16,0},{20,4},{24,8},{28,12},{1,17},{... | collective-permute-start | bytes 786440 | tf_op jit(solution)/shard_map/ppermute | solution.py:149
  226.7 1.1 convert_add_fusion.6
  227.9 1.1 convert_add_fusion.5
  229.2 1.1 convert_add_fusion.4
  230.3 20.9 %collective-permute-done.14 = bf16[2,64,1024]{2,1,0:T(8,128)(2,1)S(1)} collective-permute-done((bf16[2,64,1024]{2,1,0:T(8,128)(2,1)S(1)}, bf16[2,64,1024]{2,1,0:T(8,128)(2,1)S(1)}, u32[]{:S(2)}, u32[]{:S(2)}) %collective-permute-start.14) | collective-permute-done | bytes 262176 | tf_op jit(solution)/shard_map/ppermute | solution.py:149
  251.2 1.1 convert_add_fusion.3
  252.5 4.3 %collective-permute-done.17 = bf16[2,64,1024]{2,1,0:T(8,128)(2,1)S(1)} collective-permute-done((bf16[2,64,1024]{2,1,0:T(8,128)(2,1)S(1)}, bf16[2,64,1024]{2,1,0:T(8,128)(2,1)S(1)}, u32[]{:S(2)}, u32[]{:S(2)}) %collective-permute-start.17) | collective-permute-done | bytes 262176 | tf_op jit(solution)/shard_map/ppermute | solution.py:149
  256.8 1.1 convert_add_fusion.2
  257.9 4.5 %collective-permute-done.20 = bf16[2,64,1024]{2,1,0:T(8,128)(2,1)S(1)} collective-permute-done((bf16[2,64,1024]{2,1,0:T(8,128)(2,1)S(1)}, bf16[2,64,1024]{2,1,0:T(8,128)(2,1)S(1)}, u32[]{:S(2)}, u32[]{:S(2)}) %collective-permute-start.20) | collective-permute-done | bytes 262176 | tf_op jit(solution)/shard_map/ppermute | solution.py:149
  262.8 5.2 %collective-permute-done.23 = bf16[2,64,1024]{2,1,0:T(8,128)(2,1)S(1)} collective-permute-done((bf16[2,64,1024]{2,1,0:T(8,128)(2,1)S(1)}, bf16[2,64,1024]{2,1,0:T(8,128)(2,1)S(1)}, u32[]{:S(2)}, u32[]{:S(2)}) %collective-permute-start.23) | collective-permute-done | bytes 262176 | tf_op jit(solution)/shard_map/ppermute | solution.py:149
  (89 shorter events, 10.3 us)
Async XLA Ops:
  0.0 9.7 %copy-start = (bf16[64,8192]{1,0:T(8,128)(2,1)S(1)}, bf16[64,8192]{1,0:T(8,128)(2,1)}, u32[]{:S(2)}) copy-start(bf16[64,8192]{1,0:T(8,128)(2,1)} %param.7) | copy-start | bytes 3145732
  3.3 45.0 %all-to-all-start.1 = ((bf16[8,8,2176]{2,1,0:T(8,128)(2,1)}), bf16[8,8,2176]{2,1,0:T(8,128)(2,1)S(1)}, u32[]{:S(2)}, u32[]{:S(2)}) async-start(bf16[8,8,2176]{2,1,0:T(8,128)(2,1)} %fusion), calls=%async_computation.1 | async-start | bytes 557056 | tf_op jit(solution)/shard_map/all_to_all | solution.py:97
  31.5 15.6 %copy-start.2 = (s32[8]{0:T(128)S(1)}, s32[8]{0:T(128)}, u32[]{:S(2)}) copy-start(s32[8]{0:T(128)} %param.13) | copy-start | bytes 100
  48.3 31.7 %all-to-all-start = ((bf16[64,8,1024]{2,0,1:T(8,128)(2,1)}), bf16[64,8,1024]{2,0,1:T(8,128)(2,1)S(1)}, u32[]{:S(2)}, u32[]{:S(2)}) async-start(bf16[64,8,1024]{2,0,1:T(8,128)(2,1)} %bitcast.168), calls=%async_computation | async-start | bytes 2097152 | tf_op jit(solution)/shard_map/all_to_all | solution.py:98
  56.7 4.9 %collective-permute-start.2 = (f32[64,128]{1,0:T(8,128)S(1)}, f32[64,128]{1,0:T(8,128)S(1)}, u32[]{:S(2)}, u32[]{:S(2)}) collective-permute-start(f32[64,128]{1,0:T(8,128)S(1)} %fusion.4), channel_id=1, source_target_pairs={{0,3},{1,2},{2,1},{3,0},{4,7},{5,6},{6,5},{7,4},{8,11},{9,10},{10,... | collective-permute-start | bytes 98312 | tf_op jit(solution)/shard_map/ppermute | solution.py:115
  59.2 3.9 %collective-permute-start.1 = (f32[64,128]{1,0:T(8,128)S(1)}, f32[64,128]{1,0:T(8,128)S(1)}, u32[]{:S(2)}, u32[]{:S(2)}) collective-permute-start(f32[64,128]{1,0:T(8,128)S(1)} %fusion.4), channel_id=1, source_target_pairs={{0,2},{1,3},{2,0},{3,1},{4,6},{5,7},{6,4},{7,5},{8,10},{9,11},{10,... | collective-permute-start | bytes 98312 | tf_op jit(solution)/shard_map/ppermute | solution.py:115
  59.7 3.9 %collective-permute-start = (f32[64,128]{1,0:T(8,128)S(1)}, f32[64,128]{1,0:T(8,128)S(1)}, u32[]{:S(2)}, u32[]{:S(2)}) collective-permute-start(f32[64,128]{1,0:T(8,128)S(1)} %fusion.4), channel_id=1, source_target_pairs={{0,1},{1,0},{2,3},{3,2},{4,5},{5,4},{6,7},{7,6},{8,9},{9,8},{10,11... | collective-permute-start | bytes 98312 | tf_op jit(solution)/shard_map/ppermute | solution.py:115
  97.4 24.4 %collective-permute-start.3 = (bf16[2,256,1024]{2,1,0:T(8,128)(2,1)S(1)}, bf16[2,256,1024]{2,1,0:T(8,128)(2,1)}, u32[]{:S(2)}, u32[]{:S(2)}) collective-permute-start(bf16[2,256,1024]{2,1,0:T(8,128)(2,1)S(1)} %get-tuple-element.20), channel_id=1, source_target_pairs={{0,4},{4,0},{8,12},{12,8},{16,20},{20,16},{24,28},{28,24},{1,5},{5... | collective-permute-start | bytes 3145736 | tf_op jit(solution)/shard_map/ppermute | solution.py:142
  103.2 20.3 %collective-permute-start.6 = (bf16[2,256,1024]{2,1,0:T(8,128)(2,1)S(1)}, bf16[2,256,1024]{2,1,0:T(8,128)(2,1)}, u32[]{:S(2)}, u32[]{:S(2)}) collective-permute-start(bf16[2,256,1024]{2,1,0:T(8,128)(2,1)S(1)} %get-tuple-element.22), channel_id=1, source_target_pairs={{0,4},{4,0},{8,12},{12,8},{16,20},{20,16},{24,28},{28,24},{1,5},{5... | collective-permute-start | bytes 3145736 | tf_op jit(solution)/shard_map/ppermute | solution.py:142
  103.7 21.1 %collective-permute-start.9 = (bf16[2,256,1024]{2,1,0:T(8,128)(2,1)S(1)}, bf16[2,256,1024]{2,1,0:T(8,128)(2,1)}, u32[]{:S(2)}, u32[]{:S(2)}) collective-permute-start(bf16[2,256,1024]{2,1,0:T(8,128)(2,1)S(1)} %get-tuple-element.24), channel_id=1, source_target_pairs={{0,4},{4,0},{8,12},{12,8},{16,20},{20,16},{24,28},{28,24},{1,5},{5... | collective-permute-start | bytes 3145736 | tf_op jit(solution)/shard_map/ppermute | solution.py:142
  103.8 22.4 %collective-permute-start.12 = (bf16[2,256,1024]{2,1,0:T(8,128)(2,1)S(1)}, bf16[2,256,1024]{2,1,0:T(8,128)(2,1)}, u32[]{:S(2)}, u32[]{:S(2)}) collective-permute-start(bf16[2,256,1024]{2,1,0:T(8,128)(2,1)S(1)} %get-tuple-element.26), channel_id=1, source_target_pairs={{0,4},{4,0},{8,12},{12,8},{16,20},{20,16},{24,28},{28,24},{1,5},{5... | collective-permute-start | bytes 3145736 | tf_op jit(solution)/shard_map/ppermute | solution.py:142
  110.0 19.5 %collective-permute-start.15 = (bf16[2,256,1024]{2,1,0:T(8,128)(2,1)S(1)}, bf16[2,256,1024]{2,1,0:T(8,128)(2,1)}, u32[]{:S(2)}, u32[]{:S(2)}) collective-permute-start(bf16[2,256,1024]{2,1,0:T(8,128)(2,1)S(1)} %get-tuple-element.28), channel_id=1, source_target_pairs={{0,4},{4,0},{8,12},{12,8},{16,20},{20,16},{24,28},{28,24},{1,5},{5... | collective-permute-start | bytes 3145736 | tf_op jit(solution)/shard_map/ppermute | solution.py:142
  121.8 9.0 %collective-permute-start.18 = (bf16[2,256,1024]{2,1,0:T(8,128)(2,1)S(1)}, bf16[2,256,1024]{2,1,0:T(8,128)(2,1)S(1)}, u32[]{:S(2)}, u32[]{:S(2)}) collective-permute-start(bf16[2,256,1024]{2,1,0:T(8,128)(2,1)S(1)} %get-tuple-element.30), channel_id=1, source_target_pairs={{0,4},{4,0},{8,12},{12,8},{16,20},{20,16},{24,28},{28,24},{1,5},{5... | collective-permute-start | bytes 3145736 | tf_op jit(solution)/shard_map/ppermute | solution.py:142
  123.5 9.5 %collective-permute-start.21 = (bf16[2,256,1024]{2,1,0:T(8,128)(2,1)S(1)}, bf16[2,256,1024]{2,1,0:T(8,128)(2,1)S(1)}, u32[]{:S(2)}, u32[]{:S(2)}) collective-permute-start(bf16[2,256,1024]{2,1,0:T(8,128)(2,1)S(1)} %get-tuple-element.32), channel_id=1, source_target_pairs={{0,4},{4,0},{8,12},{12,8},{16,20},{20,16},{24,28},{28,24},{1,5},{5... | collective-permute-start | bytes 3145736 | tf_op jit(solution)/shard_map/ppermute | solution.py:142
  124.9 14.8 %collective-permute-start.4 = (bf16[2,128,1024]{2,1,0:T(8,128)(2,1)S(1)}, bf16[2,128,1024]{2,1,0:T(8,128)(2,1)S(1)}, u32[]{:S(2)}, u32[]{:S(2)}) collective-permute-start(bf16[2,128,1024]{2,1,0:T(8,128)(2,1)S(1)} %add_convert_fusion.6), channel_id=1, source_target_pairs={{0,8},{4,12},{8,0},{12,4},{16,24},{20,28},{24,16},{28,20},{1,9},{5... | collective-permute-start | bytes 1572872 | tf_op jit(solution)/shard_map/ppermute | solution.py:149
  126.2 24.7 %collective-permute-start.7 = (bf16[2,128,1024]{2,1,0:T(8,128)(2,1)S(1)}, bf16[2,128,1024]{2,1,0:T(8,128)(2,1)S(1)}, u32[]{:S(2)}, u32[]{:S(2)}) collective-permute-start(bf16[2,128,1024]{2,1,0:T(8,128)(2,1)S(1)} %add_convert_fusion.5), channel_id=1, source_target_pairs={{0,8},{4,12},{8,0},{12,4},{16,24},{20,28},{24,16},{28,20},{1,9},{5... | collective-permute-start | bytes 1572872 | tf_op jit(solution)/shard_map/ppermute | solution.py:149
  129.5 32.7 %collective-permute-start.10 = (bf16[2,128,1024]{2,1,0:T(8,128)(2,1)S(1)}, bf16[2,128,1024]{2,1,0:T(8,128)(2,1)S(1)}, u32[]{:S(2)}, u32[]{:S(2)}) collective-permute-start(bf16[2,128,1024]{2,1,0:T(8,128)(2,1)S(1)} %add_convert_fusion.4), channel_id=1, source_target_pairs={{0,8},{4,12},{8,0},{12,4},{16,24},{20,28},{24,16},{28,20},{1,9},{5... | collective-permute-start | bytes 1572872 | tf_op jit(solution)/shard_map/ppermute | solution.py:149
  130.8 48.2 %collective-permute-start.13 = (bf16[2,128,1024]{2,1,0:T(8,128)(2,1)S(1)}, bf16[2,128,1024]{2,1,0:T(8,128)(2,1)S(1)}, u32[]{:S(2)}, u32[]{:S(2)}) collective-permute-start(bf16[2,128,1024]{2,1,0:T(8,128)(2,1)S(1)} %add_convert_fusion.3), channel_id=1, source_target_pairs={{0,8},{4,12},{8,0},{12,4},{16,24},{20,28},{24,16},{28,20},{1,9},{5... | collective-permute-start | bytes 1572872 | tf_op jit(solution)/shard_map/ppermute | solution.py:149
  133.0 62.8 %collective-permute-start.16 = (bf16[2,128,1024]{2,1,0:T(8,128)(2,1)S(1)}, bf16[2,128,1024]{2,1,0:T(8,128)(2,1)S(1)}, u32[]{:S(2)}, u32[]{:S(2)}) collective-permute-start(bf16[2,128,1024]{2,1,0:T(8,128)(2,1)S(1)} %add_convert_fusion.2), channel_id=1, source_target_pairs={{0,8},{4,12},{8,0},{12,4},{16,24},{20,28},{24,16},{28,20},{1,9},{5... | collective-permute-start | bytes 1572872 | tf_op jit(solution)/shard_map/ppermute | solution.py:149
  139.7 73.0 %collective-permute-start.19 = (bf16[2,128,1024]{2,1,0:T(8,128)(2,1)S(1)}, bf16[2,128,1024]{2,1,0:T(8,128)(2,1)S(1)}, u32[]{:S(2)}, u32[]{:S(2)}) collective-permute-start(bf16[2,128,1024]{2,1,0:T(8,128)(2,1)S(1)} %add_convert_fusion.1), channel_id=1, source_target_pairs={{0,8},{4,12},{8,0},{12,4},{16,24},{20,28},{24,16},{28,20},{1,9},{5... | collective-permute-start | bytes 1572872 | tf_op jit(solution)/shard_map/ppermute | solution.py:149
  150.9 72.7 %collective-permute-start.22 = (bf16[2,128,1024]{2,1,0:T(8,128)(2,1)S(1)}, bf16[2,128,1024]{2,1,0:T(8,128)(2,1)S(1)}, u32[]{:S(2)}, u32[]{:S(2)}) collective-permute-start(bf16[2,128,1024]{2,1,0:T(8,128)(2,1)S(1)} %add_convert_fusion), channel_id=1, source_target_pairs={{0,8},{4,12},{8,0},{12,4},{16,24},{20,28},{24,16},{28,20},{1,9},{5... | collective-permute-start | bytes 1572872 | tf_op jit(solution)/shard_map/ppermute | solution.py:149
  162.1 61.5 %collective-permute-start.5 = (bf16[2,64,1024]{2,1,0:T(8,128)(2,1)S(1)}, bf16[2,64,1024]{2,1,0:T(8,128)(2,1)S(1)}, u32[]{:S(2)}, u32[]{:S(2)}) collective-permute-start(bf16[2,64,1024]{2,1,0:T(8,128)(2,1)S(1)} %add_convert_fusion.13), channel_id=1, source_target_pairs={{0,16},{4,20},{8,24},{12,28},{16,0},{20,4},{24,8},{28,12},{1,17},{... | collective-permute-start | bytes 786440 | tf_op jit(solution)/shard_map/ppermute | solution.py:149
  179.0 48.8 %collective-permute-start.8 = (bf16[2,64,1024]{2,1,0:T(8,128)(2,1)S(1)}, bf16[2,64,1024]{2,1,0:T(8,128)(2,1)S(1)}, u32[]{:S(2)}, u32[]{:S(2)}) collective-permute-start(bf16[2,64,1024]{2,1,0:T(8,128)(2,1)S(1)} %add_convert_fusion.12), channel_id=1, source_target_pairs={{0,16},{4,20},{8,24},{12,28},{16,0},{20,4},{24,8},{28,12},{1,17},{... | collective-permute-start | bytes 786440 | tf_op jit(solution)/shard_map/ppermute | solution.py:149
  195.9 33.3 %collective-permute-start.11 = (bf16[2,64,1024]{2,1,0:T(8,128)(2,1)S(1)}, bf16[2,64,1024]{2,1,0:T(8,128)(2,1)S(1)}, u32[]{:S(2)}, u32[]{:S(2)}) collective-permute-start(bf16[2,64,1024]{2,1,0:T(8,128)(2,1)S(1)} %add_convert_fusion.11), channel_id=1, source_target_pairs={{0,16},{4,20},{8,24},{12,28},{16,0},{20,4},{24,8},{28,12},{1,17},{... | collective-permute-start | bytes 786440 | tf_op jit(solution)/shard_map/ppermute | solution.py:149
  212.7 38.5 %collective-permute-start.14 = (bf16[2,64,1024]{2,1,0:T(8,128)(2,1)S(1)}, bf16[2,64,1024]{2,1,0:T(8,128)(2,1)S(1)}, u32[]{:S(2)}, u32[]{:S(2)}) collective-permute-start(bf16[2,64,1024]{2,1,0:T(8,128)(2,1)S(1)} %add_convert_fusion.10), channel_id=1, source_target_pairs={{0,16},{4,20},{8,24},{12,28},{16,0},{20,4},{24,8},{28,12},{1,17},{... | collective-permute-start | bytes 786440 | tf_op jit(solution)/shard_map/ppermute | solution.py:149
  223.6 33.2 %collective-permute-start.17 = (bf16[2,64,1024]{2,1,0:T(8,128)(2,1)S(1)}, bf16[2,64,1024]{2,1,0:T(8,128)(2,1)S(1)}, u32[]{:S(2)}, u32[]{:S(2)}) collective-permute-start(bf16[2,64,1024]{2,1,0:T(8,128)(2,1)S(1)} %add_convert_fusion.9), channel_id=1, source_target_pairs={{0,16},{4,20},{8,24},{12,28},{16,0},{20,4},{24,8},{28,12},{1,17},{... | collective-permute-start | bytes 786440 | tf_op jit(solution)/shard_map/ppermute | solution.py:149
  223.7 38.7 %collective-permute-start.20 = (bf16[2,64,1024]{2,1,0:T(8,128)(2,1)S(1)}, bf16[2,64,1024]{2,1,0:T(8,128)(2,1)S(1)}, u32[]{:S(2)}, u32[]{:S(2)}) collective-permute-start(bf16[2,64,1024]{2,1,0:T(8,128)(2,1)S(1)} %add_convert_fusion.8), channel_id=1, source_target_pairs={{0,16},{4,20},{8,24},{12,28},{16,0},{20,4},{24,8},{28,12},{1,17},{... | collective-permute-start | bytes 786440 | tf_op jit(solution)/shard_map/ppermute | solution.py:149
  227.8 40.1 %collective-permute-start.23 = (bf16[2,64,1024]{2,1,0:T(8,128)(2,1)S(1)}, bf16[2,64,1024]{2,1,0:T(8,128)(2,1)S(1)}, u32[]{:S(2)}, u32[]{:S(2)}) collective-permute-start(bf16[2,64,1024]{2,1,0:T(8,128)(2,1)S(1)} %add_convert_fusion.7), channel_id=1, source_target_pairs={{0,16},{4,20},{8,24},{12,28},{16,0},{20,4},{24,8},{28,12},{1,17},{... | collective-permute-start | bytes 786440 | tf_op jit(solution)/shard_map/ppermute | solution.py:149
  262.7 5.3 %copy-start.1 = (bf16[64,7168]{1,0:T(8,128)(2,1)}, bf16[64,7168]{1,0:T(8,128)(2,1)S(1)}, u32[]{:S(2)}) copy-start(bf16[64,7168]{1,0:T(8,128)(2,1)S(1)} %fusion.46) | copy-start | bytes 2752516

commit v2 on v1

v2 whole, which is shorter than its diff:
```python
import functools

import jax
import jax.numpy as jnp
from jax import lax
from jax.experimental import pallas as pl
from jax.experimental.pallas import tpu as pltpu
from jax.sharding import PartitionSpec as P

UNITS = 28
WIDTHS = (2, 2, 4, 4, 4, 4, 4, 2, 2)
BLOCK = 256
HOLD = 1
AHEAD = 2
LANE = 128


def interleave_kernel(x_ref, out_ref):
    source = lax.broadcasted_iota(jnp.int32, (LANE, 2 * LANE), 0)
    target = lax.broadcasted_iota(jnp.int32, (LANE, 2 * LANE), 1)
    for t in range(2):
        spacer = (target == 2 * source + t).astype(jnp.bfloat16)
        for j in range(x_ref.shape[1] // LANE):
            spaced = jnp.dot(
                x_ref[:, j * LANE : (j + 1) * LANE], spacer, preferred_element_type=jnp.float32
            )
            out_ref[t, :, 2 * j * LANE : 2 * (j + 1) * LANE] = spaced.astype(jnp.bfloat16)


def interleave(x):
    rows, depth = x.shape
    return pl.pallas_call(
        interleave_kernel,
        out_shape=jax.ShapeDtypeStruct((2, rows, 2 * depth), jnp.bfloat16),
        compiler_params=pltpu.CompilerParams(vmem_limit_bytes=32 * 2**20),
    )(x)


def partial_kernel(x_ref, d_ref, w_ref, u_ref, *rest):
    own_ref, other_ref = rest[-2:]
    half = own_ref.shape[1]
    w = w_ref[...].reshape(2 * w_ref.shape[0], w_ref.shape[2])
    u = u_ref[...].reshape(2 * u_ref.shape[0], u_ref.shape[2])
    for t in range(2):
        total = jnp.dot(x_ref[t], w, preferred_element_type=jnp.float32)
        total = total + jnp.dot(d_ref[t], u, preferred_element_type=jnp.float32)
        own_ref[t] = total[:half]
        other_ref[t] = total[half:].astype(jnp.bfloat16)


def partial_sums(x, d, w, u, end, width, block, after):
    _, rows, depth = x.shape
    inner = d.shape[2]
    first = (end - width) // block
    return pl.pallas_call(
        partial_kernel,
        grid=(width // block,),
        in_specs=[
            pl.BlockSpec((2, rows, depth), lambda j: (0, 0, 0)),
            pl.BlockSpec((2, rows, inner), lambda j: (0, 0, 0)),
            pl.BlockSpec((depth // 2, 2, block), lambda j: (0, 0, first + j)),
            pl.BlockSpec((inner // 2, 2, block), lambda j: (0, 0, first + j)),
        ]
        + [pl.BlockSpec(memory_space=pl.ANY)] * len(after),
        out_specs=[
            pl.BlockSpec((2, rows // 2, block), lambda j: (0, 0, j)),
            pl.BlockSpec((2, rows // 2, block), lambda j: (0, 0, j)),
        ],
        out_shape=[
            jax.ShapeDtypeStruct((2, rows // 2, width), jnp.float32),
            jax.ShapeDtypeStruct((2, rows // 2, width), jnp.bfloat16),
        ],
        compiler_params=pltpu.CompilerParams(vmem_limit_bytes=32 * 2**20),
        cost_estimate=pl.CostEstimate(
            flops=4 * rows * (depth + inner) * width,
            bytes_accessed=2 * (depth + inner) * width + 6 * rows * width,
            transcendentals=0,
        ),
    )(x, d, w, u, *after)


def reversed_bits(value, bits):
    out = 0
    for _ in range(bits):
        out = out * 2 + value % 2
        value //= 2
    return out


def body(
    requests,
    base_gate_up_weight,
    adapter_down_weight,
    adapter_up_weight,
    request_adapter,
    adapter_position,
    counts,
):
    rows, width = requests.shape
    groups = lax.axis_size("dp")
    lanes = lax.axis_size("tensor")
    holder_adapters, depth_part, rank_doubled = adapter_down_weight.shape
    rank = rank_doubled // 2
    extent = adapter_up_weight.shape[3]
    capacity = rows // 8
    buffer = groups * capacity
    group = lax.axis_index("dp")
    lane = lax.axis_index("tensor")
    bits = groups.bit_length() - 1
    f32, bf16, i32 = jnp.float32, jnp.bfloat16, jnp.int32

    match = request_adapter[:, None] == jnp.arange(adapter_position.shape[0], dtype=i32)[None, :]
    slot = jnp.sum(jnp.where(match, adapter_position[None, :], 0), axis=1)
    owner = slot // holder_adapters
    local = slot % holder_adapters
    owner_hot = (owner[:, None] == jnp.arange(groups, dtype=i32)[None, :]).astype(i32)
    place = jnp.sum(owner_hot * (jnp.cumsum(owner_hot, axis=0) - 1), axis=1)
    target = owner * capacity + place
    select = (target[None, :] == jnp.arange(buffer, dtype=i32)[:, None]).astype(bf16)
    row_index = jnp.arange(rows, dtype=i32)
    piece = lax.dynamic_slice_in_dim(requests, lane * depth_part, depth_part, 1)
    column = jnp.arange(LANE, dtype=i32)[None, :]
    labels = jnp.where(column == 0, local[:, None], jnp.where(column == 1, row_index[:, None], 0))
    outgoing = jnp.dot(
        select, jnp.concatenate([piece, labels.astype(bf16)], axis=1), preferred_element_type=f32
    ).astype(bf16)

    part = width // groups
    share = rows // lanes
    extra = capacity * outgoing.shape[1] // part
    mine = lax.dynamic_slice_in_dim(requests, lane * share, share, 0)
    sent = jnp.concatenate(
        [
            mine.reshape(share, groups, part).transpose(1, 0, 2),
            outgoing.reshape(groups, extra, part),
        ],
        axis=1,
    )
    came = lax.all_to_all(sent, "dp", split_axis=0, concat_axis=0, tiled=True)
    spread = came[:, :share]
    arrived = came[:, share:].reshape(buffer, outgoing.shape[1])

    def over_lanes(array, mask):
        return lax.ppermute(array, "tensor", [(i, i ^ mask) for i in range(lanes)])

    spread = jnp.stack([spread] + [over_lanes(spread, k) for k in range(1, lanes)])

    which = arrived[:, depth_part].astype(i32)
    place_row = arrived[:, depth_part + 1].astype(i32)
    mine = which[:, None] == jnp.arange(holder_adapters, dtype=i32)[None, :]
    routed = arrived[:, :depth_part]
    spaced = jnp.where(mine[:, :, None], routed[:, None, :], jnp.zeros((), bf16))
    part_down = jnp.dot(
        spaced.reshape(buffer, holder_adapters * depth_part),
        adapter_down_weight.reshape(holder_adapters * depth_part, rank_doubled),
        preferred_element_type=f32,
    )
    total_down = part_down
    for k in range(1, lanes):
        total_down = total_down + over_lanes(part_down, k)
    down = total_down.astype(bf16)
    whole_row = (jnp.arange(buffer, dtype=i32) // capacity) * rows + place_row
    to_row = (jnp.arange(groups * rows, dtype=i32)[:, None] == whole_row[None, :]).astype(bf16)
    terms = []
    for t in range(2):
        spacer = 2 * jnp.arange(rank, dtype=i32)[:, None] + t == jnp.arange(2 * rank)[None, :]
        apart = jnp.dot(
            down[:, t * rank : (t + 1) * rank], spacer.astype(bf16), preferred_element_type=f32
        ).astype(bf16)
        apart = jnp.where(mine[:, :, None], apart[:, None, :], jnp.zeros((), bf16))
        apart = apart.reshape(buffer, holder_adapters * 2 * rank)
        terms.append(jnp.dot(to_row, apart, preferred_element_type=f32).astype(bf16))
    terms = jnp.stack(terms).reshape(2, groups, rows, -1)

    order = [reversed_bits(i, bits) for i in range(groups)]
    x = jnp.concatenate(
        [
            lax.dynamic_slice(spread, (lane ^ k, group ^ b, 0, 0), (1, 1, share, part))[0, 0]
            for b in order
            for k in range(lanes)
        ],
        0,
    )
    x = interleave(x)
    d = jnp.concatenate([lax.dynamic_index_in_dim(terms, group ^ b, 1, False) for b in order], 1)
    adapter_up = adapter_up_weight.reshape(holder_adapters * rank, 2, extent)

    live = row_index < counts[group]
    unit = extent // UNITS
    ends = [unit * sum(WIDTHS[: i + 1]) for i in range(len(WIDTHS))]
    count = len(WIDTHS)
    stages = [[] for _ in WIDTHS]
    pieces = []

    def send(array, mask):
        return lax.ppermute(array, "dp", [(i, i ^ mask) for i in range(groups)])

    def begin(chunk, after):
        own, other = partial_sums(
            x, d, base_gate_up_weight, adapter_up, ends[chunk], unit * WIDTHS[chunk], BLOCK, after
        )
        stages[chunk] = [own, send(other, 1)]

    def advance(chunk, stage):
        size = groups * rows >> (stage + 1)
        parts = [a[:, size : 2 * size].astype(f32) for a in stages[chunk]]
        message = functools.reduce(jnp.add, parts).astype(bf16)
        stages[chunk].append(send(message, 1 << stage))
        return message

    def finish(chunk, after):
        if HOLD:
            stages[chunk], after = lax.optimization_barrier((stages[chunk], after))
        gate, up = functools.reduce(jnp.add, [a[:, :rows].astype(f32) for a in stages[chunk]])
        hidden = jnp.where(live[:, None], jax.nn.silu(gate) * up, 0.0)
        pieces.append(hidden.astype(bf16))

    for chunk in range(min(AHEAD, count)):
        begin(chunk, [])
    for slot in range(count + bits - 1):
        after = [
            advance(slot - stage + 1, stage)
            for stage in range(1, bits)
            if 0 <= slot - stage + 1 < count
        ]
        if slot + AHEAD < count:
            begin(slot + AHEAD, after)
        if 0 <= slot - bits + 1 < count:
            finish(slot - bits + 1, after)
    return jnp.concatenate(pieces, axis=1)


def solution(mesh):
    placed = (
        P("dp", None),
        P("dp", None, "tensor"),
        P("dp", "tensor", None),
        P("dp", None, None, "tensor"),
        P("dp"),
        P(),
        P(),
    )
    return jax.shard_map(
        body, mesh=mesh, in_specs=placed, out_specs=P("dp", "tensor"), check_vma=False
    )
```

time: 270 us -> 203 us (0.75)
  waiting for transfers between devices: 138 us -> 84.7 us
  local copies, waits for them, and re-layouts: 39.6 us -> 4.52 us
  Pallas kernels: 40.2 us -> 66.9 us
  other arithmetic: 21.4 us -> 7.69 us
  starting transfers between devices: 24.5 us -> 33.7 us
    ppermute x24 -> x33, waiting for transfers between devices: 123 us -> 66.5 us  [the longest x27 61.1 us: send(): return lax.ppermute(array, 'dp', [(i, i ^ mask) for i in range(groups)])]
    unnamed x15 -> x48, local copies, waits for them, and re-layouts: 36.5 us -> 2.89 us
    pallas_call x7 -> x10, Pallas kernels: 40.2 us -> 66.9 us  [the longest x9 65.7 us: partial_sums(): pl.pallas_call(partial_kernel, grid=(width // block,), in_specs=[pl.Block...]
    ppermute x24 -> x33, starting transfers between devices: 13.1 us -> 27.4 us  [the longest x27 20.3 us: send(): return lax.ppermute(array, 'dp', [(i, i ^ mask) for i in range(groups)])]
    convert_element_type x14 -> x18, other arithmetic: 11.8 us -> 1.71 us  [advance(): message = functools.reduce(jnp.add, parts).astype(bf16)]
    all_to_all x2 -> x1, starting transfers between devices: 11.4 us -> 6.33 us  [body(): came = lax.all_to_all(sent, 'dp', split_axis=0, concat_axis=0, tiled=True)]
    add x7 -> x10, other arithmetic: 5.74 us -> 0.92 us  [the longest x9 0.91 us: finish(): functools.reduce(jnp.add, [a[:, :rows].astype(f32) for a in stages[chunk]])]
    all_to_all x2 -> x1, waiting for transfers between devices: 15.1 us -> 18.2 us  [body(): came = lax.all_to_all(sent, 'dp', split_axis=0, concat_axis=0, tiled=True)]
  transfers between devices with their start and end apart: 26 -> 34, of which waited for: 15 -> 15; matrix products, arithmetic and copies ran while one was open for 23% -> 5% of each run, Pallas kernels for 9% -> 30%
where the time goes in v2:
time: 203 us
  waiting for transfers between devices  84.7 us (42%)
  Pallas kernels  66.9 us (33%)
  starting transfers between devices  33.7 us (17%)
  other arithmetic  7.69 us (4%)
  local copies, waits for them, and re-layouts  4.52 us (2%)
  matrix products  4.4 us (2%)
    pallas_call x9, Pallas kernels, partial_sums(): pl.pallas_call(partial_kernel, grid=(width // block,), in_specs=[pl.Block...  65.7 us
    ppermute x27, waiting for transfers between devices, send(): return lax.ppermute(array, 'dp', [(i, i ^ mask) for i in range(groups)])  61.1 us
    ppermute x27, starting transfers between devices, send(): return lax.ppermute(array, 'dp', [(i, i ^ mask) for i in range(groups)])  20.3 us
    all_to_all x1, waiting for transfers between devices, body(): came = lax.all_to_all(sent, 'dp', split_axis=0, concat_axis=0, tiled=True)  18.2 us
    ppermute x6, starting transfers between devices, over_lanes(): return lax.ppermute(array, 'tensor', [(i, i ^ mask) for i in range(lanes)])  7.11 us
    all_to_all x1, starting transfers between devices, body(): came = lax.all_to_all(sent, 'dp', split_axis=0, concat_axis=0, tiled=True)  6.33 us
    ppermute x6, waiting for transfers between devices, over_lanes(): return lax.ppermute(array, 'tensor', [(i, i ^ mask) for i in range(lanes)])  5.46 us
  transfers between devices with their start and end apart: 34, of which 15 were waited for; matrix products, arithmetic and copies ran while one was open for 5% of the time, Pallas kernels for 30%

profile of v2, /device:TPU:0, one launch (start us, length us, event | category | flops | bytes accessed | tf_op | source)
XLA Modules:
  0.0 203.0 jit_solution(10727762837617597046)
XLA Ops:
  0.0 0.9 select_reduce_fusion.1
  2.4 0.9 pad_maximum_fusion.1
  3.3 6.3 %all-to-all-start = ((bf16[8,33,1024]{2,1,0:T(8,128)(2,1)}), bf16[8,33,1024]{2,1,0:T(8,128)(2,1)S(1)}, u32[]{:S(2)}, u32[]{:S(2)}) async-start(bf16[8,33,1024]{2,1,0:T(8,128)(2,1)} %pad_maximum_fusion.1), calls=%async_computation | async-start | bytes 1310720 | tf_op jit(solution)/shard_map/all_to_all | solution.py:139
  9.6 18.2 %all-to-all-done = bf16[8,33,1024]{2,1,0:T(8,128)(2,1)S(1)} async-done(((bf16[8,33,1024]{2,1,0:T(8,128)(2,1)}), bf16[8,33,1024]{2,1,0:T(8,128)(2,1)S(1)}, u32[]{:S(2)}, u32[]{:S(2)}) %all-to-all-start) | async-done | bytes 540704 | tf_op jit(solution)/shard_map/all_to_all | solution.py:139
  27.8 2.5 %collective-permute-start.2 = (bf16[8,16,1024]{2,1,0:T(8,128)(2,1)S(1)}, bf16[8,16,1024]{2,1,0:T(8,128)(2,1)S(1)}, u32[]{:S(2)}, u32[]{:S(2)}) collective-permute-start(bf16[8,16,1024]{2,1,0:T(8,128)(2,1)S(1)} %get-tuple-element.116), channel_id=1, source_target_pairs={{0,3},{1,2},{2,1},{3,0},{4,7},{5,6},{6,5},{7,4},{8,11},{9,10},{10,... | collective-permute-start | bytes 786440 | tf_op jit(solution)/shard_map/ppermute | solution.py:144
  30.3 0.5 collective-permute-start.1
  31.4 2.9 %fusion.3 = f32[64,128]{1,0:T(8,128)S(1)} fusion(bf16[8,2048,128]{2,1,0:T(8,128)(2,1)} %param.9, pred[64,8]{0,1:T(8,128)(4,1)S(1)} %iota_compare_fusion.11, bf16[64,2048]{1,0:T(8,128)(2,1)S(1)} %slice.320), kind=kOutput, calls=%fused_computation.22 | convolution fusion | flops 269484032 | bytes 4489728 | tf_op jit(solution)/shard_map/dot_general | solution.py:153
  34.4 1.6 collective-permute-start.5
  35.9 0.5 collective-permute-start.4
  36.4 1.5 collective-permute-start.3
  38.0 1.3 collective-permute-done.5
  39.4 0.5 collective-permute-start
  39.9 3.8 %collective-permute-done.4 = f32[64,128]{1,0:T(8,128)S(1)} collective-permute-done((f32[64,128]{1,0:T(8,128)S(1)}, f32[64,128]{1,0:T(8,128)S(1)}, u32[]{:S(2)}, u32[]{:S(2)}) %collective-permute-start.4) | collective-permute-done | bytes 32800 | tf_op jit(solution)/shard_map/ppermute | solution.py:144
  44.2 0.4 convolution_convert_fusion.1
  46.6 1.2 shard_map.73.x_ref
  48.2 1.2 slice-done.2
  49.5 0.7 slice-done.3
  50.1 5.0 %shard_map.74 = (f32[2,256,512]{2,1,0:T(8,128)S(1)}, bf16[2,256,512]{2,1,0:T(8,128)(2,1)S(1)}) custom-call(bf16[2,512,2048]{2,1,0:T(8,128)(2,1)S(1)} %shard_map.73.x_ref, bf16[2,512,1024]{2,1,0:T(8,128)(2,1)S(1)} %bitcast_dynamic-update-slice_fusion.d_ref, bf16[1024,2,7168]{2,1,0:T(2,128)(2,1)} %w_ref.17, bf16[512,2,7168]{2,1,0:T(2,128)(2,1)S(1)} %bitcast.261), custom_call_target="tpu_custom_call" | custom-call | flops 3221225472 | bytes 4718592 | tf_op jit(solution)/shard_map/pallas_call | solution.py:55
  55.3 5.0 %shard_map.76 = (f32[2,256,512]{2,1,0:T(8,128)S(1)}, bf16[2,256,512]{2,1,0:T(8,128)(2,1)S(1)}) custom-call(bf16[2,512,2048]{2,1,0:T(8,128)(2,1)S(1)} %shard_map.73.x_ref, bf16[2,512,1024]{2,1,0:T(8,128)(2,1)S(1)} %bitcast_dynamic-update-slice_fusion.d_ref, bf16[1024,2,7168]{2,1,0:T(2,128)(2,1)} %w_ref.17, bf16[512,2,7168]{2,1,0:T(2,128)(2,1)S(1)} %bitcast.262), custom_call_target="tpu_custom_call" | custom-call | flops 3221225472 | bytes 4718592 | tf_op jit(solution)/shard_map/pallas_call | solution.py:55
  60.3 0.5 collective-permute-start.10
  60.9 0.6 dynamic_slice.130
  61.4 0.6 iota_compare_fusion.14
  62.5 2.0 collective-permute-start.11
  64.4 9.0 %shard_map.75 = (f32[2,256,1024]{2,1,0:T(8,128)S(1)}, bf16[2,256,1024]{2,1,0:T(8,128)(2,1)S(1)}) custom-call(bf16[2,512,2048]{2,1,0:T(8,128)(2,1)S(1)} %shard_map.73.x_ref, bf16[2,512,1024]{2,1,0:T(8,128)(2,1)S(1)} %bitcast_dynamic-update-slice_fusion.d_ref, bf16[1024,2,7168]{2,1,0:T(2,128)(2,1)} %w_ref.17, bf16[512,2,7168]{2,1,0:T(2,128)(2,1)} %bitcast.252, ...), custom_call_target="tpu_custom_call" | custom-call | flops 6442450944 | bytes 9437184 | tf_op jit(solution)/shard_map/pallas_call | solution.py:55
  73.6 0.5 collective-permute-start.8
  74.1 2.0 %collective-permute-done.11 = bf16[2,128,512]{2,1,0:T(8,128)(2,1)S(1)} collective-permute-done((bf16[2,128,512]{2,1,0:T(8,128)(2,1)S(1)}, bf16[2,128,512]{2,1,0:T(8,128)(2,1)S(1)}, u32[]{:S(2)}, u32[]{:S(2)}) %collective-permute-start.11) | collective-permute-done | bytes 262176 | tf_op jit(solution)/shard_map/ppermute | solution.py:196
  76.2 0.6 collective-permute-start.12
  76.7 9.2 %shard_map.77 = (f32[2,256,1024]{2,1,0:T(8,128)S(1)}, bf16[2,256,1024]{2,1,0:T(8,128)(2,1)S(1)}) custom-call(bf16[2,512,2048]{2,1,0:T(8,128)(2,1)S(1)} %shard_map.73.x_ref, bf16[2,512,1024]{2,1,0:T(8,128)(2,1)S(1)} %bitcast_dynamic-update-slice_fusion.d_ref, bf16[1024,2,7168]{2,1,0:T(2,128)(2,1)} %w_ref.17, bf16[512,2,7168]{2,1,0:T(2,128)(2,1)} %bitcast.253, ...), custom_call_target="tpu_custom_call" | custom-call | flops 6442450944 | bytes 9437184 | tf_op jit(solution)/shard_map/pallas_call | solution.py:55
  86.2 1.8 collective-permute-start.14
  88.0 9.0 %shard_map.78 = (f32[2,256,1024]{2,1,0:T(8,128)S(1)}, bf16[2,256,1024]{2,1,0:T(8,128)(2,1)S(1)}) custom-call(bf16[2,512,2048]{2,1,0:T(8,128)(2,1)S(1)} %shard_map.73.x_ref, bf16[2,512,1024]{2,1,0:T(8,128)(2,1)S(1)} %bitcast_dynamic-update-slice_fusion.d_ref, bf16[1024,2,7168]{2,1,0:T(2,128)(2,1)} %w_ref.17, bf16[512,2,7168]{2,1,0:T(2,128)(2,1)} %bitcast.254, ...), custom_call_target="tpu_custom_call" | custom-call | flops 6442450944 | bytes 9437184 | tf_op jit(solution)/shard_map/pallas_call | solution.py:55
  98.0 2.6 %collective-permute-done.14 = bf16[2,128,1024]{2,1,0:T(8,128)(2,1)S(1)} collective-permute-done((bf16[2,128,1024]{2,1,0:T(8,128)(2,1)S(1)}, bf16[2,128,1024]{2,1,0:T(8,128)(2,1)S(1)}, u32[]{:S(2)}, u32[]{:S(2)}) %collective-permute-start.14) | collective-permute-done | bytes 524320 | tf_op jit(solution)/shard_map/ppermute | solution.py:196
  100.7 2.9 %collective-permute-start.15 = (bf16[2,64,1024]{2,1,0:T(8,128)(2,1)S(1)}, bf16[2,64,1024]{2,1,0:T(8,128)(2,1)S(1)}, u32[]{:S(2)}, u32[]{:S(2)}) collective-permute-start(bf16[2,64,1024]{2,1,0:T(8,128)(2,1)S(1)} %add_convert_fusion.11.rest_1_), channel_id=1, source_target_pairs={{0,16},{4,20},{8,24},{12,28},{16,0},{20,4},{24,8},{28,12},{1,17},{... | collective-permute-start | bytes 786440 | tf_op jit(solution)/shard_map/ppermute | solution.py:196
  103.5 9.0 %shard_map.79 = (f32[2,256,1024]{2,1,0:T(8,128)S(1)}, bf16[2,256,1024]{2,1,0:T(8,128)(2,1)S(1)}) custom-call(bf16[2,512,2048]{2,1,0:T(8,128)(2,1)S(1)} %shard_map.73.x_ref, bf16[2,512,1024]{2,1,0:T(8,128)(2,1)S(1)} %bitcast_dynamic-update-slice_fusion.d_ref, bf16[1024,2,7168]{2,1,0:T(2,128)(2,1)} %w_ref.17, bf16[512,2,7168]{2,1,0:T(2,128)(2,1)} %bitcast.255, ...), custom_call_target="tpu_custom_call" | custom-call | flops 6442450944 | bytes 9437184 | tf_op jit(solution)/shard_map/pallas_call | solution.py:55
  112.8 4.6 %collective-permute-done.17 = bf16[2,128,1024]{2,1,0:T(8,128)(2,1)S(1)} collective-permute-done((bf16[2,128,1024]{2,1,0:T(8,128)(2,1)S(1)}, bf16[2,128,1024]{2,1,0:T(8,128)(2,1)S(1)}, u32[]{:S(2)}, u32[]{:S(2)}) %collective-permute-start.17) | collective-permute-done | bytes 524320 | tf_op jit(solution)/shard_map/ppermute | solution.py:196
  118.0 2.5 %collective-permute-start.20 = (bf16[2,128,1024]{2,1,0:T(8,128)(2,1)S(1)}, bf16[2,128,1024]{2,1,0:T(8,128)(2,1)S(1)}, u32[]{:S(2)}, u32[]{:S(2)}) collective-permute-start(bf16[2,128,1024]{2,1,0:T(8,128)(2,1)S(1)} %add_convert_fusion.2.rest_0_), channel_id=1, source_target_pairs={{0,8},{4,12},{8,0},{12,4},{16,24},{20,28},{24,16},{28,20},{1,9},{5... | collective-permute-start | bytes 1572872 | tf_op jit(solution)/shard_map/ppermute | solution.py:196
  120.5 9.0 %shard_map.80 = (f32[2,256,1024]{2,1,0:T(8,128)S(1)}, bf16[2,256,1024]{2,1,0:T(8,128)(2,1)S(1)}) custom-call(bf16[2,512,2048]{2,1,0:T(8,128)(2,1)S(1)} %shard_map.73.x_ref, bf16[2,512,1024]{2,1,0:T(8,128)(2,1)S(1)} %bitcast_dynamic-update-slice_fusion.d_ref, bf16[1024,2,7168]{2,1,0:T(2,128)(2,1)} %w_ref.17, bf16[512,2,7168]{2,1,0:T(2,128)(2,1)} %bitcast.256, ...), custom_call_target="tpu_custom_call" | custom-call | flops 6442450944 | bytes 9437184 | tf_op jit(solution)/shard_map/pallas_call | solution.py:55
  129.9 7.6 %collective-permute-done.20 = bf16[2,128,1024]{2,1,0:T(8,128)(2,1)S(1)} collective-permute-done((bf16[2,128,1024]{2,1,0:T(8,128)(2,1)S(1)}, bf16[2,128,1024]{2,1,0:T(8,128)(2,1)S(1)}, u32[]{:S(2)}, u32[]{:S(2)}) %collective-permute-start.20) | collective-permute-done | bytes 524320 | tf_op jit(solution)/shard_map/ppermute | solution.py:196
  137.9 2.2 %collective-permute-start.23 = (bf16[2,128,1024]{2,1,0:T(8,128)(2,1)S(1)}, bf16[2,128,1024]{2,1,0:T(8,128)(2,1)S(1)}, u32[]{:S(2)}, u32[]{:S(2)}) collective-permute-start(bf16[2,128,1024]{2,1,0:T(8,128)(2,1)S(1)} %add_convert_fusion.1.rest_0_), channel_id=1, source_target_pairs={{0,8},{4,12},{8,0},{12,4},{16,24},{20,28},{24,16},{28,20},{1,9},{5... | collective-permute-start | bytes 1572872 | tf_op jit(solution)/shard_map/ppermute | solution.py:196
  140.1 5.2 %shard_map.81 = (f32[2,256,512]{2,1,0:T(8,128)S(1)}, bf16[2,256,512]{2,1,0:T(8,128)(2,1)S(1)}) custom-call(bf16[2,512,2048]{2,1,0:T(8,128)(2,1)S(1)} %shard_map.73.x_ref, bf16[2,512,1024]{2,1,0:T(8,128)(2,1)S(1)} %bitcast_dynamic-update-slice_fusion.d_ref, bf16[1024,2,7168]{2,1,0:T(2,128)(2,1)} %w_ref.17, bf16[512,2,7168]{2,1,0:T(2,128)(2,1)} %bitcast.257, ...), custom_call_target="tpu_custom_call" | custom-call | flops 3221225472 | bytes 4718592 | tf_op jit(solution)/shard_map/pallas_call | solution.py:55
  145.6 10.6 %collective-permute-done.23 = bf16[2,128,1024]{2,1,0:T(8,128)(2,1)S(1)} collective-permute-done((bf16[2,128,1024]{2,1,0:T(8,128)(2,1)S(1)}, bf16[2,128,1024]{2,1,0:T(8,128)(2,1)S(1)}, u32[]{:S(2)}, u32[]{:S(2)}) %collective-permute-start.23) | collective-permute-done | bytes 524320 | tf_op jit(solution)/shard_map/ppermute | solution.py:196
  156.7 2.5 %collective-permute-start.29 = (bf16[2,128,512]{2,1,0:T(8,128)(2,1)S(1)}, bf16[2,128,512]{2,1,0:T(8,128)(2,1)S(1)}, u32[]{:S(2)}, u32[]{:S(2)}) collective-permute-start(bf16[2,128,512]{2,1,0:T(8,128)(2,1)S(1)} %add_convert_fusion.7), channel_id=1, source_target_pairs={{0,8},{4,12},{8,0},{12,4},{16,24},{20,28},{24,16},{28,20},{1,9},{5... | collective-permute-start | bytes 786440 | tf_op jit(solution)/shard_map/ppermute | solution.py:196
  159.4 5.2 %shard_map.82 = (f32[2,256,512]{2,1,0:T(8,128)S(1)}, bf16[2,256,512]{2,1,0:T(8,128)(2,1)S(1)}) custom-call(bf16[2,512,2048]{2,1,0:T(8,128)(2,1)S(1)} %shard_map.73.x_ref, bf16[2,512,1024]{2,1,0:T(8,128)(2,1)S(1)} %bitcast_dynamic-update-slice_fusion.d_ref, bf16[1024,2,7168]{2,1,0:T(2,128)(2,1)} %w_ref.17, bf16[512,2,7168]{2,1,0:T(2,128)(2,1)} %bitcast.258, ...), custom_call_target="tpu_custom_call" | custom-call | flops 3221225472 | bytes 4718592 | tf_op jit(solution)/shard_map/pallas_call | solution.py:55
  165.0 8.0 %collective-permute-done.29 = bf16[2,128,512]{2,1,0:T(8,128)(2,1)S(1)} collective-permute-done((bf16[2,128,512]{2,1,0:T(8,128)(2,1)S(1)}, bf16[2,128,512]{2,1,0:T(8,128)(2,1)S(1)}, u32[]{:S(2)}, u32[]{:S(2)}) %collective-permute-start.29) | collective-permute-done | bytes 262176 | tf_op jit(solution)/shard_map/ppermute | solution.py:196
  173.1 9.8 %collective-permute-done.26 = bf16[2,128,1024]{2,1,0:T(8,128)(2,1)S(1)} collective-permute-done((bf16[2,128,1024]{2,1,0:T(8,128)(2,1)S(1)}, bf16[2,128,1024]{2,1,0:T(8,128)(2,1)S(1)}, u32[]{:S(2)}, u32[]{:S(2)}) %collective-permute-start.26) | collective-permute-done | bytes 524320 | tf_op jit(solution)/shard_map/ppermute | solution.py:196
  183.2 2.3 %collective-permute-start.31 = (bf16[2,128,512]{2,1,0:T(8,128)(2,1)S(1)}, bf16[2,128,512]{2,1,0:T(8,128)(2,1)S(1)}, u32[]{:S(2)}, u32[]{:S(2)}) collective-permute-start(bf16[2,128,512]{2,1,0:T(8,128)(2,1)S(1)} %add_convert_fusion.5), channel_id=1, source_target_pairs={{0,8},{4,12},{8,0},{12,4},{16,24},{20,28},{24,16},{28,20},{1,9},{5... | collective-permute-start | bytes 786440 | tf_op jit(solution)/shard_map/ppermute | solution.py:196
  185.7 8.7 %collective-permute-done.27 = bf16[2,64,1024]{2,1,0:T(8,128)(2,1)S(1)} collective-permute-done((bf16[2,64,1024]{2,1,0:T(8,128)(2,1)S(1)}, bf16[2,64,1024]{2,1,0:T(8,128)(2,1)S(1)}, u32[]{:S(2)}, u32[]{:S(2)}) %collective-permute-start.27) | collective-permute-done | bytes 262176 | tf_op jit(solution)/shard_map/ppermute | solution.py:196
  195.5 6.7 %collective-permute-done.32 = bf16[2,64,512]{2,1,0:T(8,128)(2,1)S(1)} collective-permute-done((bf16[2,64,512]{2,1,0:T(8,128)(2,1)S(1)}, bf16[2,64,512]{2,1,0:T(8,128)(2,1)S(1)}, u32[]{:S(2)}, u32[]{:S(2)}) %collective-permute-start.32) | collective-permute-done | bytes 131104 | tf_op jit(solution)/shard_map/ppermute | solution.py:196
  202.3 0.7 constant_dynamic-update-slice_fusion.32
  (158 shorter events, 10.9 us)
Async XLA Ops:
  0.0 1.3 copy-start
  3.3 24.5 %all-to-all-start = ((bf16[8,33,1024]{2,1,0:T(8,128)(2,1)}), bf16[8,33,1024]{2,1,0:T(8,128)(2,1)S(1)}, u32[]{:S(2)}, u32[]{:S(2)}) async-start(bf16[8,33,1024]{2,1,0:T(8,128)(2,1)} %pad_maximum_fusion.1), calls=%async_computation | async-start | bytes 1310720 | tf_op jit(solution)/shard_map/all_to_all | solution.py:139
  27.8 17.6 %collective-permute-start.2 = (bf16[8,16,1024]{2,1,0:T(8,128)(2,1)S(1)}, bf16[8,16,1024]{2,1,0:T(8,128)(2,1)S(1)}, u32[]{:S(2)}, u32[]{:S(2)}) collective-permute-start(bf16[8,16,1024]{2,1,0:T(8,128)(2,1)S(1)} %get-tuple-element.116), channel_id=1, source_target_pairs={{0,3},{1,2},{2,1},{3,0},{4,7},{5,6},{6,5},{7,4},{8,11},{9,10},{10,... | collective-permute-start | bytes 786440 | tf_op jit(solution)/shard_map/ppermute | solution.py:144
  30.3 15.1 %collective-permute-start.1 = (bf16[8,16,1024]{2,1,0:T(8,128)(2,1)S(1)}, bf16[8,16,1024]{2,1,0:T(8,128)(2,1)S(1)}, u32[]{:S(2)}, u32[]{:S(2)}) collective-permute-start(bf16[8,16,1024]{2,1,0:T(8,128)(2,1)S(1)} %get-tuple-element.116), channel_id=1, source_target_pairs={{0,2},{1,3},{2,0},{3,1},{4,6},{5,7},{6,4},{7,5},{8,10},{9,11},{10,... | collective-permute-start | bytes 786440 | tf_op jit(solution)/shard_map/ppermute | solution.py:144
  34.4 5.0 %collective-permute-start.5 = (f32[64,128]{1,0:T(8,128)S(1)}, f32[64,128]{1,0:T(8,128)S(1)}, u32[]{:S(2)}, u32[]{:S(2)}) collective-permute-start(f32[64,128]{1,0:T(8,128)S(1)} %fusion.3), channel_id=1, source_target_pairs={{0,3},{1,2},{2,1},{3,0},{4,7},{5,6},{6,5},{7,4},{8,11},{9,10},{10,... | collective-permute-start | bytes 98312 | tf_op jit(solution)/shard_map/ppermute | solution.py:144
  35.9 7.7 %collective-permute-start.4 = (f32[64,128]{1,0:T(8,128)S(1)}, f32[64,128]{1,0:T(8,128)S(1)}, u32[]{:S(2)}, u32[]{:S(2)}) collective-permute-start(f32[64,128]{1,0:T(8,128)S(1)} %fusion.3), channel_id=1, source_target_pairs={{0,2},{1,3},{2,0},{3,1},{4,6},{5,7},{6,4},{7,5},{8,10},{9,11},{10,... | collective-permute-start | bytes 98312 | tf_op jit(solution)/shard_map/ppermute | solution.py:144
  36.4 7.2 %collective-permute-start.3 = (f32[64,128]{1,0:T(8,128)S(1)}, f32[64,128]{1,0:T(8,128)S(1)}, u32[]{:S(2)}, u32[]{:S(2)}) collective-permute-start(f32[64,128]{1,0:T(8,128)S(1)} %fusion.3), channel_id=1, source_target_pairs={{0,1},{1,0},{2,3},{3,2},{4,5},{5,4},{6,7},{7,6},{8,9},{9,8},{10,11... | collective-permute-start | bytes 98312 | tf_op jit(solution)/shard_map/ppermute | solution.py:144
  39.4 6.4 %collective-permute-start = (bf16[8,16,1024]{2,1,0:T(8,128)(2,1)S(1)}, bf16[8,16,1024]{2,1,0:T(8,128)(2,1)S(1)}, u32[]{:S(2)}, u32[]{:S(2)}) collective-permute-start(bf16[8,16,1024]{2,1,0:T(8,128)(2,1)S(1)} %get-tuple-element.116), channel_id=1, source_target_pairs={{0,1},{1,0},{2,3},{3,2},{4,5},{5,4},{6,7},{7,6},{8,9},{9,8},{10,11... | collective-permute-start | bytes 786440 | tf_op jit(solution)/shard_map/ppermute | solution.py:144
  44.7 3.2 %slice-start = ((s8[14680064]{0:T(1024)(128)(4,1)}), s8[4194304]{0:T(1024)(128)(4,1)S(1)}, s32[]{:S(2)}) async-start(s8[14680064]{0:T(1024)(128)(4,1)} %bitcast.259), calls=%async_computation.1 | async-start | bytes 8388608
  45.2 3.1 %slice-start.1 = ((s8[14680064]{0:T(1024)(128)(4,1)}), s8[4194304]{0:T(1024)(128)(4,1)S(1)}, s32[]{:S(2)}) async-start(s8[14680064]{0:T(1024)(128)(4,1)} %bitcast.259), calls=%async_computation.2 | async-start | bytes 8388608
  45.3 4.2 %slice-start.2 = ((s8[14680064]{0:T(1024)(128)(4,1)}), s8[4194304]{0:T(1024)(128)(4,1)S(1)}, s32[]{:S(2)}) async-start(s8[14680064]{0:T(1024)(128)(4,1)} %bitcast.259), calls=%async_computation.3 | async-start | bytes 8388608
  45.8 4.4 %slice-start.3 = ((s8[14680064]{0:T(1024)(128)(4,1)}), s8[2097152]{0:T(1024)(128)(4,1)S(1)}, s32[]{:S(2)}) async-start(s8[14680064]{0:T(1024)(128)(4,1)} %bitcast.259), calls=%async_computation.4 | async-start | bytes 4194304
  55.2 5.7 %copy-start.3 = (s32[8]{0:T(128)S(1)}, s32[8]{0:T(128)}, u32[]{:S(2)}) copy-start(s32[8]{0:T(128)} %param.13) | copy-start | bytes 100
  55.2 6.9 %collective-permute-start.6 = (bf16[2,256,512]{2,1,0:T(8,128)(2,1)S(1)}, bf16[2,256,512]{2,1,0:T(8,128)(2,1)S(1)}, u32[]{:S(2)}, u32[]{:S(2)}) collective-permute-start(bf16[2,256,512]{2,1,0:T(8,128)(2,1)S(1)} %get-tuple-element.60), channel_id=1, source_target_pairs={{0,4},{4,0},{8,12},{12,8},{16,20},{20,16},{24,28},{28,24},{1,5},{5... | collective-permute-start | bytes 1572872 | tf_op jit(solution)/shard_map/ppermute | solution.py:196
  60.3 2.1 %collective-permute-start.10 = (bf16[2,256,512]{2,1,0:T(8,128)(2,1)S(1)}, bf16[2,256,512]{2,1,0:T(8,128)(2,1)S(1)}, u32[]{:S(2)}, u32[]{:S(2)}) collective-permute-start(bf16[2,256,512]{2,1,0:T(8,128)(2,1)S(1)} %get-tuple-element.64), channel_id=1, source_target_pairs={{0,4},{4,0},{8,12},{12,8},{16,20},{20,16},{24,28},{28,24},{1,5},{5... | collective-permute-start | bytes 1572872 | tf_op jit(solution)/shard_map/ppermute | solution.py:196
  62.2 11.3 %collective-permute-start.7 = (bf16[2,128,512]{2,1,0:T(8,128)(2,1)S(1)}, bf16[2,128,512]{2,1,0:T(8,128)(2,1)S(1)}, u32[]{:S(2)}, u32[]{:S(2)}) collective-permute-start(bf16[2,128,512]{2,1,0:T(8,128)(2,1)S(1)} %add_convert_fusion.13.rest_0_), channel_id=1, source_target_pairs={{0,8},{4,12},{8,0},{12,4},{16,24},{20,28},{24,16},{28,20},{1,9},{5... | collective-permute-start | bytes 786440 | tf_op jit(solution)/shard_map/ppermute | solution.py:196
  62.5 13.6 %collective-permute-start.11 = (bf16[2,128,512]{2,1,0:T(8,128)(2,1)S(1)}, bf16[2,128,512]{2,1,0:T(8,128)(2,1)S(1)}, u32[]{:S(2)}, u32[]{:S(2)}) collective-permute-start(bf16[2,128,512]{2,1,0:T(8,128)(2,1)S(1)} %add_convert_fusion.12.rest_0_), channel_id=1, source_target_pairs={{0,8},{4,12},{8,0},{12,4},{16,24},{20,28},{24,16},{28,20},{1,9},{5... | collective-permute-start | bytes 786440 | tf_op jit(solution)/shard_map/ppermute | solution.py:196
  73.4 12.6 %collective-permute-start.9 = (bf16[2,256,1024]{2,1,0:T(8,128)(2,1)S(1)}, bf16[2,256,1024]{2,1,0:T(8,128)(2,1)S(1)}, u32[]{:S(2)}, u32[]{:S(2)}) collective-permute-start(bf16[2,256,1024]{2,1,0:T(8,128)(2,1)S(1)} %get-tuple-element.62), channel_id=1, source_target_pairs={{0,4},{4,0},{8,12},{12,8},{16,20},{20,16},{24,28},{28,24},{1,5},{5... | collective-permute-start | bytes 3145736 | tf_op jit(solution)/shard_map/ppermute | solution.py:196
  73.6 14.4 %collective-permute-start.8 = (bf16[2,64,512]{2,1,0:T(8,128)(2,1)S(1)}, bf16[2,64,512]{2,1,0:T(8,128)(2,1)S(1)}, u32[]{:S(2)}, u32[]{:S(2)}) collective-permute-start(bf16[2,64,512]{2,1,0:T(8,128)(2,1)S(1)} %add_convert_fusion.17.rest_1_), channel_id=1, source_target_pairs={{0,16},{4,20},{8,24},{12,28},{16,0},{20,4},{24,8},{28,12},{1,17},{... | collective-permute-start | bytes 393224 | tf_op jit(solution)/shard_map/ppermute | solution.py:196
  76.2 36.4 %collective-permute-start.12 = (bf16[2,64,512]{2,1,0:T(8,128)(2,1)S(1)}, bf16[2,64,512]{2,1,0:T(8,128)(2,1)S(1)}, u32[]{:S(2)}, u32[]{:S(2)}) collective-permute-start(bf16[2,64,512]{2,1,0:T(8,128)(2,1)S(1)} %add_convert_fusion.16.rest_1_), channel_id=1, source_target_pairs={{0,16},{4,20},{8,24},{12,28},{16,0},{20,4},{24,8},{28,12},{1,17},{... | collective-permute-start | bytes 393224 | tf_op jit(solution)/shard_map/ppermute | solution.py:196
  85.9 11.5 %collective-permute-start.13 = (bf16[2,256,1024]{2,1,0:T(8,128)(2,1)S(1)}, bf16[2,256,1024]{2,1,0:T(8,128)(2,1)S(1)}, u32[]{:S(2)}, u32[]{:S(2)}) collective-permute-start(bf16[2,256,1024]{2,1,0:T(8,128)(2,1)S(1)} %get-tuple-element.70), channel_id=1, source_target_pairs={{0,4},{4,0},{8,12},{12,8},{16,20},{20,16},{24,28},{28,24},{1,5},{5... | collective-permute-start | bytes 3145736 | tf_op jit(solution)/shard_map/ppermute | solution.py:196
  86.2 14.4 %collective-permute-start.14 = (bf16[2,128,1024]{2,1,0:T(8,128)(2,1)S(1)}, bf16[2,128,1024]{2,1,0:T(8,128)(2,1)S(1)}, u32[]{:S(2)}, u32[]{:S(2)}) collective-permute-start(bf16[2,128,1024]{2,1,0:T(8,128)(2,1)S(1)} %add_convert_fusion.4.rest_0_), channel_id=1, source_target_pairs={{0,8},{4,12},{8,0},{12,4},{16,24},{20,28},{24,16},{28,20},{1,9},{5... | collective-permute-start | bytes 1572872 | tf_op jit(solution)/shard_map/ppermute | solution.py:196
  97.0 20.8 %collective-permute-start.16 = (bf16[2,256,1024]{2,1,0:T(8,128)(2,1)S(1)}, bf16[2,256,1024]{2,1,0:T(8,128)(2,1)S(1)}, u32[]{:S(2)}, u32[]{:S(2)}) collective-permute-start(bf16[2,256,1024]{2,1,0:T(8,128)(2,1)S(1)} %get-tuple-element.76), channel_id=1, source_target_pairs={{0,4},{4,0},{8,12},{12,8},{16,20},{20,16},{24,28},{28,24},{1,5},{5... | collective-permute-start | bytes 3145736 | tf_op jit(solution)/shard_map/ppermute | solution.py:196
  97.6 19.8 %collective-permute-start.17 = (bf16[2,128,1024]{2,1,0:T(8,128)(2,1)S(1)}, bf16[2,128,1024]{2,1,0:T(8,128)(2,1)S(1)}, u32[]{:S(2)}, u32[]{:S(2)}) collective-permute-start(bf16[2,128,1024]{2,1,0:T(8,128)(2,1)S(1)} %add_convert_fusion.3.rest_0_), channel_id=1, source_target_pairs={{0,8},{4,12},{8,0},{12,4},{16,24},{20,28},{24,16},{28,20},{1,9},{5... | collective-permute-start | bytes 1572872 | tf_op jit(solution)/shard_map/ppermute | solution.py:196
  100.7 28.9 %collective-permute-start.15 = (bf16[2,64,1024]{2,1,0:T(8,128)(2,1)S(1)}, bf16[2,64,1024]{2,1,0:T(8,128)(2,1)S(1)}, u32[]{:S(2)}, u32[]{:S(2)}) collective-permute-start(bf16[2,64,1024]{2,1,0:T(8,128)(2,1)S(1)} %add_convert_fusion.11.rest_1_), channel_id=1, source_target_pairs={{0,16},{4,20},{8,24},{12,28},{16,0},{20,4},{24,8},{28,12},{1,17},{... | collective-permute-start | bytes 786440 | tf_op jit(solution)/shard_map/ppermute | solution.py:196
  112.6 25.1 %collective-permute-start.19 = (bf16[2,256,1024]{2,1,0:T(8,128)(2,1)S(1)}, bf16[2,256,1024]{2,1,0:T(8,128)(2,1)S(1)}, u32[]{:S(2)}, u32[]{:S(2)}) collective-permute-start(bf16[2,256,1024]{2,1,0:T(8,128)(2,1)S(1)} %get-tuple-element.82), channel_id=1, source_target_pairs={{0,4},{4,0},{8,12},{12,8},{16,20},{20,16},{24,28},{28,24},{1,5},{5... | collective-permute-start | bytes 3145736 | tf_op jit(solution)/shard_map/ppermute | solution.py:196
  117.5 27.8 %collective-permute-start.18 = (bf16[2,64,1024]{2,1,0:T(8,128)(2,1)S(1)}, bf16[2,64,1024]{2,1,0:T(8,128)(2,1)S(1)}, u32[]{:S(2)}, u32[]{:S(2)}) collective-permute-start(bf16[2,64,1024]{2,1,0:T(8,128)(2,1)S(1)} %add_convert_fusion.10.rest_1_), channel_id=1, source_target_pairs={{0,16},{4,20},{8,24},{12,28},{16,0},{20,4},{24,8},{28,12},{1,17},{... | collective-permute-start | bytes 786440 | tf_op jit(solution)/shard_map/ppermute | solution.py:196
  118.0 19.5 %collective-permute-start.20 = (bf16[2,128,1024]{2,1,0:T(8,128)(2,1)S(1)}, bf16[2,128,1024]{2,1,0:T(8,128)(2,1)S(1)}, u32[]{:S(2)}, u32[]{:S(2)}) collective-permute-start(bf16[2,128,1024]{2,1,0:T(8,128)(2,1)S(1)} %add_convert_fusion.2.rest_0_), channel_id=1, source_target_pairs={{0,8},{4,12},{8,0},{12,4},{16,24},{20,28},{24,16},{28,20},{1,9},{5... | collective-permute-start | bytes 1572872 | tf_op jit(solution)/shard_map/ppermute | solution.py:196
  129.5 29.7 %collective-permute-start.22 = (bf16[2,256,1024]{2,1,0:T(8,128)(2,1)S(1)}, bf16[2,256,1024]{2,1,0:T(8,128)(2,1)S(1)}, u32[]{:S(2)}, u32[]{:S(2)}) collective-permute-start(bf16[2,256,1024]{2,1,0:T(8,128)(2,1)S(1)} %get-tuple-element.88), channel_id=1, source_target_pairs={{0,4},{4,0},{8,12},{12,8},{16,20},{20,16},{24,28},{28,24},{1,5},{5... | collective-permute-start | bytes 3145736 | tf_op jit(solution)/shard_map/ppermute | solution.py:196
  137.5 27.1 %collective-permute-start.21 = (bf16[2,64,1024]{2,1,0:T(8,128)(2,1)S(1)}, bf16[2,64,1024]{2,1,0:T(8,128)(2,1)S(1)}, u32[]{:S(2)}, u32[]{:S(2)}) collective-permute-start(bf16[2,64,1024]{2,1,0:T(8,128)(2,1)S(1)} %add_convert_fusion.9.rest_1_), channel_id=1, source_target_pairs={{0,16},{4,20},{8,24},{12,28},{16,0},{20,4},{24,8},{28,12},{1,17},{... | collective-permute-start | bytes 786440 | tf_op jit(solution)/shard_map/ppermute | solution.py:196
  137.9 18.3 %collective-permute-start.23 = (bf16[2,128,1024]{2,1,0:T(8,128)(2,1)S(1)}, bf16[2,128,1024]{2,1,0:T(8,128)(2,1)S(1)}, u32[]{:S(2)}, u32[]{:S(2)}) collective-permute-start(bf16[2,128,1024]{2,1,0:T(8,128)(2,1)S(1)} %add_convert_fusion.1.rest_0_), channel_id=1, source_target_pairs={{0,8},{4,12},{8,0},{12,4},{16,24},{20,28},{24,16},{28,20},{1,9},{5... | collective-permute-start | bytes 1572872 | tf_op jit(solution)/shard_map/ppermute | solution.py:196
  145.3 11.3 %collective-permute-start.25 = (bf16[2,256,512]{2,1,0:T(8,128)(2,1)S(1)}, bf16[2,256,512]{2,1,0:T(8,128)(2,1)S(1)}, u32[]{:S(2)}, u32[]{:S(2)}) collective-permute-start(bf16[2,256,512]{2,1,0:T(8,128)(2,1)S(1)} %get-tuple-element.94), channel_id=1, source_target_pairs={{0,4},{4,0},{8,12},{12,8},{16,20},{20,16},{24,28},{28,24},{1,5},{5... | collective-permute-start | bytes 1572872 | tf_op jit(solution)/shard_map/ppermute | solution.py:196
  156.3 26.8 %collective-permute-start.24 = (bf16[2,64,1024]{2,1,0:T(8,128)(2,1)S(1)}, bf16[2,64,1024]{2,1,0:T(8,128)(2,1)S(1)}, u32[]{:S(2)}, u32[]{:S(2)}) collective-permute-start(bf16[2,64,1024]{2,1,0:T(8,128)(2,1)S(1)} %add_convert_fusion.8.rest_1_), channel_id=1, source_target_pairs={{0,16},{4,20},{8,24},{12,28},{16,0},{20,4},{24,8},{28,12},{1,17},{... | collective-permute-start | bytes 786440 | tf_op jit(solution)/shard_map/ppermute | solution.py:196
  156.7 16.3 %collective-permute-start.29 = (bf16[2,128,512]{2,1,0:T(8,128)(2,1)S(1)}, bf16[2,128,512]{2,1,0:T(8,128)(2,1)S(1)}, u32[]{:S(2)}, u32[]{:S(2)}) collective-permute-start(bf16[2,128,512]{2,1,0:T(8,128)(2,1)S(1)} %add_convert_fusion.7), channel_id=1, source_target_pairs={{0,8},{4,12},{8,0},{12,4},{16,24},{20,28},{24,16},{28,20},{1,9},{5... | collective-permute-start | bytes 786440 | tf_op jit(solution)/shard_map/ppermute | solution.py:196
  159.4 23.5 %collective-permute-start.26 = (bf16[2,128,1024]{2,1,0:T(8,128)(2,1)S(1)}, bf16[2,128,1024]{2,1,0:T(8,128)(2,1)S(1)}, u32[]{:S(2)}, u32[]{:S(2)}) collective-permute-start(bf16[2,128,1024]{2,1,0:T(8,128)(2,1)S(1)} %add_convert_fusion.rest_0_), channel_id=1, source_target_pairs={{0,8},{4,12},{8,0},{12,4},{16,24},{20,28},{24,16},{28,20},{1,9},{5... | collective-permute-start | bytes 1572872 | tf_op jit(solution)/shard_map/ppermute | solution.py:196
  164.7 18.4 %collective-permute-start.28 = (bf16[2,256,512]{2,1,0:T(8,128)(2,1)S(1)}, bf16[2,256,512]{2,1,0:T(8,128)(2,1)S(1)}, u32[]{:S(2)}, u32[]{:S(2)}) collective-permute-start(bf16[2,256,512]{2,1,0:T(8,128)(2,1)S(1)} %get-tuple-element.100), channel_id=1, source_target_pairs={{0,4},{4,0},{8,12},{12,8},{16,20},{20,16},{24,28},{28,24},{1,5},{5... | collective-permute-start | bytes 1572872 | tf_op jit(solution)/shard_map/ppermute | solution.py:196
  173.0 22.0 %collective-permute-start.30 = (bf16[2,64,512]{2,1,0:T(8,128)(2,1)S(1)}, bf16[2,64,512]{2,1,0:T(8,128)(2,1)S(1)}, u32[]{:S(2)}, u32[]{:S(2)}) collective-permute-start(bf16[2,64,512]{2,1,0:T(8,128)(2,1)S(1)} %add_convert_fusion.15), channel_id=1, source_target_pairs={{0,16},{4,20},{8,24},{12,28},{16,0},{20,4},{24,8},{28,12},{1,17},{... | collective-permute-start | bytes 393224 | tf_op jit(solution)/shard_map/ppermute | solution.py:196
  183.0 11.4 %collective-permute-start.27 = (bf16[2,64,1024]{2,1,0:T(8,128)(2,1)S(1)}, bf16[2,64,1024]{2,1,0:T(8,128)(2,1)S(1)}, u32[]{:S(2)}, u32[]{:S(2)}) collective-permute-start(bf16[2,64,1024]{2,1,0:T(8,128)(2,1)S(1)} %add_convert_fusion.6), channel_id=1, source_target_pairs={{0,16},{4,20},{8,24},{12,28},{16,0},{20,4},{24,8},{28,12},{1,17},{... | collective-permute-start | bytes 786440 | tf_op jit(solution)/shard_map/ppermute | solution.py:196
  183.2 11.5 %collective-permute-start.31 = (bf16[2,128,512]{2,1,0:T(8,128)(2,1)S(1)}, bf16[2,128,512]{2,1,0:T(8,128)(2,1)S(1)}, u32[]{:S(2)}, u32[]{:S(2)}) collective-permute-start(bf16[2,128,512]{2,1,0:T(8,128)(2,1)S(1)} %add_convert_fusion.5), channel_id=1, source_target_pairs={{0,8},{4,12},{8,0},{12,4},{16,24},{20,28},{24,16},{28,20},{1,9},{5... | collective-permute-start | bytes 786440 | tf_op jit(solution)/shard_map/ppermute | solution.py:196
  194.7 8.2 %copy-start.1 = (bf16[64,8192]{1,0:T(8,128)(2,1)S(1)}, bf16[64,8192]{1,0:T(8,128)(2,1)}, u32[]{:S(2)}) copy-start(bf16[64,8192]{1,0:T(8,128)(2,1)} %param.7) | copy-start | bytes 3145732
  194.8 7.4 %collective-permute-start.32 = (bf16[2,64,512]{2,1,0:T(8,128)(2,1)S(1)}, bf16[2,64,512]{2,1,0:T(8,128)(2,1)S(1)}, u32[]{:S(2)}, u32[]{:S(2)}) collective-permute-start(bf16[2,64,512]{2,1,0:T(8,128)(2,1)S(1)} %add_convert_fusion.14), channel_id=1, source_target_pairs={{0,16},{4,20},{8,24},{12,28},{16,0},{20,4},{24,8},{28,12},{1,17},{... | collective-permute-start | bytes 393224 | tf_op jit(solution)/shard_map/ppermute | solution.py:196
  195.5 6.8 %copy-start.2 = (bf16[64,7168]{1,0:T(8,128)(2,1)}, bf16[64,7168]{1,0:T(8,128)(2,1)S(1)}, u32[]{:S(2)}) copy-start(bf16[64,7168]{1,0:T(8,128)(2,1)S(1)} %constant_dynamic-update-slice_fusion.33) | copy-start | bytes 2752516

commit v3 on v2

--- a/solution.py
+++ b/solution.py
@@ -8,10 +8,11 @@
 from jax.sharding import PartitionSpec as P
 
 UNITS = 28
-WIDTHS = (2, 2, 4, 4, 4, 4, 4, 2, 2)
-BLOCK = 256
+WIDTHS = (2, 4, 5, 5, 5, 4, 3)
+AHEAD = 2
+BATCHES = ()
 HOLD = 1
-AHEAD = 2
+CHAIN = 1
 LANE = 128
 
 
@@ -70,7 +71,7 @@
             jax.ShapeDtypeStruct((2, rows // 2, width), jnp.float32),
             jax.ShapeDtypeStruct((2, rows // 2, width), jnp.bfloat16),
         ],
-        compiler_params=pltpu.CompilerParams(vmem_limit_bytes=32 * 2**20),
+        compiler_params=pltpu.CompilerParams(vmem_limit_bytes=42 * 2**20),
         cost_estimate=pl.CostEstimate(
             flops=4 * rows * (depth + inner) * width,
             bytes_accessed=2 * (depth + inner) * width + 6 * rows * width,
@@ -143,7 +144,8 @@
     def over_lanes(array, mask):
         return lax.ppermute(array, "tensor", [(i, i ^ mask) for i in range(lanes)])
 
-    spread = jnp.stack([spread] + [over_lanes(spread, k) for k in range(1, lanes)])
+    spread = jnp.concatenate([spread] + [over_lanes(spread, k) for k in range(1, lanes)], 0)
+    spread = spread.reshape(groups * rows, part)
 
     which = arrived[:, depth_part].astype(i32)
     place_row = arrived[:, depth_part + 1].astype(i32)
@@ -159,8 +161,23 @@
     for k in range(1, lanes):
         total_down = total_down + over_lanes(part_down, k)
     down = total_down.astype(bf16)
-    whole_row = (jnp.arange(buffer, dtype=i32) // capacity) * rows + place_row
-    to_row = (jnp.arange(groups * rows, dtype=i32)[:, None] == whole_row[None, :]).astype(bf16)
+    order = jnp.array([reversed_bits(i, bits) for i in range(groups)], i32)
+    pack = 3 * rows // 4
+    before = jnp.cumsum(counts) - counts
+
+    def position(of_group, of_row):
+        near = of_group[:, None] == jnp.arange(groups, dtype=i32)[None, :]
+        start = jnp.sum(jnp.where(near, before[None, :], 0), axis=1)
+        limit = jnp.sum(jnp.where(near, counts[None, :], 0), axis=1)
+        return jnp.where(of_row < limit, start + of_row, -groups * rows)
+
+    number = jnp.arange(groups * rows, dtype=i32)
+    from_lane = lane ^ (number // (groups * share))
+    came_at = position(number // share % groups, from_lane * share + number % share)
+    packed = ((group ^ order)[:, None] * pack + jnp.arange(pack, dtype=i32)[None, :]).reshape(-1)
+    pick = (packed[:, None] == came_at[None, :]).astype(bf16)
+    slot_at = position(jnp.arange(buffer, dtype=i32) // capacity, place_row)
+    to_row = (packed[:, None] == slot_at[None, :]).astype(bf16)
     terms = []
     for t in range(2):
         spacer = 2 * jnp.arange(rank, dtype=i32)[:, None] + t == jnp.arange(2 * rank)[None, :]
@@ -170,22 +187,25 @@
         apart = jnp.where(mine[:, :, None], apart[:, None, :], jnp.zeros((), bf16))
         apart = apart.reshape(buffer, holder_adapters * 2 * rank)
         terms.append(jnp.dot(to_row, apart, preferred_element_type=f32).astype(bf16))
-    terms = jnp.stack(terms).reshape(2, groups, rows, -1)
-
-    order = [reversed_bits(i, bits) for i in range(groups)]
-    x = jnp.concatenate(
-        [
-            lax.dynamic_slice(spread, (lane ^ k, group ^ b, 0, 0), (1, 1, share, part))[0, 0]
-            for b in order
-            for k in range(lanes)
-        ],
-        0,
-    )
-    x = interleave(x)
-    d = jnp.concatenate([lax.dynamic_index_in_dim(terms, group ^ b, 1, False) for b in order], 1)
+    d = jnp.stack(terms)
+    x = interleave(jnp.dot(pick, spread, preferred_element_type=f32).astype(bf16))
     adapter_up = adapter_up_weight.reshape(holder_adapters * rank, 2, extent)
 
-    live = row_index < counts[group]
+    chips = groups // 2
+    total = groups * pack
+    reach = 0
+    for chip in range(chips):
+        low = max(0, total - 2 * rows * (chips - chip)) // (2 * pack)
+        high = (min(2 * rows * (chip + 1), total) - 1) // (2 * pack)
+        reach = max(reach, chip - low, high - chip)
+    shifts = [0] + [k * sign for k in range(1, reach + 1) for sign in (1, -1)]
+    both = jnp.concatenate([jnp.full((rows,), group), jnp.full((rows,), group ^ 1)])
+    wanted = position(both, jnp.concatenate([row_index, row_index]))
+    held = jnp.concatenate(
+        [(group + 2 * k) * pack + jnp.arange(pack, dtype=i32) for k in shifts]
+    )
+    give = (wanted[:, None] == held[None, :]).astype(bf16)
+
     unit = extent // UNITS
     ends = [unit * sum(WIDTHS[: i + 1]) for i in range(len(WIDTHS))]
     count = len(WIDTHS)
@@ -197,24 +217,44 @@
 
     def begin(chunk, after):
         own, other = partial_sums(
-            x, d, base_gate_up_weight, adapter_up, ends[chunk], unit * WIDTHS[chunk], BLOCK, after
+            x, d, base_gate_up_weight, adapter_up, ends[chunk], unit * WIDTHS[chunk], unit, after
         )
         stages[chunk] = [own, send(other, 1)]
 
     def advance(chunk, stage):
-        size = groups * rows >> (stage + 1)
+        size = total >> (stage + 1)
+        if CHAIN and stage in last:
+            stages[chunk], _ = lax.optimization_barrier((stages[chunk], last[stage]))
         parts = [a[:, size : 2 * size].astype(f32) for a in stages[chunk]]
         message = functools.reduce(jnp.add, parts).astype(bf16)
         stages[chunk].append(send(message, 1 << stage))
+        if stage > 1:
+            last[stage] = message
         return message
 
     def finish(chunk, after):
         if HOLD:
             stages[chunk], after = lax.optimization_barrier((stages[chunk], after))
-        gate, up = functools.reduce(jnp.add, [a[:, :rows].astype(f32) for a in stages[chunk]])
-        hidden = jnp.where(live[:, None], jax.nn.silu(gate) * up, 0.0)
-        pieces.append(hidden.astype(bf16))
-
+        gate, up = functools.reduce(jnp.add, [a[:, :pack].astype(f32) for a in stages[chunk]])
+        pieces.append((jax.nn.silu(gate) * up).astype(bf16))
+
+    def deliver():
+        mine = jnp.concatenate(pieces, axis=1)
+        pieces.clear()
+        near = [mine] + [
+            lax.ppermute(
+                mine,
+                "dp",
+                [(i + 2 * k, i) for i in range(groups) if 0 <= i + 2 * k < groups],
+            )
+            for k in shifts[1:]
+        ]
+        chosen = jnp.dot(give, jnp.concatenate(near, 0), preferred_element_type=f32).astype(bf16)
+        outputs.append(chosen[:rows] + send(chosen[rows:], 1))
+        return chosen
+
+    outputs = []
+    last = {}
     for chunk in range(min(AHEAD, count)):
         begin(chunk, [])
     for slot in range(count + bits - 1):
@@ -223,11 +263,15 @@
             for stage in range(1, bits)
             if 0 <= slot - stage + 1 < count
         ]
+        done = slot - bits + 1
+        if done - 1 in BATCHES:
+            after.append(deliver())
         if slot + AHEAD < count:
             begin(slot + AHEAD, after)
-        if 0 <= slot - bits + 1 < count:
-            finish(slot - bits + 1, after)
-    return jnp.concatenate(pieces, axis=1)
+        if 0 <= done < count:
+            finish(done, after)
+    deliver()
+    return jnp.concatenate(outputs, axis=1)
 
 
 def solution(mesh):

time: 203 us -> 191 us (0.941)
  Pallas kernels: 66.9 us -> 51.4 us
  waiting for transfers between devices: 84.7 us -> 91.7 us
  starting transfers between devices: 33.7 us -> 29 us
    ppermute x0 -> x2, waiting for transfers between devices: none -> 15.7 us  [deliver(): lax.ppermute(mine, 'dp', [(i + 2 * k, i) for i in range(groups) if 0 <= i...]
    pallas_call x9 -> x7, Pallas kernels: 65.7 us -> 50.4 us  [partial_sums(): pl.pallas_call(partial_kernel, grid=(width // block,), in_specs=[pl.Block...]
    ppermute x27 -> x22, waiting for transfers between devices: 61.1 us -> 52.9 us  [send(): return lax.ppermute(array, 'dp', [(i, i ^ mask) for i in range(groups)])]
    ppermute x27 -> x22, starting transfers between devices: 20.3 us -> 12.9 us  [send(): return lax.ppermute(array, 'dp', [(i, i ^ mask) for i in range(groups)])]
    ppermute x0 -> x2, starting transfers between devices: none -> 2.63 us  [deliver(): lax.ppermute(mine, 'dp', [(i + 2 * k, i) for i in range(groups) if 0 <= i...]
  transfers between devices with their start and end apart: 34 -> 31, of which waited for: 15 -> 15; matrix products, arithmetic and copies ran while one was open for 5% -> 6% of each run, Pallas kernels for 30% -> 24%
where the time goes in v3:
time: 191 us
  waiting for transfers between devices  91.7 us (48%)
  Pallas kernels  51.4 us (27%)
  starting transfers between devices  29 us (15%)
  other arithmetic  9.6 us (5%)
  matrix products  5.74 us (3%)
  local copies, waits for them, and re-layouts  2.56 us (1%)
    ppermute x22, waiting for transfers between devices, send(): return lax.ppermute(array, 'dp', [(i, i ^ mask) for i in range(groups)])  52.9 us
    pallas_call x7, Pallas kernels, partial_sums(): pl.pallas_call(partial_kernel, grid=(width // block,), in_specs=[pl.Block...  50.4 us
    all_to_all x1, waiting for transfers between devices, body(): came = lax.all_to_all(sent, 'dp', split_axis=0, concat_axis=0, tiled=True)  17.5 us
    ppermute x2, waiting for transfers between devices, deliver(): lax.ppermute(mine, 'dp', [(i + 2 * k, i) for i in range(groups) if 0 <= i...  15.7 us
    ppermute x22, starting transfers between devices, send(): return lax.ppermute(array, 'dp', [(i, i ^ mask) for i in range(groups)])  12.9 us
    ppermute x6, starting transfers between devices, over_lanes(): return lax.ppermute(array, 'tensor', [(i, i ^ mask) for i in range(lanes)])  7.11 us
    all_to_all x1, starting transfers between devices, body(): came = lax.all_to_all(sent, 'dp', split_axis=0, concat_axis=0, tiled=True)  6.33 us
    ppermute x6, waiting for transfers between devices, over_lanes(): return lax.ppermute(array, 'tensor', [(i, i ^ mask) for i in range(lanes)])  5.64 us
  transfers between devices with their start and end apart: 31, of which 15 were waited for; matrix products, arithmetic and copies ran while one was open for 6% of the time, Pallas kernels for 24%

profile of v3, /device:TPU:0, one launch (start us, length us, event | category | flops | bytes accessed | tf_op | source)
XLA Modules:
  0.0 190.7 jit_solution(3823464134921631278)
XLA Ops:
  0.0 0.9 select_reduce_fusion.3
  2.4 0.9 pad_maximum_fusion.2
  3.3 6.3 %all-to-all-start = ((bf16[8,33,1024]{2,1,0:T(8,128)(2,1)}), bf16[8,33,1024]{2,1,0:T(8,128)(2,1)S(1)}, u32[]{:S(2)}, u32[]{:S(2)}) async-start(bf16[8,33,1024]{2,1,0:T(8,128)(2,1)} %pad_maximum_fusion.2), calls=%async_computation | async-start | bytes 1310720 | tf_op jit(solution)/shard_map/all_to_all | solution.py:140
  10.3 17.5 %all-to-all-done = bf16[8,33,1024]{2,1,0:T(8,128)(2,1)S(1)} async-done(((bf16[8,33,1024]{2,1,0:T(8,128)(2,1)}), bf16[8,33,1024]{2,1,0:T(8,128)(2,1)S(1)}, u32[]{:S(2)}, u32[]{:S(2)}) %all-to-all-start) | async-done | bytes 540704 | tf_op jit(solution)/shard_map/all_to_all | solution.py:140
  27.8 2.5 %collective-permute-start.2 = (bf16[8,16,1024]{2,1,0:T(8,128)(2,1)S(1)}, bf16[8,16,1024]{2,1,0:T(8,128)(2,1)S(1)}, u32[]{:S(2)}, u32[]{:S(2)}) collective-permute-start(bf16[8,16,1024]{2,1,0:T(8,128)(2,1)S(1)} %slice.260), channel_id=1, source_target_pairs={{0,3},{1,2},{2,1},{3,0},{4,7},{5,6},{6,5},{7,4},{8,11},{9,10},{10,... | collective-permute-start | bytes 786440 | tf_op jit(solution)/shard_map/ppermute | solution.py:145
  31.4 3.0 %fusion.10 = f32[64,128]{1,0:T(8,128)S(1)} fusion(bf16[8,2048,128]{2,1,0:T(8,128)(2,1)} %param.10, pred[64,8]{0,1:T(8,128)(4,1)S(1)} %iota_compare_fusion.10, bf16[64,2048]{1,0:T(8,128)(2,1)S(1)} %slice.264), kind=kOutput, calls=%fused_computation.16 | convolution fusion | flops 269484032 | bytes 4489728 | tf_op jit(solution)/shard_map/dot_general | solution.py:155
  34.4 1.6 collective-permute-start.5
  36.5 1.5 collective-permute-start.3
  38.1 1.3 collective-permute-done.5
  39.9 3.7 %collective-permute-done.4 = f32[64,128]{1,0:T(8,128)S(1)} collective-permute-done((f32[64,128]{1,0:T(8,128)S(1)}, f32[64,128]{1,0:T(8,128)S(1)}, u32[]{:S(2)}, u32[]{:S(2)}) %collective-permute-start.4) | collective-permute-done | bytes 32800 | tf_op jit(solution)/shard_map/ppermute | solution.py:145
  45.2 0.6 collective-permute-done
  46.0 0.6 convolution_convert_fusion.4.x_ref
  46.6 1.0 shard_map.82.x_ref
  47.5 4.3 %shard_map.83 = (f32[2,192,512]{2,1,0:T(8,128)S(1)}, bf16[2,192,512]{2,1,0:T(8,128)(2,1)S(1)}) custom-call(bf16[2,384,2048]{2,1,0:T(8,128)(2,1)S(1)} %shard_map.82.x_ref, bf16[2,384,1024]{2,1,0:T(8,128)(2,1)S(1)} %pad_maximum_fusion.d_ref, bf16[1024,2,7168]{2,1,0:T(2,128)(2,1)} %w_ref.13, bf16[512,2,7168]{2,1,0:T(2,128)(2,1)} %bitcast.123), custom_call_target="tpu_custom_call" | custom-call | flops 2415919104 | bytes 4325376 | tf_op jit(solution)/shard_map/pallas_call | solution.py:56
  51.9 7.2 %shard_map.85 = (f32[2,192,1024]{2,1,0:T(8,128)S(1)}, bf16[2,192,1024]{2,1,0:T(8,128)(2,1)S(1)}) custom-call(bf16[2,384,2048]{2,1,0:T(8,128)(2,1)S(1)} %shard_map.82.x_ref, bf16[2,384,1024]{2,1,0:T(8,128)(2,1)S(1)} %pad_maximum_fusion.d_ref, bf16[1024,2,7168]{2,1,0:T(2,128)(2,1)} %w_ref.13, bf16[512,2,7168]{2,1,0:T(2,128)(2,1)} %bitcast.124), custom_call_target="tpu_custom_call" | custom-call | flops 4831838208 | bytes 8650752 | tf_op jit(solution)/shard_map/pallas_call | solution.py:56
  59.1 0.5 collective-permute-start.10
  59.8 8.6 %shard_map.84 = (f32[2,192,1280]{2,1,0:T(8,128)S(1)}, bf16[2,192,1280]{2,1,0:T(8,128)(2,1)S(1)}) custom-call(bf16[2,384,2048]{2,1,0:T(8,128)(2,1)S(1)} %shard_map.82.x_ref, bf16[2,384,1024]{2,1,0:T(8,128)(2,1)S(1)} %pad_maximum_fusion.d_ref, bf16[1024,2,7168]{2,1,0:T(2,128)(2,1)} %w_ref.13, bf16[512,2,7168]{2,1,0:T(2,128)(2,1)} %bitcast.125, ...), custom_call_target="tpu_custom_call" | custom-call | flops 6039797760 | bytes 10813440 | tf_op jit(solution)/shard_map/pallas_call | solution.py:56
  68.6 2.0 %collective-permute-start.8 = (bf16[2,48,512]{2,1,0:T(8,128)(2,1)S(1)}, bf16[2,48,512]{2,1,0:T(8,128)(2,1)S(1)}, u32[]{:S(2)}, u32[]{:S(2)}) collective-permute-start(bf16[2,48,512]{2,1,0:T(8,128)(2,1)S(1)} %add_convert_fusion.13.rest_1_), channel_id=1, source_target_pairs={{0,16},{4,20},{8,24},{12,28},{16,0},{20,4},{24,8},{28,12},{1,17},{... | collective-permute-start | bytes 294920 | tf_op jit(solution)/shard_map/ppermute | solution.py:216
  70.8 8.6 %shard_map.86 = (f32[2,192,1280]{2,1,0:T(8,128)S(1)}, bf16[2,192,1280]{2,1,0:T(8,128)(2,1)S(1)}) custom-call(bf16[2,384,2048]{2,1,0:T(8,128)(2,1)S(1)} %shard_map.82.x_ref, bf16[2,384,1024]{2,1,0:T(8,128)(2,1)S(1)} %pad_maximum_fusion.d_ref, bf16[1024,2,7168]{2,1,0:T(2,128)(2,1)} %w_ref.13, bf16[512,2,7168]{2,1,0:T(2,128)(2,1)} %bitcast.126, ...), custom_call_target="tpu_custom_call" | custom-call | flops 6039797760 | bytes 10813440 | tf_op jit(solution)/shard_map/pallas_call | solution.py:56
  79.8 3.4 %collective-permute-done.11 = bf16[2,96,1024]{2,1,0:T(8,128)(2,1)S(1)} collective-permute-done((bf16[2,96,1024]{2,1,0:T(8,128)(2,1)S(1)}, bf16[2,96,1024]{2,1,0:T(8,128)(2,1)S(1)}, u32[]{:S(2)}, u32[]{:S(2)}) %collective-permute-start.11) | collective-permute-done | bytes 393248 | tf_op jit(solution)/shard_map/ppermute | solution.py:216
  83.2 2.1 %collective-permute-start.12 = (bf16[2,48,1024]{2,1,0:T(8,128)(2,1)S(1)}, bf16[2,48,1024]{2,1,0:T(8,128)(2,1)S(1)}, u32[]{:S(2)}, u32[]{:S(2)}) collective-permute-start(bf16[2,48,1024]{2,1,0:T(8,128)(2,1)S(1)} %add_convert_fusion.10.rest_1_), channel_id=1, source_target_pairs={{0,16},{4,20},{8,24},{12,28},{16,0},{20,4},{24,8},{28,12},{1,17},{... | collective-permute-start | bytes 589832 | tf_op jit(solution)/shard_map/ppermute | solution.py:216
  85.4 0.7 collective-permute-start.14
  86.1 8.6 %shard_map.87 = (f32[2,192,1280]{2,1,0:T(8,128)S(1)}, bf16[2,192,1280]{2,1,0:T(8,128)(2,1)S(1)}) custom-call(bf16[2,384,2048]{2,1,0:T(8,128)(2,1)S(1)} %shard_map.82.x_ref, bf16[2,384,1024]{2,1,0:T(8,128)(2,1)S(1)} %pad_maximum_fusion.d_ref, bf16[1024,2,7168]{2,1,0:T(2,128)(2,1)} %w_ref.13, bf16[512,2,7168]{2,1,0:T(2,128)(2,1)} %bitcast.127, ...), custom_call_target="tpu_custom_call" | custom-call | flops 6039797760 | bytes 10813440 | tf_op jit(solution)/shard_map/pallas_call | solution.py:56
  94.9 0.7 fusion.54
  95.6 1.5 collective-permute-start.17
  97.1 6.3 %collective-permute-done.14 = bf16[2,96,1280]{2,1,0:T(8,128)(2,1)S(1)} collective-permute-done((bf16[2,96,1280]{2,1,0:T(8,128)(2,1)S(1)}, bf16[2,96,1280]{2,1,0:T(8,128)(2,1)S(1)}, u32[]{:S(2)}, u32[]{:S(2)}) %collective-permute-start.14) | collective-permute-done | bytes 491552 | tf_op jit(solution)/shard_map/ppermute | solution.py:216
  103.5 0.7 copy-done.4
  104.5 7.2 %shard_map.88 = (f32[2,192,1024]{2,1,0:T(8,128)S(1)}, bf16[2,192,1024]{2,1,0:T(8,128)(2,1)S(1)}) custom-call(bf16[2,384,2048]{2,1,0:T(8,128)(2,1)S(1)} %shard_map.82.x_ref, bf16[2,384,1024]{2,1,0:T(8,128)(2,1)S(1)} %pad_maximum_fusion.d_ref, bf16[1024,2,7168]{2,1,0:T(2,128)(2,1)} %w_ref.13, bf16[512,2,7168]{2,1,0:T(2,128)(2,1)} %bitcast.128, ...), custom_call_target="tpu_custom_call" | custom-call | flops 4831838208 | bytes 8650752 | tf_op jit(solution)/shard_map/pallas_call | solution.py:56
  111.9 0.7 fusion.43
  112.6 5.0 %collective-permute-done.17 = bf16[2,96,1280]{2,1,0:T(8,128)(2,1)S(1)} collective-permute-done((bf16[2,96,1280]{2,1,0:T(8,128)(2,1)S(1)}, bf16[2,96,1280]{2,1,0:T(8,128)(2,1)S(1)}, u32[]{:S(2)}, u32[]{:S(2)}) %collective-permute-start.17) | collective-permute-done | bytes 491552 | tf_op jit(solution)/shard_map/ppermute | solution.py:216
  118.4 1.3 collective-permute-start.20
  119.7 5.8 %shard_map.89 = (f32[2,192,768]{2,1,0:T(8,128)S(1)}, bf16[2,192,768]{2,1,0:T(8,128)(2,1)S(1)}) custom-call(bf16[2,384,2048]{2,1,0:T(8,128)(2,1)S(1)} %shard_map.82.x_ref, bf16[2,384,1024]{2,1,0:T(8,128)(2,1)S(1)} %pad_maximum_fusion.d_ref, bf16[1024,2,7168]{2,1,0:T(2,128)(2,1)} %w_ref.13, bf16[512,2,7168]{2,1,0:T(2,128)(2,1)} %bitcast.129, ...), custom_call_target="tpu_custom_call" | custom-call | flops 3623878656 | bytes 6488064 | tf_op jit(solution)/shard_map/pallas_call | solution.py:56
  125.6 1.0 convert_add_fusion.2
  126.7 0.7 fusion.40
  127.5 0.8 collective-permute-start.23
  128.3 12.0 %collective-permute-done.20 = bf16[2,96,1280]{2,1,0:T(8,128)(2,1)S(1)} collective-permute-done((bf16[2,96,1280]{2,1,0:T(8,128)(2,1)S(1)}, bf16[2,96,1280]{2,1,0:T(8,128)(2,1)S(1)}, u32[]{:S(2)}, u32[]{:S(2)}) %collective-permute-start.20) | collective-permute-done | bytes 491552 | tf_op jit(solution)/shard_map/ppermute | solution.py:216
  140.8 2.5 %collective-permute-start.25 = (bf16[2,96,768]{2,1,0:T(8,128)(2,1)S(1)}, bf16[2,96,768]{2,1,0:T(8,128)(2,1)S(1)}, u32[]{:S(2)}, u32[]{:S(2)}) collective-permute-start(bf16[2,96,768]{2,1,0:T(8,128)(2,1)S(1)} %add_convert_fusion.5), channel_id=1, source_target_pairs={{0,8},{4,12},{8,0},{12,4},{16,24},{20,28},{24,16},{28,20},{1,9},{5... | collective-permute-start | bytes 884744 | tf_op jit(solution)/shard_map/ppermute | solution.py:216
  143.3 10.2 %collective-permute-done.23 = bf16[2,96,1024]{2,1,0:T(8,128)(2,1)S(1)} collective-permute-done((bf16[2,96,1024]{2,1,0:T(8,128)(2,1)S(1)}, bf16[2,96,1024]{2,1,0:T(8,128)(2,1)S(1)}, u32[]{:S(2)}, u32[]{:S(2)}) %collective-permute-start.23) | collective-permute-done | bytes 393248 | tf_op jit(solution)/shard_map/ppermute | solution.py:216
  153.9 3.6 %collective-permute-done.25 = bf16[2,96,768]{2,1,0:T(8,128)(2,1)S(1)} collective-permute-done((bf16[2,96,768]{2,1,0:T(8,128)(2,1)S(1)}, bf16[2,96,768]{2,1,0:T(8,128)(2,1)S(1)}, u32[]{:S(2)}, u32[]{:S(2)}) %collective-permute-start.25) | collective-permute-done | bytes 294944 | tf_op jit(solution)/shard_map/ppermute | solution.py:216
  157.6 8.5 %collective-permute-done.24 = bf16[2,48,1024]{2,1,0:T(8,128)(2,1)S(1)} collective-permute-done((bf16[2,48,1024]{2,1,0:T(8,128)(2,1)S(1)}, bf16[2,48,1024]{2,1,0:T(8,128)(2,1)S(1)}, u32[]{:S(2)}, u32[]{:S(2)}) %collective-permute-start.24) | collective-permute-done | bytes 196640 | tf_op jit(solution)/shard_map/ppermute | solution.py:216
  166.2 1.4 collective-permute-done.26
  167.8 1.3 collective-permute-start.28
  169.1 1.3 collective-permute-start.27
  170.7 11.5 %collective-permute-done.28 = bf16[48,7168]{1,0:T(8,128)(2,1)S(1)} collective-permute-done((bf16[48,7168]{1,0:T(8,128)(2,1)S(1)}, bf16[48,7168]{1,0:T(8,128)(2,1)S(1)}, u32[]{:S(2)}, u32[]{:S(2)}) %collective-permute-start.28) | collective-permute-done | bytes 688160 | tf_op jit(solution)/shard_map/ppermute | solution.py:245
  182.3 4.2 %collective-permute-done.27 = bf16[48,7168]{1,0:T(8,128)(2,1)S(1)} collective-permute-done((bf16[48,7168]{1,0:T(8,128)(2,1)S(1)}, bf16[48,7168]{1,0:T(8,128)(2,1)S(1)}, u32[]{:S(2)}, u32[]{:S(2)}) %collective-permute-start.27) | collective-permute-done | bytes 688160 | tf_op jit(solution)/shard_map/ppermute | solution.py:245
  186.4 0.7 convolution_convert_fusion
  187.2 2.5 %collective-permute-done.29 = bf16[64,7168]{1,0:T(8,128)(2,1)S(1)} collective-permute-done((bf16[64,7168]{1,0:T(8,128)(2,1)S(1)}, bf16[64,7168]{1,0:T(8,128)(2,1)S(1)}, u32[]{:S(2)}, u32[]{:S(2)}) %collective-permute-start.29) | collective-permute-done | bytes 917536 | tf_op jit(solution)/shard_map/ppermute | solution.py:216
  189.7 1.0 slice_add_fusion
  (123 shorter events, 9.9 us)
Async XLA Ops:
  0.0 1.3 copy-start
  2.0 7.6 %copy-start.8 = (s32[8]{0:T(128)S(1)}, s32[8]{0:T(128)}, u32[]{:S(2)}) copy-start(s32[8]{0:T(128)} %constant.139.clone) | copy-start | bytes 100
  2.1 7.7 %copy-start.6 = (s32[8]{0:T(128)S(1)}, s32[8]{0:T(128)}, u32[]{:S(2)}) copy-start(s32[8]{0:T(128)} %param.14) | copy-start | bytes 100
  3.3 24.5 %all-to-all-start = ((bf16[8,33,1024]{2,1,0:T(8,128)(2,1)}), bf16[8,33,1024]{2,1,0:T(8,128)(2,1)S(1)}, u32[]{:S(2)}, u32[]{:S(2)}) async-start(bf16[8,33,1024]{2,1,0:T(8,128)(2,1)} %pad_maximum_fusion.2), calls=%async_computation | async-start | bytes 1310720 | tf_op jit(solution)/shard_map/all_to_all | solution.py:140
  27.8 17.4 %collective-permute-start.2 = (bf16[8,16,1024]{2,1,0:T(8,128)(2,1)S(1)}, bf16[8,16,1024]{2,1,0:T(8,128)(2,1)S(1)}, u32[]{:S(2)}, u32[]{:S(2)}) collective-permute-start(bf16[8,16,1024]{2,1,0:T(8,128)(2,1)S(1)} %slice.260), channel_id=1, source_target_pairs={{0,3},{1,2},{2,1},{3,0},{4,7},{5,6},{6,5},{7,4},{8,11},{9,10},{10,... | collective-permute-start | bytes 786440 | tf_op jit(solution)/shard_map/ppermute | solution.py:145
  30.3 14.9 %collective-permute-start.1 = (bf16[8,16,1024]{2,1,0:T(8,128)(2,1)S(1)}, bf16[8,16,1024]{2,1,0:T(8,128)(2,1)S(1)}, u32[]{:S(2)}, u32[]{:S(2)}) collective-permute-start(bf16[8,16,1024]{2,1,0:T(8,128)(2,1)S(1)} %slice.260), channel_id=1, source_target_pairs={{0,2},{1,3},{2,0},{3,1},{4,6},{5,7},{6,4},{7,5},{8,10},{9,11},{10,... | collective-permute-start | bytes 786440 | tf_op jit(solution)/shard_map/ppermute | solution.py:145
  34.4 5.0 %collective-permute-start.5 = (f32[64,128]{1,0:T(8,128)S(1)}, f32[64,128]{1,0:T(8,128)S(1)}, u32[]{:S(2)}, u32[]{:S(2)}) collective-permute-start(f32[64,128]{1,0:T(8,128)S(1)} %fusion.10), channel_id=1, source_target_pairs={{0,3},{1,2},{2,1},{3,0},{4,7},{5,6},{6,5},{7,4},{8,11},{9,10},{10,... | collective-permute-start | bytes 98312 | tf_op jit(solution)/shard_map/ppermute | solution.py:145
  36.0 7.7 %collective-permute-start.4 = (f32[64,128]{1,0:T(8,128)S(1)}, f32[64,128]{1,0:T(8,128)S(1)}, u32[]{:S(2)}, u32[]{:S(2)}) collective-permute-start(f32[64,128]{1,0:T(8,128)S(1)} %fusion.10), channel_id=1, source_target_pairs={{0,2},{1,3},{2,0},{3,1},{4,6},{5,7},{6,4},{7,5},{8,10},{9,11},{10,... | collective-permute-start | bytes 98312 | tf_op jit(solution)/shard_map/ppermute | solution.py:145
  36.5 7.2 %collective-permute-start.3 = (f32[64,128]{1,0:T(8,128)S(1)}, f32[64,128]{1,0:T(8,128)S(1)}, u32[]{:S(2)}, u32[]{:S(2)}) collective-permute-start(f32[64,128]{1,0:T(8,128)S(1)} %fusion.10), channel_id=1, source_target_pairs={{0,1},{1,0},{2,3},{3,2},{4,5},{5,4},{6,7},{7,6},{8,9},{9,8},{10,11... | collective-permute-start | bytes 98312 | tf_op jit(solution)/shard_map/ppermute | solution.py:145
  39.4 6.4 %collective-permute-start = (bf16[8,16,1024]{2,1,0:T(8,128)(2,1)S(1)}, bf16[8,16,1024]{2,1,0:T(8,128)(2,1)S(1)}, u32[]{:S(2)}, u32[]{:S(2)}) collective-permute-start(bf16[8,16,1024]{2,1,0:T(8,128)(2,1)S(1)} %slice.260), channel_id=1, source_target_pairs={{0,1},{1,0},{2,3},{3,2},{4,5},{5,4},{6,7},{7,6},{8,9},{9,8},{10,11... | collective-permute-start | bytes 786440 | tf_op jit(solution)/shard_map/ppermute | solution.py:145
  51.8 7.8 %collective-permute-start.6 = (bf16[2,192,512]{2,1,0:T(8,128)(2,1)S(1)}, bf16[2,192,512]{2,1,0:T(8,128)(2,1)S(1)}, u32[]{:S(2)}, u32[]{:S(2)}) collective-permute-start(bf16[2,192,512]{2,1,0:T(8,128)(2,1)S(1)} %get-tuple-element.66), channel_id=1, source_target_pairs={{0,4},{4,0},{8,12},{12,8},{16,20},{20,16},{24,28},{28,24},{1,5},{5... | collective-permute-start | bytes 1179656 | tf_op jit(solution)/shard_map/ppermute | solution.py:216
  59.1 11.5 %collective-permute-start.10 = (bf16[2,192,1024]{2,1,0:T(8,128)(2,1)S(1)}, bf16[2,192,1024]{2,1,0:T(8,128)(2,1)S(1)}, u32[]{:S(2)}, u32[]{:S(2)}) collective-permute-start(bf16[2,192,1024]{2,1,0:T(8,128)(2,1)S(1)} %get-tuple-element.70), channel_id=1, source_target_pairs={{0,4},{4,0},{8,12},{12,8},{16,20},{20,16},{24,28},{28,24},{1,5},{5... | collective-permute-start | bytes 2359304 | tf_op jit(solution)/shard_map/ppermute | solution.py:216
  59.7 8.8 %collective-permute-start.7 = (bf16[2,96,512]{2,1,0:T(8,128)(2,1)S(1)}, bf16[2,96,512]{2,1,0:T(8,128)(2,1)S(1)}, u32[]{:S(2)}, u32[]{:S(2)}) collective-permute-start(bf16[2,96,512]{2,1,0:T(8,128)(2,1)S(1)} %add_convert_fusion.11.rest_0_), channel_id=1, source_target_pairs={{0,8},{4,12},{8,0},{12,4},{16,24},{20,28},{24,16},{28,20},{1,9},{5... | collective-permute-start | bytes 589832 | tf_op jit(solution)/shard_map/ppermute | solution.py:216
  68.5 16.9 %collective-permute-start.9 = (bf16[2,192,1280]{2,1,0:T(8,128)(2,1)S(1)}, bf16[2,192,1280]{2,1,0:T(8,128)(2,1)S(1)}, u32[]{:S(2)}, u32[]{:S(2)}) collective-permute-start(bf16[2,192,1280]{2,1,0:T(8,128)(2,1)S(1)} %get-tuple-element.68), channel_id=1, source_target_pairs={{0,4},{4,0},{8,12},{12,8},{16,20},{20,16},{24,28},{28,24},{1,5},{5... | collective-permute-start | bytes 2949128 | tf_op jit(solution)/shard_map/ppermute | solution.py:216
  68.6 17.5 %collective-permute-start.8 = (bf16[2,48,512]{2,1,0:T(8,128)(2,1)S(1)}, bf16[2,48,512]{2,1,0:T(8,128)(2,1)S(1)}, u32[]{:S(2)}, u32[]{:S(2)}) collective-permute-start(bf16[2,48,512]{2,1,0:T(8,128)(2,1)S(1)} %add_convert_fusion.13.rest_1_), channel_id=1, source_target_pairs={{0,16},{4,20},{8,24},{12,28},{16,0},{20,4},{24,8},{28,12},{1,17},{... | collective-permute-start | bytes 294920 | tf_op jit(solution)/shard_map/ppermute | solution.py:216
  70.7 12.4 %collective-permute-start.11 = (bf16[2,96,1024]{2,1,0:T(8,128)(2,1)S(1)}, bf16[2,96,1024]{2,1,0:T(8,128)(2,1)S(1)}, u32[]{:S(2)}, u32[]{:S(2)}) collective-permute-start(bf16[2,96,1024]{2,1,0:T(8,128)(2,1)S(1)} %add_convert_fusion.4.rest_0_), channel_id=1, source_target_pairs={{0,8},{4,12},{8,0},{12,4},{16,24},{20,28},{24,16},{28,20},{1,9},{5... | collective-permute-start | bytes 1179656 | tf_op jit(solution)/shard_map/ppermute | solution.py:216
  79.5 16.1 %collective-permute-start.13 = (bf16[2,192,1280]{2,1,0:T(8,128)(2,1)S(1)}, bf16[2,192,1280]{2,1,0:T(8,128)(2,1)S(1)}, u32[]{:S(2)}, u32[]{:S(2)}) collective-permute-start(bf16[2,192,1280]{2,1,0:T(8,128)(2,1)S(1)} %get-tuple-element.79), channel_id=1, source_target_pairs={{0,4},{4,0},{8,12},{12,8},{16,20},{20,16},{24,28},{28,24},{1,5},{5... | collective-permute-start | bytes 2949128 | tf_op jit(solution)/shard_map/ppermute | solution.py:216
  83.2 28.4 %collective-permute-start.12 = (bf16[2,48,1024]{2,1,0:T(8,128)(2,1)S(1)}, bf16[2,48,1024]{2,1,0:T(8,128)(2,1)S(1)}, u32[]{:S(2)}, u32[]{:S(2)}) collective-permute-start(bf16[2,48,1024]{2,1,0:T(8,128)(2,1)S(1)} %add_convert_fusion.10.rest_1_), channel_id=1, source_target_pairs={{0,16},{4,20},{8,24},{12,28},{16,0},{20,4},{24,8},{28,12},{1,17},{... | collective-permute-start | bytes 589832 | tf_op jit(solution)/shard_map/ppermute | solution.py:216
  85.4 18.0 %collective-permute-start.14 = (bf16[2,96,1280]{2,1,0:T(8,128)(2,1)S(1)}, bf16[2,96,1280]{2,1,0:T(8,128)(2,1)S(1)}, u32[]{:S(2)}, u32[]{:S(2)}) collective-permute-start(bf16[2,96,1280]{2,1,0:T(8,128)(2,1)S(1)} %add_convert_fusion.2.rest_0_), channel_id=1, source_target_pairs={{0,8},{4,12},{8,0},{12,4},{16,24},{20,28},{24,16},{28,20},{1,9},{5... | collective-permute-start | bytes 1474568 | tf_op jit(solution)/shard_map/ppermute | solution.py:216
  94.7 23.0 %collective-permute-start.16 = (bf16[2,192,1280]{2,1,0:T(8,128)(2,1)S(1)}, bf16[2,192,1280]{2,1,0:T(8,128)(2,1)S(1)}, u32[]{:S(2)}, u32[]{:S(2)}) collective-permute-start(bf16[2,192,1280]{2,1,0:T(8,128)(2,1)S(1)} %get-tuple-element.88), channel_id=1, source_target_pairs={{0,4},{4,0},{8,12},{12,8},{16,20},{20,16},{24,28},{28,24},{1,5},{5... | collective-permute-start | bytes 2949128 | tf_op jit(solution)/shard_map/ppermute | solution.py:216
  95.6 22.0 %collective-permute-start.17 = (bf16[2,96,1280]{2,1,0:T(8,128)(2,1)S(1)}, bf16[2,96,1280]{2,1,0:T(8,128)(2,1)S(1)}, u32[]{:S(2)}, u32[]{:S(2)}) collective-permute-start(bf16[2,96,1280]{2,1,0:T(8,128)(2,1)S(1)} %add_convert_fusion.1.rest_0_), channel_id=1, source_target_pairs={{0,8},{4,12},{8,0},{12,4},{16,24},{20,28},{24,16},{28,20},{1,9},{5... | collective-permute-start | bytes 1474568 | tf_op jit(solution)/shard_map/ppermute | solution.py:216
  103.4 0.8 copy-start.4
  104.2 21.3 %collective-permute-start.15 = (bf16[2,48,1280]{2,1,0:T(8,128)(2,1)S(1)}, bf16[2,48,1280]{2,1,0:T(8,128)(2,1)}, u32[]{:S(2)}, u32[]{:S(2)}) collective-permute-start(bf16[2,48,1280]{2,1,0:T(8,128)(2,1)S(1)} %add_convert_fusion.8.rest_1_), channel_id=1, source_target_pairs={{0,16},{4,20},{8,24},{12,28},{16,0},{20,4},{24,8},{28,12},{1,17},{... | collective-permute-start | bytes 737288 | tf_op jit(solution)/shard_map/ppermute | solution.py:216
  111.7 15.7 %collective-permute-start.19 = (bf16[2,192,1024]{2,1,0:T(8,128)(2,1)S(1)}, bf16[2,192,1024]{2,1,0:T(8,128)(2,1)S(1)}, u32[]{:S(2)}, u32[]{:S(2)}) collective-permute-start(bf16[2,192,1024]{2,1,0:T(8,128)(2,1)S(1)} %get-tuple-element.97), channel_id=1, source_target_pairs={{0,4},{4,0},{8,12},{12,8},{16,20},{20,16},{24,28},{28,24},{1,5},{5... | collective-permute-start | bytes 2359304 | tf_op jit(solution)/shard_map/ppermute | solution.py:216
  117.6 0.8 copy-start.2
  117.7 22.8 %collective-permute-start.18 = (bf16[2,48,1280]{2,1,0:T(8,128)(2,1)S(1)}, bf16[2,48,1280]{2,1,0:T(8,128)(2,1)S(1)}, u32[]{:S(2)}, u32[]{:S(2)}) collective-permute-start(bf16[2,48,1280]{2,1,0:T(8,128)(2,1)S(1)} %add_convert_fusion.7.rest_1_), channel_id=1, source_target_pairs={{0,16},{4,20},{8,24},{12,28},{16,0},{20,4},{24,8},{28,12},{1,17},{... | collective-permute-start | bytes 737288 | tf_op jit(solution)/shard_map/ppermute | solution.py:216
  118.4 7.2 %copy-start.5 = (bf16[2,96,1280]{2,1,0:T(8,128)(2,1)S(1)}, bf16[2,96,1280]{2,1,0:T(8,128)(2,1)}, u32[]{:S(2)}) copy-start(bf16[2,96,1280]{2,1,0:T(8,128)(2,1)} %copy-done.4) | copy-start | bytes 1474564
  118.4 21.9 %collective-permute-start.20 = (bf16[2,96,1280]{2,1,0:T(8,128)(2,1)S(1)}, bf16[2,96,1280]{2,1,0:T(8,128)(2,1)S(1)}, u32[]{:S(2)}, u32[]{:S(2)}) collective-permute-start(bf16[2,96,1280]{2,1,0:T(8,128)(2,1)S(1)} %add_convert_fusion.rest_0_), channel_id=1, source_target_pairs={{0,8},{4,12},{8,0},{12,4},{16,24},{20,28},{24,16},{28,20},{1,9},{5... | collective-permute-start | bytes 1474568 | tf_op jit(solution)/shard_map/ppermute | solution.py:216
  125.6 15.2 %collective-permute-start.22 = (bf16[2,192,768]{2,1,0:T(8,128)(2,1)S(1)}, bf16[2,192,768]{2,1,0:T(8,128)(2,1)S(1)}, u32[]{:S(2)}, u32[]{:S(2)}) collective-permute-start(bf16[2,192,768]{2,1,0:T(8,128)(2,1)S(1)} %get-tuple-element.106), channel_id=1, source_target_pairs={{0,4},{4,0},{8,12},{12,8},{16,20},{20,16},{24,28},{28,24},{1,5},{5... | collective-permute-start | bytes 1769480 | tf_op jit(solution)/shard_map/ppermute | solution.py:216
  126.7 13.8 %copy-start.3 = (bf16[2,96,1280]{2,1,0:T(8,128)(2,1)S(1)}, bf16[2,96,1280]{2,1,0:T(8,128)(2,1)}, u32[]{:S(2)}) copy-start(bf16[2,96,1280]{2,1,0:T(8,128)(2,1)} %copy-done.2) | copy-start | bytes 1474564
  127.4 13.2 %copy-start.7 = (bf16[48,7168]{1,0:T(8,128)(2,1)S(1)}, bf16[48,7168]{1,0:T(8,128)(2,1)}, u32[]{:S(2)}) copy-start(bf16[48,7168]{1,0:T(8,128)(2,1)} %fusion.40) | copy-start | bytes 2064388
  127.5 26.0 %collective-permute-start.23 = (bf16[2,96,1024]{2,1,0:T(8,128)(2,1)S(1)}, bf16[2,96,1024]{2,1,0:T(8,128)(2,1)S(1)}, u32[]{:S(2)}, u32[]{:S(2)}) collective-permute-start(bf16[2,96,1024]{2,1,0:T(8,128)(2,1)S(1)} %add_convert_fusion.3), channel_id=1, source_target_pairs={{0,8},{4,12},{8,0},{12,4},{16,24},{20,28},{24,16},{28,20},{1,9},{5... | collective-permute-start | bytes 1179656 | tf_op jit(solution)/shard_map/ppermute | solution.py:216
  140.4 13.2 %collective-permute-start.21 = (bf16[2,48,1280]{2,1,0:T(8,128)(2,1)S(1)}, bf16[2,48,1280]{2,1,0:T(8,128)(2,1)S(1)}, u32[]{:S(2)}, u32[]{:S(2)}) collective-permute-start(bf16[2,48,1280]{2,1,0:T(8,128)(2,1)S(1)} %add_convert_fusion.6), channel_id=1, source_target_pairs={{0,16},{4,20},{8,24},{12,28},{16,0},{20,4},{24,8},{28,12},{1,17},{... | collective-permute-start | bytes 737288 | tf_op jit(solution)/shard_map/ppermute | solution.py:216
  140.8 16.6 %collective-permute-start.25 = (bf16[2,96,768]{2,1,0:T(8,128)(2,1)S(1)}, bf16[2,96,768]{2,1,0:T(8,128)(2,1)S(1)}, u32[]{:S(2)}, u32[]{:S(2)}) collective-permute-start(bf16[2,96,768]{2,1,0:T(8,128)(2,1)S(1)} %add_convert_fusion.5), channel_id=1, source_target_pairs={{0,8},{4,12},{8,0},{12,4},{16,24},{20,28},{24,16},{28,20},{1,9},{5... | collective-permute-start | bytes 884744 | tf_op jit(solution)/shard_map/ppermute | solution.py:216
  153.6 12.5 %collective-permute-start.24 = (bf16[2,48,1024]{2,1,0:T(8,128)(2,1)S(1)}, bf16[2,48,1024]{2,1,0:T(8,128)(2,1)S(1)}, u32[]{:S(2)}, u32[]{:S(2)}) collective-permute-start(bf16[2,48,1024]{2,1,0:T(8,128)(2,1)S(1)} %add_convert_fusion.9), channel_id=1, source_target_pairs={{0,16},{4,20},{8,24},{12,28},{16,0},{20,4},{24,8},{28,12},{1,17},{... | collective-permute-start | bytes 589832 | tf_op jit(solution)/shard_map/ppermute | solution.py:216
  157.5 10.2 %collective-permute-start.26 = (bf16[2,48,768]{2,1,0:T(8,128)(2,1)S(1)}, bf16[2,48,768]{2,1,0:T(8,128)(2,1)S(1)}, u32[]{:S(2)}, u32[]{:S(2)}) collective-permute-start(bf16[2,48,768]{2,1,0:T(8,128)(2,1)S(1)} %add_convert_fusion.12), channel_id=1, source_target_pairs={{0,16},{4,20},{8,24},{12,28},{16,0},{20,4},{24,8},{28,12},{1,17},{... | collective-permute-start | bytes 442376 | tf_op jit(solution)/shard_map/ppermute | solution.py:216
  167.8 14.5 %collective-permute-start.28 = (bf16[48,7168]{1,0:T(8,128)(2,1)S(1)}, bf16[48,7168]{1,0:T(8,128)(2,1)S(1)}, u32[]{:S(2)}, u32[]{:S(2)}) collective-permute-start(bf16[48,7168]{1,0:T(8,128)(2,1)S(1)} %fusion.51), channel_id=1, source_target_pairs={{0,8},{4,12},{8,16},{12,20},{16,24},{20,28},{1,9},{5,13},{9,17},{1... | collective-permute-start | bytes 2064392 | tf_op jit(solution)/shard_map/ppermute | solution.py:245
  169.1 17.3 %collective-permute-start.27 = (bf16[48,7168]{1,0:T(8,128)(2,1)S(1)}, bf16[48,7168]{1,0:T(8,128)(2,1)S(1)}, u32[]{:S(2)}, u32[]{:S(2)}) collective-permute-start(bf16[48,7168]{1,0:T(8,128)(2,1)S(1)} %fusion.51), channel_id=1, source_target_pairs={{8,0},{12,4},{16,8},{20,12},{24,16},{28,20},{9,1},{13,5},{17,9},{2... | collective-permute-start | bytes 2064392 | tf_op jit(solution)/shard_map/ppermute | solution.py:245
  186.4 4.3 %copy-start.1 = (bf16[64,8192]{1,0:T(8,128)(2,1)S(1)}, bf16[64,8192]{1,0:T(8,128)(2,1)}, u32[]{:S(2)}) copy-start(bf16[64,8192]{1,0:T(8,128)(2,1)} %param.8) | copy-start | bytes 3145732
  187.2 2.5 %collective-permute-start.29 = (bf16[64,7168]{1,0:T(8,128)(2,1)S(1)}, bf16[64,7168]{1,0:T(8,128)(2,1)S(1)}, u32[]{:S(2)}, u32[]{:S(2)}) collective-permute-start(bf16[64,7168]{1,0:T(8,128)(2,1)S(1)} %slice.277), channel_id=1, source_target_pairs={{0,4},{4,0},{8,12},{12,8},{16,20},{20,16},{24,28},{28,24},{1,5},{5... | collective-permute-start | bytes 2752520 | tf_op jit(solution)/shard_map/ppermute | solution.py:216

commit v4 on v3

--- a/solution.py
+++ b/solution.py
@@ -8,7 +8,7 @@
 from jax.sharding import PartitionSpec as P
 
 UNITS = 28
-WIDTHS = (2, 4, 5, 5, 5, 4, 3)
+WIDTHS = (1, 3, 5, 5, 6, 5, 3)
 AHEAD = 2
 BATCHES = ()
 HOLD = 1

time: 191 us -> 194 us (1.016)
    convert_element_type x14, other arithmetic: 0.98 us -> 2.94 us  [advance(): message = functools.reduce(jnp.add, parts).astype(bf16)]
  transfers between devices with their start and end apart: 31 -> 31, of which waited for: 15 -> 15; matrix products, arithmetic and copies ran while one was open for 6% -> 6% of each run, Pallas kernels for 24% -> 25%
where the time goes in v4:
time: 194 us; the launch traced here: 193 us
  waiting for transfers between devices  92 us (47%)
  Pallas kernels  51.3 us (26%)
  starting transfers between devices  30.1 us (16%)
  other arithmetic  10.6 us (5%)
  matrix products  5.74 us (3%)
  local copies, waits for them, and re-layouts  2.57 us (1%)
    ppermute x22, waiting for transfers between devices, send(): return lax.ppermute(array, 'dp', [(i, i ^ mask) for i in range(groups)])  53.4 us
    pallas_call x7, Pallas kernels, partial_sums(): pl.pallas_call(partial_kernel, grid=(width // block,), in_specs=[pl.Block...  50.4 us
    all_to_all x1, waiting for transfers between devices, body(): came = lax.all_to_all(sent, 'dp', split_axis=0, concat_axis=0, tiled=True)  17.5 us
    ppermute x2, waiting for transfers between devices, deliver(): lax.ppermute(mine, 'dp', [(i + 2 * k, i) for i in range(groups) if 0 <= i...  15.4 us
    ppermute x22, starting transfers between devices, send(): return lax.ppermute(array, 'dp', [(i, i ^ mask) for i in range(groups)])  14.1 us
    ppermute x6, starting transfers between devices, over_lanes(): return lax.ppermute(array, 'tensor', [(i, i ^ mask) for i in range(lanes)])  7.11 us
    all_to_all x1, starting transfers between devices, body(): came = lax.all_to_all(sent, 'dp', split_axis=0, concat_axis=0, tiled=True)  6.33 us
    ppermute x6, waiting for transfers between devices, over_lanes(): return lax.ppermute(array, 'tensor', [(i, i ^ mask) for i in range(lanes)])  5.64 us
  transfers between devices with their start and end apart: 31, of which 15 were waited for; matrix products, arithmetic and copies ran while one was open for 6% of the time, Pallas kernels for 25%

profile of v4, /device:TPU:0, one launch (start us, length us, event | category | flops | bytes accessed | tf_op | source)
XLA Modules:
  0.0 193.1 jit_solution(7378621481444165914)
XLA Ops:
  0.0 0.9 select_reduce_fusion.3
  2.4 0.9 pad_maximum_fusion.2
  3.3 6.3 %all-to-all-start = ((bf16[8,33,1024]{2,1,0:T(8,128)(2,1)}), bf16[8,33,1024]{2,1,0:T(8,128)(2,1)S(1)}, u32[]{:S(2)}, u32[]{:S(2)}) async-start(bf16[8,33,1024]{2,1,0:T(8,128)(2,1)} %pad_maximum_fusion.2), calls=%async_computation | async-start | bytes 1310720 | tf_op jit(solution)/shard_map/all_to_all | solution.py:140
  10.3 17.5 %all-to-all-done = bf16[8,33,1024]{2,1,0:T(8,128)(2,1)S(1)} async-done(((bf16[8,33,1024]{2,1,0:T(8,128)(2,1)}), bf16[8,33,1024]{2,1,0:T(8,128)(2,1)S(1)}, u32[]{:S(2)}, u32[]{:S(2)}) %all-to-all-start) | async-done | bytes 540704 | tf_op jit(solution)/shard_map/all_to_all | solution.py:140
  27.8 2.5 %collective-permute-start.2 = (bf16[8,16,1024]{2,1,0:T(8,128)(2,1)S(1)}, bf16[8,16,1024]{2,1,0:T(8,128)(2,1)S(1)}, u32[]{:S(2)}, u32[]{:S(2)}) collective-permute-start(bf16[8,16,1024]{2,1,0:T(8,128)(2,1)S(1)} %slice.260), channel_id=1, source_target_pairs={{0,3},{1,2},{2,1},{3,0},{4,7},{5,6},{6,5},{7,4},{8,11},{9,10},{10,... | collective-permute-start | bytes 786440 | tf_op jit(solution)/shard_map/ppermute | solution.py:145
  31.4 3.0 %fusion.10 = f32[64,128]{1,0:T(8,128)S(1)} fusion(bf16[8,2048,128]{2,1,0:T(8,128)(2,1)} %param.10, pred[64,8]{0,1:T(8,128)(4,1)S(1)} %iota_compare_fusion.10, bf16[64,2048]{1,0:T(8,128)(2,1)S(1)} %slice.264), kind=kOutput, calls=%fused_computation.17 | convolution fusion | flops 269484032 | bytes 4489728 | tf_op jit(solution)/shard_map/dot_general | solution.py:155
  34.4 1.6 collective-permute-start.5
  36.5 1.5 collective-permute-start.3
  38.1 1.3 collective-permute-done.5
  39.4 0.5 collective-permute-start
  39.9 3.7 %collective-permute-done.4 = f32[64,128]{1,0:T(8,128)S(1)} collective-permute-done((f32[64,128]{1,0:T(8,128)S(1)}, f32[64,128]{1,0:T(8,128)S(1)}, u32[]{:S(2)}, u32[]{:S(2)}) %collective-permute-start.4) | collective-permute-done | bytes 32800 | tf_op jit(solution)/shard_map/ppermute | solution.py:145
  45.2 0.6 collective-permute-done
  46.0 0.6 convolution_convert_fusion.4.x_ref
  46.6 1.0 shard_map.82.x_ref
  47.6 2.8 %shard_map.83 = (f32[2,192,256]{2,1,0:T(8,128)S(1)}, bf16[2,192,256]{2,1,0:T(8,128)(2,1)S(1)}) custom-call(bf16[2,384,2048]{2,1,0:T(8,128)(2,1)S(1)} %shard_map.82.x_ref, bf16[2,384,1024]{2,1,0:T(8,128)(2,1)S(1)} %pad_maximum_fusion.d_ref, bf16[1024,2,7168]{2,1,0:T(2,128)(2,1)} %w_ref.13, bf16[512,2,7168]{2,1,0:T(2,128)(2,1)} %bitcast.123), custom_call_target="tpu_custom_call" | custom-call | flops 1207959552 | bytes 2162688 | tf_op jit(solution)/shard_map/pallas_call | solution.py:56
  50.4 5.7 %shard_map.85 = (f32[2,192,768]{2,1,0:T(8,128)S(1)}, bf16[2,192,768]{2,1,0:T(8,128)(2,1)S(1)}) custom-call(bf16[2,384,2048]{2,1,0:T(8,128)(2,1)S(1)} %shard_map.82.x_ref, bf16[2,384,1024]{2,1,0:T(8,128)(2,1)S(1)} %pad_maximum_fusion.d_ref, bf16[1024,2,7168]{2,1,0:T(2,128)(2,1)} %w_ref.13, bf16[512,2,7168]{2,1,0:T(2,128)(2,1)} %bitcast.124), custom_call_target="tpu_custom_call" | custom-call | flops 3623878656 | bytes 6488064 | tf_op jit(solution)/shard_map/pallas_call | solution.py:56
  56.2 0.5 collective-permute-start.10
  56.8 8.6 %shard_map.84 = (f32[2,192,1280]{2,1,0:T(8,128)S(1)}, bf16[2,192,1280]{2,1,0:T(8,128)(2,1)S(1)}) custom-call(bf16[2,384,2048]{2,1,0:T(8,128)(2,1)S(1)} %shard_map.82.x_ref, bf16[2,384,1024]{2,1,0:T(8,128)(2,1)S(1)} %pad_maximum_fusion.d_ref, bf16[1024,2,7168]{2,1,0:T(2,128)(2,1)} %w_ref.13, bf16[512,2,7168]{2,1,0:T(2,128)(2,1)} %bitcast.125, ...), custom_call_target="tpu_custom_call" | custom-call | flops 6039797760 | bytes 10813440 | tf_op jit(solution)/shard_map/pallas_call | solution.py:56
  65.6 2.0 %collective-permute-start.8 = (bf16[2,48,256]{2,1,0:T(8,128)(2,1)S(1)}, bf16[2,48,256]{2,1,0:T(8,128)(2,1)S(1)}, u32[]{:S(2)}, u32[]{:S(2)}) collective-permute-start(bf16[2,48,256]{2,1,0:T(8,128)(2,1)S(1)} %add_convert_fusion.13.rest_1_), channel_id=1, source_target_pairs={{0,16},{4,20},{8,24},{12,28},{16,0},{20,4},{24,8},{28,12},{1,17},{... | collective-permute-start | bytes 147464 | tf_op jit(solution)/shard_map/ppermute | solution.py:216
  67.8 8.6 %shard_map.86 = (f32[2,192,1280]{2,1,0:T(8,128)S(1)}, bf16[2,192,1280]{2,1,0:T(8,128)(2,1)S(1)}) custom-call(bf16[2,384,2048]{2,1,0:T(8,128)(2,1)S(1)} %shard_map.82.x_ref, bf16[2,384,1024]{2,1,0:T(8,128)(2,1)S(1)} %pad_maximum_fusion.d_ref, bf16[1024,2,7168]{2,1,0:T(2,128)(2,1)} %w_ref.13, bf16[512,2,7168]{2,1,0:T(2,128)(2,1)} %bitcast.126, ...), custom_call_target="tpu_custom_call" | custom-call | flops 6039797760 | bytes 10813440 | tf_op jit(solution)/shard_map/pallas_call | solution.py:56
  77.1 2.5 %collective-permute-start.12 = (bf16[2,48,768]{2,1,0:T(8,128)(2,1)S(1)}, bf16[2,48,768]{2,1,0:T(8,128)(2,1)S(1)}, u32[]{:S(2)}, u32[]{:S(2)}) collective-permute-start(bf16[2,48,768]{2,1,0:T(8,128)(2,1)S(1)} %add_convert_fusion.11.rest_1_), channel_id=1, source_target_pairs={{0,16},{4,20},{8,24},{12,28},{16,0},{20,4},{24,8},{28,12},{1,17},{... | collective-permute-start | bytes 442376 | tf_op jit(solution)/shard_map/ppermute | solution.py:216
  80.1 10.1 %shard_map.87 = (f32[2,192,1536]{2,1,0:T(8,128)S(1)}, bf16[2,192,1536]{2,1,0:T(8,128)(2,1)S(1)}) custom-call(bf16[2,384,2048]{2,1,0:T(8,128)(2,1)S(1)} %shard_map.82.x_ref, bf16[2,384,1024]{2,1,0:T(8,128)(2,1)S(1)} %pad_maximum_fusion.d_ref, bf16[1024,2,7168]{2,1,0:T(2,128)(2,1)} %w_ref.13, bf16[512,2,7168]{2,1,0:T(2,128)(2,1)} %bitcast.127, ...), custom_call_target="tpu_custom_call" | custom-call | flops 7247757312 | bytes 12976128 | tf_op jit(solution)/shard_map/pallas_call | solution.py:56
  90.5 1.7 collective-permute-start.17
  92.2 3.5 %collective-permute-done.14 = bf16[2,96,1280]{2,1,0:T(8,128)(2,1)S(1)} collective-permute-done((bf16[2,96,1280]{2,1,0:T(8,128)(2,1)S(1)}, bf16[2,96,1280]{2,1,0:T(8,128)(2,1)S(1)}, u32[]{:S(2)}, u32[]{:S(2)}) %collective-permute-start.14) | collective-permute-done | bytes 491552 | tf_op jit(solution)/shard_map/ppermute | solution.py:216
  95.8 0.7 copy-done.4
  96.5 1.1 collective-permute-start.15
  97.5 8.6 %shard_map.88 = (f32[2,192,1280]{2,1,0:T(8,128)S(1)}, bf16[2,192,1280]{2,1,0:T(8,128)(2,1)S(1)}) custom-call(bf16[2,384,2048]{2,1,0:T(8,128)(2,1)S(1)} %shard_map.82.x_ref, bf16[2,384,1024]{2,1,0:T(8,128)(2,1)S(1)} %pad_maximum_fusion.d_ref, bf16[1024,2,7168]{2,1,0:T(2,128)(2,1)} %w_ref.13, bf16[512,2,7168]{2,1,0:T(2,128)(2,1)} %bitcast.128, ...), custom_call_target="tpu_custom_call" | custom-call | flops 6039797760 | bytes 10813440 | tf_op jit(solution)/shard_map/pallas_call | solution.py:56
  106.4 4.4 %collective-permute-done.17 = bf16[2,96,1280]{2,1,0:T(8,128)(2,1)S(1)} collective-permute-done((bf16[2,96,1280]{2,1,0:T(8,128)(2,1)S(1)}, bf16[2,96,1280]{2,1,0:T(8,128)(2,1)S(1)}, u32[]{:S(2)}, u32[]{:S(2)}) %collective-permute-start.17) | collective-permute-done | bytes 491552 | tf_op jit(solution)/shard_map/ppermute | solution.py:216
  111.0 0.5 copy-done.2
  111.6 1.8 collective-permute-start.20
  113.4 5.8 %shard_map.89 = (f32[2,192,768]{2,1,0:T(8,128)S(1)}, bf16[2,192,768]{2,1,0:T(8,128)(2,1)S(1)}) custom-call(bf16[2,384,2048]{2,1,0:T(8,128)(2,1)S(1)} %shard_map.82.x_ref, bf16[2,384,1024]{2,1,0:T(8,128)(2,1)S(1)} %pad_maximum_fusion.d_ref, bf16[1024,2,7168]{2,1,0:T(2,128)(2,1)} %w_ref.13, bf16[512,2,7168]{2,1,0:T(2,128)(2,1)} %bitcast.129, ...), custom_call_target="tpu_custom_call" | custom-call | flops 3623878656 | bytes 6488064 | tf_op jit(solution)/shard_map/pallas_call | solution.py:56
  119.4 1.0 convert_add_fusion.3
  120.5 1.2 add_convert_fusion.1
  121.9 11.0 %collective-permute-done.20 = bf16[2,96,1536]{2,1,0:T(8,128)(2,1)S(1)} collective-permute-done((bf16[2,96,1536]{2,1,0:T(8,128)(2,1)S(1)}, bf16[2,96,1536]{2,1,0:T(8,128)(2,1)S(1)}, u32[]{:S(2)}, u32[]{:S(2)}) %collective-permute-start.20) | collective-permute-done | bytes 589856 | tf_op jit(solution)/shard_map/ppermute | solution.py:216
  133.2 2.5 %collective-permute-start.25 = (bf16[2,96,768]{2,1,0:T(8,128)(2,1)S(1)}, bf16[2,96,768]{2,1,0:T(8,128)(2,1)S(1)}, u32[]{:S(2)}, u32[]{:S(2)}) collective-permute-start(bf16[2,96,768]{2,1,0:T(8,128)(2,1)S(1)} %add_convert_fusion.4), channel_id=1, source_target_pairs={{0,8},{4,12},{8,0},{12,4},{16,24},{20,28},{24,16},{28,20},{1,9},{5... | collective-permute-start | bytes 884744 | tf_op jit(solution)/shard_map/ppermute | solution.py:216
  135.9 13.9 %collective-permute-done.23 = bf16[2,96,1280]{2,1,0:T(8,128)(2,1)S(1)} collective-permute-done((bf16[2,96,1280]{2,1,0:T(8,128)(2,1)S(1)}, bf16[2,96,1280]{2,1,0:T(8,128)(2,1)S(1)}, u32[]{:S(2)}, u32[]{:S(2)}) %collective-permute-start.23) | collective-permute-done | bytes 491552 | tf_op jit(solution)/shard_map/ppermute | solution.py:216
  149.8 1.0 add_convert_fusion.7
  150.9 6.5 %collective-permute-done.25 = bf16[2,96,768]{2,1,0:T(8,128)(2,1)S(1)} collective-permute-done((bf16[2,96,768]{2,1,0:T(8,128)(2,1)S(1)}, bf16[2,96,768]{2,1,0:T(8,128)(2,1)S(1)}, u32[]{:S(2)}, u32[]{:S(2)}) %collective-permute-start.25) | collective-permute-done | bytes 294944 | tf_op jit(solution)/shard_map/ppermute | solution.py:216
  157.8 9.8 %collective-permute-done.24 = bf16[2,48,1280]{2,1,0:T(8,128)(2,1)S(1)} collective-permute-done((bf16[2,48,1280]{2,1,0:T(8,128)(2,1)S(1)}, bf16[2,48,1280]{2,1,0:T(8,128)(2,1)S(1)}, u32[]{:S(2)}, u32[]{:S(2)}) %collective-permute-start.24) | collective-permute-done | bytes 245792 | tf_op jit(solution)/shard_map/ppermute | solution.py:216
  167.5 1.6 collective-permute-done.26
  169.1 1.0 convert_add_fusion.1
  170.4 1.3 collective-permute-start.28
  171.7 1.3 collective-permute-start.27
  173.3 11.3 %collective-permute-done.28 = bf16[48,7168]{1,0:T(8,128)(2,1)S(1)} collective-permute-done((bf16[48,7168]{1,0:T(8,128)(2,1)S(1)}, bf16[48,7168]{1,0:T(8,128)(2,1)S(1)}, u32[]{:S(2)}, u32[]{:S(2)}) %collective-permute-start.28) | collective-permute-done | bytes 688160 | tf_op jit(solution)/shard_map/ppermute | solution.py:245
  184.6 4.2 %collective-permute-done.27 = bf16[48,7168]{1,0:T(8,128)(2,1)S(1)} collective-permute-done((bf16[48,7168]{1,0:T(8,128)(2,1)S(1)}, bf16[48,7168]{1,0:T(8,128)(2,1)S(1)}, u32[]{:S(2)}, u32[]{:S(2)}) %collective-permute-start.27) | collective-permute-done | bytes 688160 | tf_op jit(solution)/shard_map/ppermute | solution.py:245
  188.7 0.7 convolution_convert_fusion
  189.6 2.5 %collective-permute-done.29 = bf16[64,7168]{1,0:T(8,128)(2,1)S(1)} collective-permute-done((bf16[64,7168]{1,0:T(8,128)(2,1)S(1)}, bf16[64,7168]{1,0:T(8,128)(2,1)S(1)}, u32[]{:S(2)}, u32[]{:S(2)}) %collective-permute-start.29) | collective-permute-done | bytes 917536 | tf_op jit(solution)/shard_map/ppermute | solution.py:216
  192.0 1.0 slice_add_fusion
  (127 shorter events, 9.4 us)
Async XLA Ops:
  0.0 1.3 copy-start
  2.0 7.6 %copy-start.10 = (s32[8]{0:T(128)S(1)}, s32[8]{0:T(128)}, u32[]{:S(2)}) copy-start(s32[8]{0:T(128)} %constant.139.clone) | copy-start | bytes 100
  2.1 7.7 %copy-start.6 = (s32[8]{0:T(128)S(1)}, s32[8]{0:T(128)}, u32[]{:S(2)}) copy-start(s32[8]{0:T(128)} %param.14) | copy-start | bytes 100
  3.3 24.5 %all-to-all-start = ((bf16[8,33,1024]{2,1,0:T(8,128)(2,1)}), bf16[8,33,1024]{2,1,0:T(8,128)(2,1)S(1)}, u32[]{:S(2)}, u32[]{:S(2)}) async-start(bf16[8,33,1024]{2,1,0:T(8,128)(2,1)} %pad_maximum_fusion.2), calls=%async_computation | async-start | bytes 1310720 | tf_op jit(solution)/shard_map/all_to_all | solution.py:140
  10.0 20.3 %copy-start.8 = (s32[8]{0:T(128)}, s32[8]{0:T(128)S(1)}, u32[]{:S(2)}) copy-start(s32[8]{0:T(128)S(1)} %bitcast_subtract_fusion) | copy-start | bytes 100
  27.8 17.4 %collective-permute-start.2 = (bf16[8,16,1024]{2,1,0:T(8,128)(2,1)S(1)}, bf16[8,16,1024]{2,1,0:T(8,128)(2,1)S(1)}, u32[]{:S(2)}, u32[]{:S(2)}) collective-permute-start(bf16[8,16,1024]{2,1,0:T(8,128)(2,1)S(1)} %slice.260), channel_id=1, source_target_pairs={{0,3},{1,2},{2,1},{3,0},{4,7},{5,6},{6,5},{7,4},{8,11},{9,10},{10,... | collective-permute-start | bytes 786440 | tf_op jit(solution)/shard_map/ppermute | solution.py:145
  30.3 14.9 %collective-permute-start.1 = (bf16[8,16,1024]{2,1,0:T(8,128)(2,1)S(1)}, bf16[8,16,1024]{2,1,0:T(8,128)(2,1)S(1)}, u32[]{:S(2)}, u32[]{:S(2)}) collective-permute-start(bf16[8,16,1024]{2,1,0:T(8,128)(2,1)S(1)} %slice.260), channel_id=1, source_target_pairs={{0,2},{1,3},{2,0},{3,1},{4,6},{5,7},{6,4},{7,5},{8,10},{9,11},{10,... | collective-permute-start | bytes 786440 | tf_op jit(solution)/shard_map/ppermute | solution.py:145
  34.4 5.0 %collective-permute-start.5 = (f32[64,128]{1,0:T(8,128)S(1)}, f32[64,128]{1,0:T(8,128)S(1)}, u32[]{:S(2)}, u32[]{:S(2)}) collective-permute-start(f32[64,128]{1,0:T(8,128)S(1)} %fusion.10), channel_id=1, source_target_pairs={{0,3},{1,2},{2,1},{3,0},{4,7},{5,6},{6,5},{7,4},{8,11},{9,10},{10,... | collective-permute-start | bytes 98312 | tf_op jit(solution)/shard_map/ppermute | solution.py:145
  36.0 7.7 %collective-permute-start.4 = (f32[64,128]{1,0:T(8,128)S(1)}, f32[64,128]{1,0:T(8,128)S(1)}, u32[]{:S(2)}, u32[]{:S(2)}) collective-permute-start(f32[64,128]{1,0:T(8,128)S(1)} %fusion.10), channel_id=1, source_target_pairs={{0,2},{1,3},{2,0},{3,1},{4,6},{5,7},{6,4},{7,5},{8,10},{9,11},{10,... | collective-permute-start | bytes 98312 | tf_op jit(solution)/shard_map/ppermute | solution.py:145
  36.5 7.2 %collective-permute-start.3 = (f32[64,128]{1,0:T(8,128)S(1)}, f32[64,128]{1,0:T(8,128)S(1)}, u32[]{:S(2)}, u32[]{:S(2)}) collective-permute-start(f32[64,128]{1,0:T(8,128)S(1)} %fusion.10), channel_id=1, source_target_pairs={{0,1},{1,0},{2,3},{3,2},{4,5},{5,4},{6,7},{7,6},{8,9},{9,8},{10,11... | collective-permute-start | bytes 98312 | tf_op jit(solution)/shard_map/ppermute | solution.py:145
  39.4 6.4 %collective-permute-start = (bf16[8,16,1024]{2,1,0:T(8,128)(2,1)S(1)}, bf16[8,16,1024]{2,1,0:T(8,128)(2,1)S(1)}, u32[]{:S(2)}, u32[]{:S(2)}) collective-permute-start(bf16[8,16,1024]{2,1,0:T(8,128)(2,1)S(1)} %slice.260), channel_id=1, source_target_pairs={{0,1},{1,0},{2,3},{3,2},{4,5},{5,4},{6,7},{7,6},{8,9},{9,8},{10,11... | collective-permute-start | bytes 786440 | tf_op jit(solution)/shard_map/ppermute | solution.py:145
  50.4 6.4 %collective-permute-start.6 = (bf16[2,192,256]{2,1,0:T(8,128)(2,1)S(1)}, bf16[2,192,256]{2,1,0:T(8,128)(2,1)S(1)}, u32[]{:S(2)}, u32[]{:S(2)}) collective-permute-start(bf16[2,192,256]{2,1,0:T(8,128)(2,1)S(1)} %get-tuple-element.66), channel_id=1, source_target_pairs={{0,4},{4,0},{8,12},{12,8},{16,20},{20,16},{24,28},{28,24},{1,5},{5... | collective-permute-start | bytes 589832 | tf_op jit(solution)/shard_map/ppermute | solution.py:216
  56.2 11.5 %collective-permute-start.10 = (bf16[2,192,768]{2,1,0:T(8,128)(2,1)S(1)}, bf16[2,192,768]{2,1,0:T(8,128)(2,1)S(1)}, u32[]{:S(2)}, u32[]{:S(2)}) collective-permute-start(bf16[2,192,768]{2,1,0:T(8,128)(2,1)S(1)} %get-tuple-element.70), channel_id=1, source_target_pairs={{0,4},{4,0},{8,12},{12,8},{16,20},{20,16},{24,28},{28,24},{1,5},{5... | collective-permute-start | bytes 1769480 | tf_op jit(solution)/shard_map/ppermute | solution.py:216
  56.8 8.8 %collective-permute-start.7 = (bf16[2,96,256]{2,1,0:T(8,128)(2,1)S(1)}, bf16[2,96,256]{2,1,0:T(8,128)(2,1)S(1)}, u32[]{:S(2)}, u32[]{:S(2)}) collective-permute-start(bf16[2,96,256]{2,1,0:T(8,128)(2,1)S(1)} %add_convert_fusion.12.rest_0_), channel_id=1, source_target_pairs={{0,8},{4,12},{8,0},{12,4},{16,24},{20,28},{24,16},{28,20},{1,9},{5... | collective-permute-start | bytes 294920 | tf_op jit(solution)/shard_map/ppermute | solution.py:216
  65.5 14.1 %collective-permute-start.9 = (bf16[2,192,1280]{2,1,0:T(8,128)(2,1)S(1)}, bf16[2,192,1280]{2,1,0:T(8,128)(2,1)S(1)}, u32[]{:S(2)}, u32[]{:S(2)}) collective-permute-start(bf16[2,192,1280]{2,1,0:T(8,128)(2,1)S(1)} %get-tuple-element.68), channel_id=1, source_target_pairs={{0,4},{4,0},{8,12},{12,8},{16,20},{20,16},{24,28},{28,24},{1,5},{5... | collective-permute-start | bytes 2949128 | tf_op jit(solution)/shard_map/ppermute | solution.py:216
  65.6 14.5 %collective-permute-start.8 = (bf16[2,48,256]{2,1,0:T(8,128)(2,1)S(1)}, bf16[2,48,256]{2,1,0:T(8,128)(2,1)S(1)}, u32[]{:S(2)}, u32[]{:S(2)}) collective-permute-start(bf16[2,48,256]{2,1,0:T(8,128)(2,1)S(1)} %add_convert_fusion.13.rest_1_), channel_id=1, source_target_pairs={{0,16},{4,20},{8,24},{12,28},{16,0},{20,4},{24,8},{28,12},{1,17},{... | collective-permute-start | bytes 147464 | tf_op jit(solution)/shard_map/ppermute | solution.py:216
  67.7 9.3 %collective-permute-start.11 = (bf16[2,96,768]{2,1,0:T(8,128)(2,1)S(1)}, bf16[2,96,768]{2,1,0:T(8,128)(2,1)S(1)}, u32[]{:S(2)}, u32[]{:S(2)}) collective-permute-start(bf16[2,96,768]{2,1,0:T(8,128)(2,1)S(1)} %add_convert_fusion.6.rest_0_), channel_id=1, source_target_pairs={{0,8},{4,12},{8,0},{12,4},{16,24},{20,28},{24,16},{28,20},{1,9},{5... | collective-permute-start | bytes 884744 | tf_op jit(solution)/shard_map/ppermute | solution.py:216
  76.4 13.9 %collective-permute-start.13 = (bf16[2,192,1280]{2,1,0:T(8,128)(2,1)S(1)}, bf16[2,192,1280]{2,1,0:T(8,128)(2,1)S(1)}, u32[]{:S(2)}, u32[]{:S(2)}) collective-permute-start(bf16[2,192,1280]{2,1,0:T(8,128)(2,1)S(1)} %get-tuple-element.79), channel_id=1, source_target_pairs={{0,4},{4,0},{8,12},{12,8},{16,20},{20,16},{24,28},{28,24},{1,5},{5... | collective-permute-start | bytes 2949128 | tf_op jit(solution)/shard_map/ppermute | solution.py:216
  77.1 29.1 %collective-permute-start.12 = (bf16[2,48,768]{2,1,0:T(8,128)(2,1)S(1)}, bf16[2,48,768]{2,1,0:T(8,128)(2,1)S(1)}, u32[]{:S(2)}, u32[]{:S(2)}) collective-permute-start(bf16[2,48,768]{2,1,0:T(8,128)(2,1)S(1)} %add_convert_fusion.11.rest_1_), channel_id=1, source_target_pairs={{0,16},{4,20},{8,24},{12,28},{16,0},{20,4},{24,8},{28,12},{1,17},{... | collective-permute-start | bytes 442376 | tf_op jit(solution)/shard_map/ppermute | solution.py:216
  79.7 16.0 %collective-permute-start.14 = (bf16[2,96,1280]{2,1,0:T(8,128)(2,1)S(1)}, bf16[2,96,1280]{2,1,0:T(8,128)(2,1)S(1)}, u32[]{:S(2)}, u32[]{:S(2)}) collective-permute-start(bf16[2,96,1280]{2,1,0:T(8,128)(2,1)S(1)} %add_convert_fusion.3.rest_0_), channel_id=1, source_target_pairs={{0,8},{4,12},{8,0},{12,4},{16,24},{20,28},{24,16},{28,20},{1,9},{5... | collective-permute-start | bytes 1474568 | tf_op jit(solution)/shard_map/ppermute | solution.py:216
  90.2 20.7 %collective-permute-start.16 = (bf16[2,192,1536]{2,1,0:T(8,128)(2,1)S(1)}, bf16[2,192,1536]{2,1,0:T(8,128)(2,1)S(1)}, u32[]{:S(2)}, u32[]{:S(2)}) collective-permute-start(bf16[2,192,1536]{2,1,0:T(8,128)(2,1)S(1)} %get-tuple-element.88), channel_id=1, source_target_pairs={{0,4},{4,0},{8,12},{12,8},{16,20},{20,16},{24,28},{28,24},{1,5},{5... | collective-permute-start | bytes 3538952 | tf_op jit(solution)/shard_map/ppermute | solution.py:216
  90.5 20.3 %collective-permute-start.17 = (bf16[2,96,1280]{2,1,0:T(8,128)(2,1)S(1)}, bf16[2,96,1280]{2,1,0:T(8,128)(2,1)S(1)}, u32[]{:S(2)}, u32[]{:S(2)}) collective-permute-start(bf16[2,96,1280]{2,1,0:T(8,128)(2,1)S(1)} %add_convert_fusion.2.rest_0_), channel_id=1, source_target_pairs={{0,8},{4,12},{8,0},{12,4},{16,24},{20,28},{24,16},{28,20},{1,9},{5... | collective-permute-start | bytes 1474568 | tf_op jit(solution)/shard_map/ppermute | solution.py:216
  95.7 0.8 copy-start.4
  96.5 22.8 %collective-permute-start.15 = (bf16[2,48,1280]{2,1,0:T(8,128)(2,1)S(1)}, bf16[2,48,1280]{2,1,0:T(8,128)(2,1)}, u32[]{:S(2)}, u32[]{:S(2)}) collective-permute-start(bf16[2,48,1280]{2,1,0:T(8,128)(2,1)S(1)} %add_convert_fusion.9.rest_1_), channel_id=1, source_target_pairs={{0,16},{4,20},{8,24},{12,28},{16,0},{20,4},{24,8},{28,12},{1,17},{... | collective-permute-start | bytes 737288 | tf_op jit(solution)/shard_map/ppermute | solution.py:216
  106.2 14.3 %collective-permute-start.19 = (bf16[2,192,1280]{2,1,0:T(8,128)(2,1)S(1)}, bf16[2,192,1280]{2,1,0:T(8,128)(2,1)}, u32[]{:S(2)}, u32[]{:S(2)}) collective-permute-start(bf16[2,192,1280]{2,1,0:T(8,128)(2,1)S(1)} %get-tuple-element.97), channel_id=1, source_target_pairs={{0,4},{4,0},{8,12},{12,8},{16,20},{20,16},{24,28},{28,24},{1,5},{5... | collective-permute-start | bytes 2949128 | tf_op jit(solution)/shard_map/ppermute | solution.py:216
  110.8 0.8 copy-start.2
  110.8 22.3 %collective-permute-start.18 = (bf16[2,48,1280]{2,1,0:T(8,128)(2,1)S(1)}, bf16[2,48,1280]{2,1,0:T(8,128)(2,1)S(1)}, u32[]{:S(2)}, u32[]{:S(2)}) collective-permute-start(bf16[2,48,1280]{2,1,0:T(8,128)(2,1)S(1)} %add_convert_fusion.8.rest_1_), channel_id=1, source_target_pairs={{0,16},{4,20},{8,24},{12,28},{16,0},{20,4},{24,8},{28,12},{1,17},{... | collective-permute-start | bytes 737288 | tf_op jit(solution)/shard_map/ppermute | solution.py:216
  111.6 7.8 %copy-start.5 = (bf16[2,96,1280]{2,1,0:T(8,128)(2,1)S(1)}, bf16[2,96,1280]{2,1,0:T(8,128)(2,1)}, u32[]{:S(2)}) copy-start(bf16[2,96,1280]{2,1,0:T(8,128)(2,1)} %copy-done.4) | copy-start | bytes 1474564
  111.6 21.4 %collective-permute-start.20 = (bf16[2,96,1536]{2,1,0:T(8,128)(2,1)S(1)}, bf16[2,96,1536]{2,1,0:T(8,128)(2,1)S(1)}, u32[]{:S(2)}, u32[]{:S(2)}) collective-permute-start(bf16[2,96,1536]{2,1,0:T(8,128)(2,1)S(1)} %add_convert_fusion.rest_0_), channel_id=1, source_target_pairs={{0,8},{4,12},{8,0},{12,4},{16,24},{20,28},{24,16},{28,20},{1,9},{5... | collective-permute-start | bytes 1769480 | tf_op jit(solution)/shard_map/ppermute | solution.py:216
  119.3 13.9 %collective-permute-start.22 = (bf16[2,192,768]{2,1,0:T(8,128)(2,1)S(1)}, bf16[2,192,768]{2,1,0:T(8,128)(2,1)S(1)}, u32[]{:S(2)}, u32[]{:S(2)}) collective-permute-start(bf16[2,192,768]{2,1,0:T(8,128)(2,1)S(1)} %get-tuple-element.106), channel_id=1, source_target_pairs={{0,4},{4,0},{8,12},{12,8},{16,20},{20,16},{24,28},{28,24},{1,5},{5... | collective-permute-start | bytes 1769480 | tf_op jit(solution)/shard_map/ppermute | solution.py:216
  120.5 15.2 %copy-start.3 = (bf16[2,96,1280]{2,1,0:T(8,128)(2,1)S(1)}, bf16[2,96,1280]{2,1,0:T(8,128)(2,1)}, u32[]{:S(2)}) copy-start(bf16[2,96,1280]{2,1,0:T(8,128)(2,1)} %copy-done.2) | copy-start | bytes 1474564
  121.7 28.1 %collective-permute-start.23 = (bf16[2,96,1280]{2,1,0:T(8,128)(2,1)S(1)}, bf16[2,96,1280]{2,1,0:T(8,128)(2,1)S(1)}, u32[]{:S(2)}, u32[]{:S(2)}) collective-permute-start(bf16[2,96,1280]{2,1,0:T(8,128)(2,1)S(1)} %add_convert_fusion.1), channel_id=1, source_target_pairs={{0,8},{4,12},{8,0},{12,4},{16,24},{20,28},{24,16},{28,20},{1,9},{5... | collective-permute-start | bytes 1474568 | tf_op jit(solution)/shard_map/ppermute | solution.py:216
  133.1 17.9 %collective-permute-start.21 = (bf16[2,48,1536]{2,1,0:T(8,128)(2,1)S(1)}, bf16[2,48,1536]{2,1,0:T(8,128)(2,1)S(1)}, u32[]{:S(2)}, u32[]{:S(2)}) collective-permute-start(bf16[2,48,1536]{2,1,0:T(8,128)(2,1)S(1)} %add_convert_fusion.5), channel_id=1, source_target_pairs={{0,16},{4,20},{8,24},{12,28},{16,0},{20,4},{24,8},{28,12},{1,17},{... | collective-permute-start | bytes 884744 | tf_op jit(solution)/shard_map/ppermute | solution.py:216
  133.2 24.2 %collective-permute-start.25 = (bf16[2,96,768]{2,1,0:T(8,128)(2,1)S(1)}, bf16[2,96,768]{2,1,0:T(8,128)(2,1)S(1)}, u32[]{:S(2)}, u32[]{:S(2)}) collective-permute-start(bf16[2,96,768]{2,1,0:T(8,128)(2,1)S(1)} %add_convert_fusion.4), channel_id=1, source_target_pairs={{0,8},{4,12},{8,0},{12,4},{16,24},{20,28},{24,16},{28,20},{1,9},{5... | collective-permute-start | bytes 884744 | tf_op jit(solution)/shard_map/ppermute | solution.py:216
  150.8 16.7 %collective-permute-start.24 = (bf16[2,48,1280]{2,1,0:T(8,128)(2,1)S(1)}, bf16[2,48,1280]{2,1,0:T(8,128)(2,1)S(1)}, u32[]{:S(2)}, u32[]{:S(2)}) collective-permute-start(bf16[2,48,1280]{2,1,0:T(8,128)(2,1)S(1)} %add_convert_fusion.7), channel_id=1, source_target_pairs={{0,16},{4,20},{8,24},{12,28},{16,0},{20,4},{24,8},{28,12},{1,17},{... | collective-permute-start | bytes 737288 | tf_op jit(solution)/shard_map/ppermute | solution.py:216
  157.4 11.7 %collective-permute-start.26 = (bf16[2,48,768]{2,1,0:T(8,128)(2,1)S(1)}, bf16[2,48,768]{2,1,0:T(8,128)(2,1)S(1)}, u32[]{:S(2)}, u32[]{:S(2)}) collective-permute-start(bf16[2,48,768]{2,1,0:T(8,128)(2,1)S(1)} %add_convert_fusion.10), channel_id=1, source_target_pairs={{0,16},{4,20},{8,24},{12,28},{16,0},{20,4},{24,8},{28,12},{1,17},{... | collective-permute-start | bytes 442376 | tf_op jit(solution)/shard_map/ppermute | solution.py:216
  157.7 15.4 %copy-start.7 = (s32[8]{0:T(128)S(1)}, s32[8]{0:T(128)}, u32[]{:S(2)}) copy-start(s32[8]{0:T(128)} %param.14) | copy-start | bytes 100
  157.8 15.4 %copy-start.9 = (s32[8]{0:T(128)S(1)}, s32[8]{0:T(128)}, u32[]{:S(2)}) copy-start(s32[8]{0:T(128)} %copy-done.8) | copy-start | bytes 100
  170.4 14.2 %collective-permute-start.28 = (bf16[48,7168]{1,0:T(8,128)(2,1)S(1)}, bf16[48,7168]{1,0:T(8,128)(2,1)S(1)}, u32[]{:S(2)}, u32[]{:S(2)}) collective-permute-start(bf16[48,7168]{1,0:T(8,128)(2,1)S(1)} %fusion.49), channel_id=1, source_target_pairs={{0,8},{4,12},{8,16},{12,20},{16,24},{20,28},{1,9},{5,13},{9,17},{1... | collective-permute-start | bytes 2064392 | tf_op jit(solution)/shard_map/ppermute | solution.py:245
  171.7 17.0 %collective-permute-start.27 = (bf16[48,7168]{1,0:T(8,128)(2,1)S(1)}, bf16[48,7168]{1,0:T(8,128)(2,1)S(1)}, u32[]{:S(2)}, u32[]{:S(2)}) collective-permute-start(bf16[48,7168]{1,0:T(8,128)(2,1)S(1)} %fusion.49), channel_id=1, source_target_pairs={{8,0},{12,4},{16,8},{20,12},{24,16},{28,20},{9,1},{13,5},{17,9},{2... | collective-permute-start | bytes 2064392 | tf_op jit(solution)/shard_map/ppermute | solution.py:245
  188.7 4.3 %copy-start.1 = (bf16[64,8192]{1,0:T(8,128)(2,1)S(1)}, bf16[64,8192]{1,0:T(8,128)(2,1)}, u32[]{:S(2)}) copy-start(bf16[64,8192]{1,0:T(8,128)(2,1)} %param.8) | copy-start | bytes 3145732
  189.5 2.5 %collective-permute-start.29 = (bf16[64,7168]{1,0:T(8,128)(2,1)S(1)}, bf16[64,7168]{1,0:T(8,128)(2,1)S(1)}, u32[]{:S(2)}, u32[]{:S(2)}) collective-permute-start(bf16[64,7168]{1,0:T(8,128)(2,1)S(1)} %slice.277), channel_id=1, source_target_pairs={{0,4},{4,0},{8,12},{12,8},{16,20},{20,16},{24,28},{28,24},{1,5},{5... | collective-permute-start | bytes 2752520 | tf_op jit(solution)/shard_map/ppermute | solution.py:216
